TPU v7x, 1024 devices: a whole 4x8x16 slice. The times are simulated.
1024 devices in a mesh: row: 64 (over y, x, z_hi), col: 16 (over z_lo, core).
Axes of the slice: x: 4, y: 8, z: 16 (z_hi: 2, z_lo: 8; z = z_hi * 8 + z_lo), core: 2. Of those that a mesh axis runs over, the one named last changes fastest.
Arguments:
- a_blocks: bfloat16 [256, 64, 128, 128], P('row', 'col'), may hold values from -6 to 6
- a_rows: int32 [256, 64], P('row', 'col'), may hold values from 0 to 1
- a_count: int32 [256, 16], P('row', 'col'), may hold values from 0 to 4
- b_blocks: bfloat16 [128, 64, 128, 128], P('row', 'col'), may hold values from -0.5 to 0.5
- b_cols: int32 [128, 64], P('row', 'col'), may hold values from 0 to 1
- b_count: int32 [128, 16], P('row', 'col'), may hold values from 0 to 4
- c_keep: int32 [128, 32], P('row', 'col'), may hold values 0 or 1
Outputs:
- c_blocks: float32 [128, 32, 128, 128], P('row', 'col')
Inputs may be any that keep to these rules, and one draw needn't show every extreme that they name: `a_count`: some block columns of some A piece are full in every draw. `b_count`: some block rows of some B piece are full in every draw.
All inputs are finite; a program needn't handle non-finite values. No bound on the sum of `c_keep` on one device may be relied on, other than what follows from the above.
Results may differ from a plain program's by a relative error of at most 0.0003.
Values may be sent and summed in bfloat16 or wider, within the bound.
No kernel may reach another device: no remote copies, remote signals or barrier semaphores. Data moves between devices by JAX's collectives and lax.ppermute only.
A program may use at most 32 MiB of HBM per device.

v0:
```python
import jax
import jax.numpy as jnp
from jax import lax
from jax.sharding import PartitionSpec as P


def passed_along(x, axis, by):
    peers = lax.axis_size(axis)
    return lax.ppermute(x, axis, [(i, (i + by) % peers) for i in range(peers)])


def block_products(a_part, b_part, tile_rows):
    a_tiles, a_which, a_many = a_part
    b_tiles, b_which, b_many = b_part
    slot_ids = lax.broadcasted_iota(jnp.int32, a_which.shape, 1)
    a_live = slot_ids < a_many
    b_live = slot_ids < b_many
    picks = jnp.arange(tile_rows, dtype=jnp.int32)
    row_hits = jnp.where((a_which[:, :, None] == picks) & a_live[:, :, None], 1.0, 0.0).astype(
        jnp.float32
    )
    col_hits = jnp.where((b_which[:, :, None] == picks) & b_live[:, :, None], 1.0, 0.0).astype(
        jnp.float32
    )
    products = jnp.einsum("kdxy,keyz->kdexz", a_tiles, b_tiles, preferred_element_type=jnp.float32)
    weight = jnp.einsum(
        "kdi,kej->ijkde", row_hits, col_hits, precision=lax.Precision.HIGHEST
    ).reshape(tile_rows * tile_rows, -1)
    placed = jnp.dot(weight, products.reshape(weight.shape[1], -1), precision=lax.Precision.HIGHEST)
    width = a_tiles.shape[-1]
    return placed.reshape(tile_rows, tile_rows, width, width)


def pick_half(part, half, block_cols):
    return tuple(
        (lax.dynamic_slice_in_dim(member, half * block_cols, block_cols, 0) for member in part)
    )


def per_device(a_blocks, a_rows, a_count, b_blocks, b_cols, b_count, c_keep):
    tile_rows = c_keep.shape[0]
    block_cols = b_blocks.shape[0]
    columns = lax.axis_size("col")
    sections = columns // 2
    col_at = lax.axis_index("col")
    own_a = (a_blocks, a_rows, a_count)
    own_b = (b_blocks, b_cols, b_count)
    summed = block_products(pick_half(own_a, 0, block_cols), own_b, tile_rows)
    moving_a = own_a
    moving_b = own_b
    for section_at in range(1, sections):
        moving_a = passed_along((moving_a[0], moving_a[1], moving_a[2]), "col", -1)
        moving_b = passed_along((moving_b[0], moving_b[1], moving_b[2]), "row", -1)
        half = (col_at + section_at) // columns
        summed = summed + block_products(pick_half(moving_a, half, block_cols), moving_b, tile_rows)
    return jnp.where(c_keep[:, :, None, None] == 1, summed, jnp.zeros_like(summed))


def solution(mesh):
    placed = (
        P("row", "col", None, None),
        P("row", "col"),
        P("row", "col"),
        P("row", "col", None, None),
        P("row", "col"),
        P("row", "col"),
        P("row", "col"),
    )
    return jax.shard_map(
        per_device,
        mesh=mesh,
        in_specs=placed,
        out_specs=P("row", "col", None, None),
        check_vma=False,
    )
```

profile of v0, /device:TPU:1, one launch (start us, length us, event | category | flops | bytes accessed | tf_op | source)
XLA Modules:
  0.0 524.2 jit_solution(15895477539853220590)
XLA Ops:
  0.0 16.2 %collective-permute-start.4 = (bf16[4,4,128,128]{3,2,1,0:T(8,128)(2,1)}, bf16[4,4,128,128]{3,2,1,0:T(8,128)(2,1)S(1)}, u32[]{:S(2)}, u32[]{:S(2)}) collective-permute-start(bf16[4,4,128,128]{3,2,1,0:T(8,128)(2,1)} %param.7), channel_id=1, source_target_pairs={{0,15},{1,0},{2,1},{3,2},{4,3},{5,4},{6,5},{7,6},{8,7},{9,8},{10,9... | collective-permute-start | bytes 1572872 | tf_op jit(solution)/shard_map/ppermute | solution.py:9
  16.2 11.5 %collective-permute-start.5 = (bf16[2,4,128,128]{3,2,1,0:T(8,128)(2,1)}, bf16[2,4,128,128]{3,2,1,0:T(8,128)(2,1)S(1)}, u32[]{:S(2)}, u32[]{:S(2)}) collective-permute-start(bf16[2,4,128,128]{3,2,1,0:T(8,128)(2,1)} %param.10), channel_id=1, source_target_pairs={{0,1008},{16,0},{32,16},{48,32},{64,48},{80,64},{96,80},{112,96},{... | collective-permute-start | bytes 786440 | tf_op jit(solution)/shard_map/ppermute | solution.py:9
  27.7 8.6 %collective-permute-start.2 = (s32[4,4]{1,0:T(4,128)}, s32[4,4]{1,0:T(4,128)S(1)}, u32[]{:S(2)}, u32[]{:S(2)}) collective-permute-start(s32[4,4]{1,0:T(4,128)} %param.8), channel_id=1, source_target_pairs={{0,15},{1,0},{2,1},{3,2},{4,3},{5,4},{6,5},{7,6},{8,7},{9,8},{10,9... | collective-permute-start | bytes 200 | tf_op jit(solution)/shard_map/ppermute | solution.py:9
  36.3 2.3 collective-permute-start.3
  38.6 2.4 collective-permute-start.1
  42.7 1.8 copy.11
  44.9 6.9 %collective-permute-done.1 = s32[2,1]{0,1:T(1,128)S(1)} collective-permute-done((s32[2,1]{0,1:T(1,128)}, s32[2,1]{0,1:T(1,128)S(1)}, u32[]{:S(2)}, u32[]{:S(2)}) %collective-permute-start.1) | collective-permute-done | bytes 40 | tf_op jit(solution)/shard_map/ppermute | solution.py:9
  51.9 6.8 %collective-permute-start.7 = (s32[2,1]{0,1:T(1,128)S(1)}, s32[2,1]{0,1:T(1,128)S(1)}, u32[]{:S(2)}, u32[]{:S(2)}) collective-permute-start(s32[2,1]{0,1:T(1,128)S(1)} %collective-permute-done.1), channel_id=1, source_target_pairs={{0,1008},{16,0},{32,16},{48,32},{64,48},{80,64},{96,80},{112,96},{... | collective-permute-start | bytes 32 | tf_op jit(solution)/shard_map/ppermute | solution.py:9
  58.7 6.1 %collective-permute-done.7 = s32[2,1]{0,1:T(1,128)S(1)} collective-permute-done((s32[2,1]{0,1:T(1,128)S(1)}, s32[2,1]{0,1:T(1,128)S(1)}, u32[]{:S(2)}, u32[]{:S(2)}) %collective-permute-start.7) | collective-permute-done | bytes 40 | tf_op jit(solution)/shard_map/ppermute | solution.py:9
  64.9 11.1 %collective-permute-start = (s32[2,4]{1,0:T(2,128)S(1)}, s32[2,4]{1,0:T(2,128)S(1)}, u32[]{:S(2)}, u32[]{:S(2)}) collective-permute-start(s32[2,4]{1,0:T(2,128)S(1)} %copy-done.1), channel_id=1, source_target_pairs={{0,1008},{16,0},{32,16},{48,32},{64,48},{80,64},{96,80},{112,96},{... | collective-permute-start | bytes 104 | tf_op jit(solution)/shard_map/ppermute | solution.py:9
  76.1 3.2 collective-permute-start.13
  79.3 9.8 %collective-permute-done.13 = s32[2,1]{0,1:T(1,128)S(1)} collective-permute-done((s32[2,1]{0,1:T(1,128)S(1)}, s32[2,1]{0,1:T(1,128)S(1)}, u32[]{:S(2)}, u32[]{:S(2)}) %collective-permute-start.13) | collective-permute-done | bytes 40 | tf_op jit(solution)/shard_map/ppermute | solution.py:9
  89.2 7.4 %collective-permute-start.19 = (s32[2,1]{0,1:T(1,128)S(1)}, s32[2,1]{0,1:T(1,128)S(1)}, u32[]{:S(2)}, u32[]{:S(2)}) collective-permute-start(s32[2,1]{0,1:T(1,128)S(1)} %collective-permute-done.13), channel_id=1, source_target_pairs={{0,1008},{16,0},{32,16},{48,32},{64,48},{80,64},{96,80},{112,96},{... | collective-permute-start | bytes 32 | tf_op jit(solution)/shard_map/ppermute | solution.py:9
  96.6 5.6 %collective-permute-done.19 = s32[2,1]{0,1:T(1,128)S(1)} collective-permute-done((s32[2,1]{0,1:T(1,128)S(1)}, s32[2,1]{0,1:T(1,128)S(1)}, u32[]{:S(2)}, u32[]{:S(2)}) %collective-permute-start.19) | collective-permute-done | bytes 40 | tf_op jit(solution)/shard_map/ppermute | solution.py:9
  102.2 7.0 %collective-permute-start.9 = (s32[4,1]{0,1:T(1,128)S(1)}, s32[4,1]{0,1:T(1,128)S(1)}, u32[]{:S(2)}, u32[]{:S(2)}) collective-permute-start(s32[4,1]{0,1:T(1,128)S(1)} %collective-permute-done.3), channel_id=1, source_target_pairs={{0,15},{1,0},{2,1},{3,2},{4,3},{5,4},{6,5},{7,6},{8,7},{9,8},{10,9... | collective-permute-start | bytes 56 | tf_op jit(solution)/shard_map/ppermute | solution.py:9
  109.3 9.3 %collective-permute-done.9 = s32[4,1]{0,1:T(1,128)S(1)} collective-permute-done((s32[4,1]{0,1:T(1,128)S(1)}, s32[4,1]{0,1:T(1,128)S(1)}, u32[]{:S(2)}, u32[]{:S(2)}) %collective-permute-start.9) | collective-permute-done | bytes 48 | tf_op jit(solution)/shard_map/ppermute | solution.py:9
  118.8 1.9 collective-permute-start.15
  120.7 10.1 %collective-permute-start.25 = (s32[2,1]{0,1:T(1,128)S(1)}, s32[2,1]{0,1:T(1,128)S(1)}, u32[]{:S(2)}, u32[]{:S(2)}) collective-permute-start(s32[2,1]{0,1:T(1,128)S(1)} %collective-permute-done.19), channel_id=1, source_target_pairs={{0,1008},{16,0},{32,16},{48,32},{64,48},{80,64},{96,80},{112,96},{... | collective-permute-start | bytes 32 | tf_op jit(solution)/shard_map/ppermute | solution.py:9
  130.8 2.9 collective-permute-done.25
  133.7 14.3 %collective-permute-start.6 = (s32[2,4]{1,0:T(2,128)S(1)}, s32[2,4]{1,0:T(2,128)S(1)}, u32[]{:S(2)}, u32[]{:S(2)}) collective-permute-start(s32[2,4]{1,0:T(2,128)S(1)} %collective-permute-done), channel_id=1, source_target_pairs={{0,1008},{16,0},{32,16},{48,32},{64,48},{80,64},{96,80},{112,96},{... | collective-permute-start | bytes 104 | tf_op jit(solution)/shard_map/ppermute | solution.py:9
  148.1 1.9 collective-permute-start.31
  150.1 10.9 %collective-permute-done.31 = s32[2,1]{0,1:T(1,128)S(1)} collective-permute-done((s32[2,1]{0,1:T(1,128)S(1)}, s32[2,1]{0,1:T(1,128)S(1)}, u32[]{:S(2)}, u32[]{:S(2)}) %collective-permute-start.31) | collective-permute-done | bytes 40 | tf_op jit(solution)/shard_map/ppermute | solution.py:9
  161.1 6.1 %collective-permute-start.37 = (s32[2,1]{0,1:T(1,128)S(1)}, s32[2,1]{0,1:T(1,128)S(1)}, u32[]{:S(2)}, u32[]{:S(2)}) collective-permute-start(s32[2,1]{0,1:T(1,128)S(1)} %collective-permute-done.31), channel_id=1, source_target_pairs={{0,1008},{16,0},{32,16},{48,32},{64,48},{80,64},{96,80},{112,96},{... | collective-permute-start | bytes 32 | tf_op jit(solution)/shard_map/ppermute | solution.py:9
  167.3 6.9 %collective-permute-done.37 = s32[2,1]{0,1:T(1,128)S(1)} collective-permute-done((s32[2,1]{0,1:T(1,128)S(1)}, s32[2,1]{0,1:T(1,128)S(1)}, u32[]{:S(2)}, u32[]{:S(2)}) %collective-permute-start.37) | collective-permute-done | bytes 40 | tf_op jit(solution)/shard_map/ppermute | solution.py:9
  174.1 10.7 %collective-permute-start.21 = (s32[4,1]{0,1:T(1,128)S(1)}, s32[4,1]{0,1:T(1,128)S(1)}, u32[]{:S(2)}, u32[]{:S(2)}) collective-permute-start(s32[4,1]{0,1:T(1,128)S(1)} %collective-permute-done.15), channel_id=1, source_target_pairs={{0,15},{1,0},{2,1},{3,2},{4,3},{5,4},{6,5},{7,6},{8,7},{9,8},{10,9... | collective-permute-start | bytes 56 | tf_op jit(solution)/shard_map/ppermute | solution.py:9
  185.9 2.4 collective-permute-start.8
  188.3 10.2 %collective-permute-start.27 = (s32[4,1]{0,1:T(1,128)S(1)}, s32[4,1]{0,1:T(1,128)S(1)}, u32[]{:S(2)}, u32[]{:S(2)}) collective-permute-start(s32[4,1]{0,1:T(1,128)S(1)} %collective-permute-done.21), channel_id=1, source_target_pairs={{0,15},{1,0},{2,1},{3,2},{4,3},{5,4},{6,5},{7,6},{8,7},{9,8},{10,9... | collective-permute-start | bytes 56 | tf_op jit(solution)/shard_map/ppermute | solution.py:9
  198.5 10.1 %collective-permute-start.12 = (s32[2,4]{1,0:T(2,128)S(1)}, s32[2,4]{1,0:T(2,128)S(1)}, u32[]{:S(2)}, u32[]{:S(2)}) collective-permute-start(s32[2,4]{1,0:T(2,128)S(1)} %collective-permute-done.6), channel_id=1, source_target_pairs={{0,1008},{16,0},{32,16},{48,32},{64,48},{80,64},{96,80},{112,96},{... | collective-permute-start | bytes 104 | tf_op jit(solution)/shard_map/ppermute | solution.py:9
  208.8 2.2 collective-permute-start.33
  211.6 14.3 %collective-permute-start.18 = (s32[2,4]{1,0:T(2,128)S(1)}, s32[2,4]{1,0:T(2,128)S(1)}, u32[]{:S(2)}, u32[]{:S(2)}) collective-permute-start(s32[2,4]{1,0:T(2,128)S(1)} %collective-permute-done.12), channel_id=1, source_target_pairs={{0,1008},{16,0},{32,16},{48,32},{64,48},{80,64},{96,80},{112,96},{... | collective-permute-start | bytes 104 | tf_op jit(solution)/shard_map/ppermute | solution.py:9
  226.0 3.3 collective-permute-start.39
  231.2 1.9 collective-permute-start.14
  233.1 9.9 %collective-permute-start.24 = (s32[2,4]{1,0:T(2,128)S(1)}, s32[2,4]{1,0:T(2,128)S(1)}, u32[]{:S(2)}, u32[]{:S(2)}) collective-permute-start(s32[2,4]{1,0:T(2,128)S(1)} %collective-permute-done.18), channel_id=1, source_target_pairs={{0,1008},{16,0},{32,16},{48,32},{64,48},{80,64},{96,80},{112,96},{... | collective-permute-start | bytes 104 | tf_op jit(solution)/shard_map/ppermute | solution.py:9
  243.1 3.1 collective-permute-done.24
  246.2 14.1 %collective-permute-start.30 = (s32[2,4]{1,0:T(2,128)S(1)}, s32[2,4]{1,0:T(2,128)S(1)}, u32[]{:S(2)}, u32[]{:S(2)}) collective-permute-start(s32[2,4]{1,0:T(2,128)S(1)} %collective-permute-done.24), channel_id=1, source_target_pairs={{0,1008},{16,0},{32,16},{48,32},{64,48},{80,64},{96,80},{112,96},{... | collective-permute-start | bytes 104 | tf_op jit(solution)/shard_map/ppermute | solution.py:9
  260.5 5.6 %collective-permute-start.20 = (s32[4,4]{1,0:T(4,128)S(1)}, s32[4,4]{1,0:T(4,128)S(1)}, u32[]{:S(2)}, u32[]{:S(2)}) collective-permute-start(s32[4,4]{1,0:T(4,128)S(1)} %collective-permute-done.14), channel_id=1, source_target_pairs={{0,15},{1,0},{2,1},{3,2},{4,3},{5,4},{6,5},{7,6},{8,7},{9,8},{10,9... | collective-permute-start | bytes 200 | tf_op jit(solution)/shard_map/ppermute | solution.py:9
  266.2 11.3 %collective-permute-start.36 = (s32[2,4]{1,0:T(2,128)S(1)}, s32[2,4]{1,0:T(2,128)S(1)}, u32[]{:S(2)}, u32[]{:S(2)}) collective-permute-start(s32[2,4]{1,0:T(2,128)S(1)} %collective-permute-done.30), channel_id=1, source_target_pairs={{0,1008},{16,0},{32,16},{48,32},{64,48},{80,64},{96,80},{112,96},{... | collective-permute-start | bytes 104 | tf_op jit(solution)/shard_map/ppermute | solution.py:9
  279.3 6.4 %collective-permute-start.26 = (s32[4,4]{1,0:T(4,128)S(1)}, s32[4,4]{1,0:T(4,128)S(1)}, u32[]{:S(2)}, u32[]{:S(2)}) collective-permute-start(s32[4,4]{1,0:T(4,128)S(1)} %collective-permute-done.20), channel_id=1, source_target_pairs={{0,15},{1,0},{2,1},{3,2},{4,3},{5,4},{6,5},{7,6},{8,7},{9,8},{10,9... | collective-permute-start | bytes 200 | tf_op jit(solution)/shard_map/ppermute | solution.py:9
  286.6 2.4 collective-permute-start.32
  289.1 2.4 collective-permute-done.32
  291.5 9.0 %collective-permute-start.38 = (s32[4,4]{1,0:T(4,128)S(1)}, s32[4,4]{1,0:T(4,128)S(1)}, u32[]{:S(2)}, u32[]{:S(2)}) collective-permute-start(s32[4,4]{1,0:T(4,128)S(1)} %collective-permute-done.32), channel_id=1, source_target_pairs={{0,15},{1,0},{2,1},{3,2},{4,3},{5,4},{6,5},{7,6},{8,7},{9,8},{10,9... | collective-permute-start | bytes 200 | tf_op jit(solution)/shard_map/ppermute | solution.py:9
  301.4 17.0 %collective-permute-start.11 = (bf16[2,4,128,128]{3,2,1,0:T(8,128)(2,1)S(1)}, bf16[2,4,128,128]{3,2,1,0:T(8,128)(2,1)S(1)}, u32[]{:S(2)}, u32[]{:S(2)}) collective-permute-start(bf16[2,4,128,128]{3,2,1,0:T(8,128)(2,1)S(1)} %collective-permute-done.5), channel_id=1, source_target_pairs={{0,1008},{16,0},{32,16},{48,32},{64,48},{80,64},{96,80},{112,96},{... | collective-permute-start | bytes 786440 | tf_op jit(solution)/shard_map/ppermute | solution.py:9
  318.6 11.4 %collective-permute-start.10 = (bf16[4,4,128,128]{3,2,1,0:T(8,128)(2,1)S(1)}, bf16[4,4,128,128]{3,2,1,0:T(8,128)(2,1)S(1)}, u32[]{:S(2)}, u32[]{:S(2)}) collective-permute-start(bf16[4,4,128,128]{3,2,1,0:T(8,128)(2,1)S(1)} %collective-permute-done.4), channel_id=1, source_target_pairs={{0,15},{1,0},{2,1},{3,2},{4,3},{5,4},{6,5},{7,6},{8,7},{9,8},{10,9... | collective-permute-start | bytes 1572872 | tf_op jit(solution)/shard_map/ppermute | solution.py:9
  330.0 6.6 %collective-permute-done.11 = bf16[2,4,128,128]{3,2,1,0:T(8,128)(2,1)S(1)} collective-permute-done((bf16[2,4,128,128]{3,2,1,0:T(8,128)(2,1)S(1)}, bf16[2,4,128,128]{3,2,1,0:T(8,128)(2,1)S(1)}, u32[]{:S(2)}, u32[]{:S(2)}) %collective-permute-start.11) | collective-permute-done | bytes 262176 | tf_op jit(solution)/shard_map/ppermute | solution.py:9
  336.5 2.2 collective-permute-start.17
  339.2 21.4 %collective-permute-done.17 = bf16[2,4,128,128]{3,2,1,0:T(8,128)(2,1)S(1)} collective-permute-done((bf16[2,4,128,128]{3,2,1,0:T(8,128)(2,1)S(1)}, bf16[2,4,128,128]{3,2,1,0:T(8,128)(2,1)S(1)}, u32[]{:S(2)}, u32[]{:S(2)}) %collective-permute-start.17) | collective-permute-done | bytes 262176 | tf_op jit(solution)/shard_map/ppermute | solution.py:9
  360.6 8.3 %collective-permute-start.23 = (bf16[2,4,128,128]{3,2,1,0:T(8,128)(2,1)S(1)}, bf16[2,4,128,128]{3,2,1,0:T(8,128)(2,1)S(1)}, u32[]{:S(2)}, u32[]{:S(2)}) collective-permute-start(bf16[2,4,128,128]{3,2,1,0:T(8,128)(2,1)S(1)} %collective-permute-done.17), channel_id=1, source_target_pairs={{0,1008},{16,0},{32,16},{48,32},{64,48},{80,64},{96,80},{112,96},{... | collective-permute-start | bytes 786440 | tf_op jit(solution)/shard_map/ppermute | solution.py:9
  368.9 2.3 fusion.12
  371.2 19.0 %collective-permute-start.16 = (bf16[4,4,128,128]{3,2,1,0:T(8,128)(2,1)S(1)}, bf16[4,4,128,128]{3,2,1,0:T(8,128)(2,1)S(1)}, u32[]{:S(2)}, u32[]{:S(2)}) collective-permute-start(bf16[4,4,128,128]{3,2,1,0:T(8,128)(2,1)S(1)} %collective-permute-done.10), channel_id=1, source_target_pairs={{0,15},{1,0},{2,1},{3,2},{4,3},{5,4},{6,5},{7,6},{8,7},{9,8},{10,9... | collective-permute-start | bytes 1572872 | tf_op jit(solution)/shard_map/ppermute | solution.py:9
  390.3 4.5 collective-permute-start.29
  395.1 2.3 fusion.10
  397.5 19.1 %collective-permute-done.29 = bf16[2,4,128,128]{3,2,1,0:T(8,128)(2,1)S(1)} collective-permute-done((bf16[2,4,128,128]{3,2,1,0:T(8,128)(2,1)S(1)}, bf16[2,4,128,128]{3,2,1,0:T(8,128)(2,1)S(1)}, u32[]{:S(2)}, u32[]{:S(2)}) %collective-permute-start.29) | collective-permute-done | bytes 262176 | tf_op jit(solution)/shard_map/ppermute | solution.py:9
  416.5 9.3 %collective-permute-start.35 = (bf16[2,4,128,128]{3,2,1,0:T(8,128)(2,1)S(1)}, bf16[2,4,128,128]{3,2,1,0:T(8,128)(2,1)S(1)}, u32[]{:S(2)}, u32[]{:S(2)}) collective-permute-start(bf16[2,4,128,128]{3,2,1,0:T(8,128)(2,1)S(1)} %collective-permute-done.29), channel_id=1, source_target_pairs={{0,1008},{16,0},{32,16},{48,32},{64,48},{80,64},{96,80},{112,96},{... | collective-permute-start | bytes 786440 | tf_op jit(solution)/shard_map/ppermute | solution.py:9
  425.8 35.4 %collective-permute-start.22 = (bf16[4,4,128,128]{3,2,1,0:T(8,128)(2,1)S(1)}, bf16[4,4,128,128]{3,2,1,0:T(8,128)(2,1)S(1)}, u32[]{:S(2)}, u32[]{:S(2)}) collective-permute-start(bf16[4,4,128,128]{3,2,1,0:T(8,128)(2,1)S(1)} %collective-permute-done.16), channel_id=1, source_target_pairs={{0,15},{1,0},{2,1},{3,2},{4,3},{5,4},{6,5},{7,6},{8,7},{9,8},{10,9... | collective-permute-start | bytes 1572872 | tf_op jit(solution)/shard_map/ppermute | solution.py:9
  461.6 2.3 fusion.8
  463.9 1.9 collective-permute-start.41
  465.9 18.7 %collective-permute-start.28 = (bf16[4,4,128,128]{3,2,1,0:T(8,128)(2,1)S(1)}, bf16[4,4,128,128]{3,2,1,0:T(8,128)(2,1)S(1)}, u32[]{:S(2)}, u32[]{:S(2)}) collective-permute-start(bf16[4,4,128,128]{3,2,1,0:T(8,128)(2,1)S(1)} %collective-permute-done.22), channel_id=1, source_target_pairs={{0,15},{1,0},{2,1},{3,2},{4,3},{5,4},{6,5},{7,6},{8,7},{9,8},{10,9... | collective-permute-start | bytes 1572872 | tf_op jit(solution)/shard_map/ppermute | solution.py:9
  485.0 2.3 fusion.6
  487.3 10.7 %collective-permute-start.34 = (bf16[4,4,128,128]{3,2,1,0:T(8,128)(2,1)S(1)}, bf16[4,4,128,128]{3,2,1,0:T(8,128)(2,1)S(1)}, u32[]{:S(2)}, u32[]{:S(2)}) collective-permute-start(bf16[4,4,128,128]{3,2,1,0:T(8,128)(2,1)S(1)} %collective-permute-done.28), channel_id=1, source_target_pairs={{0,15},{1,0},{2,1},{3,2},{4,3},{5,4},{6,5},{7,6},{8,7},{9,8},{10,9... | collective-permute-start | bytes 1572872 | tf_op jit(solution)/shard_map/ppermute | solution.py:9
  498.5 2.3 fusion.4
  500.8 14.6 %collective-permute-start.40 = (bf16[4,4,128,128]{3,2,1,0:T(8,128)(2,1)S(1)}, bf16[4,4,128,128]{3,2,1,0:T(8,128)(2,1)S(1)}, u32[]{:S(2)}, u32[]{:S(2)}) collective-permute-start(bf16[4,4,128,128]{3,2,1,0:T(8,128)(2,1)S(1)} %collective-permute-done.34), channel_id=1, source_target_pairs={{0,15},{1,0},{2,1},{3,2},{4,3},{5,4},{6,5},{7,6},{8,7},{9,8},{10,9... | collective-permute-start | bytes 1572872 | tf_op jit(solution)/shard_map/ppermute | solution.py:9
  515.8 2.3 fusion.2
  518.5 2.3 fusion
  520.9 2.6 fusion.23
  (115 shorter events, 14.2 us)
Async XLA Ops:
  0.0 42.6 %copy-start.2 = (s32[4,4]{1,0:T(4,128)S(1)}, s32[4,4]{1,0:T(4,128)}, u32[]{:S(2)}) copy-start(s32[4,4]{1,0:T(4,128)} %param.8) | copy-start | bytes 196
  0.0 42.6 %copy-start.5 = (s32[4,1]{0,1:T(1,128)S(1)}, s32[4,1]{0,1:T(1,128)}, u32[]{:S(2)}) copy-start(s32[4,1]{0,1:T(1,128)} %param.9) | copy-start | bytes 52
  0.0 318.6 %collective-permute-start.4 = (bf16[4,4,128,128]{3,2,1,0:T(8,128)(2,1)}, bf16[4,4,128,128]{3,2,1,0:T(8,128)(2,1)S(1)}, u32[]{:S(2)}, u32[]{:S(2)}) collective-permute-start(bf16[4,4,128,128]{3,2,1,0:T(8,128)(2,1)} %param.7), channel_id=1, source_target_pairs={{0,15},{1,0},{2,1},{3,2},{4,3},{5,4},{6,5},{7,6},{8,7},{9,8},{10,9... | collective-permute-start | bytes 1572872 | tf_op jit(solution)/shard_map/ppermute | solution.py:9
  16.2 285.2 %collective-permute-start.5 = (bf16[2,4,128,128]{3,2,1,0:T(8,128)(2,1)}, bf16[2,4,128,128]{3,2,1,0:T(8,128)(2,1)S(1)}, u32[]{:S(2)}, u32[]{:S(2)}) collective-permute-start(bf16[2,4,128,128]{3,2,1,0:T(8,128)(2,1)} %param.10), channel_id=1, source_target_pairs={{0,1008},{16,0},{32,16},{48,32},{64,48},{80,64},{96,80},{112,96},{... | collective-permute-start | bytes 786440 | tf_op jit(solution)/shard_map/ppermute | solution.py:9
  27.7 158.0 %collective-permute-start.2 = (s32[4,4]{1,0:T(4,128)}, s32[4,4]{1,0:T(4,128)S(1)}, u32[]{:S(2)}, u32[]{:S(2)}) collective-permute-start(s32[4,4]{1,0:T(4,128)} %param.8), channel_id=1, source_target_pairs={{0,15},{1,0},{2,1},{3,2},{4,3},{5,4},{6,5},{7,6},{8,7},{9,8},{10,9... | collective-permute-start | bytes 200 | tf_op jit(solution)/shard_map/ppermute | solution.py:9
  36.3 39.7 %collective-permute-start.3 = (s32[4,1]{0,1:T(1,128)}, s32[4,1]{0,1:T(1,128)S(1)}, u32[]{:S(2)}, u32[]{:S(2)}) collective-permute-start(s32[4,1]{0,1:T(1,128)} %param.9), channel_id=1, source_target_pairs={{0,15},{1,0},{2,1},{3,2},{4,3},{5,4},{6,5},{7,6},{8,7},{9,8},{10,9... | collective-permute-start | bytes 56 | tf_op jit(solution)/shard_map/ppermute | solution.py:9
  38.6 13.2 %collective-permute-start.1 = (s32[2,1]{0,1:T(1,128)}, s32[2,1]{0,1:T(1,128)S(1)}, u32[]{:S(2)}, u32[]{:S(2)}) collective-permute-start(s32[2,1]{0,1:T(1,128)} %param.12), channel_id=1, source_target_pairs={{0,1008},{16,0},{32,16},{48,32},{64,48},{80,64},{96,80},{112,96},{... | collective-permute-start | bytes 32 | tf_op jit(solution)/shard_map/ppermute | solution.py:9
  42.6 2.0 copy-start.4
  42.6 2.0 copy-start.1
  42.7 2.2 copy-start.3
  51.9 13.0 %collective-permute-start.7 = (s32[2,1]{0,1:T(1,128)S(1)}, s32[2,1]{0,1:T(1,128)S(1)}, u32[]{:S(2)}, u32[]{:S(2)}) collective-permute-start(s32[2,1]{0,1:T(1,128)S(1)} %collective-permute-done.1), channel_id=1, source_target_pairs={{0,1008},{16,0},{32,16},{48,32},{64,48},{80,64},{96,80},{112,96},{... | collective-permute-start | bytes 32 | tf_op jit(solution)/shard_map/ppermute | solution.py:9
  64.9 55.8 %collective-permute-start = (s32[2,4]{1,0:T(2,128)S(1)}, s32[2,4]{1,0:T(2,128)S(1)}, u32[]{:S(2)}, u32[]{:S(2)}) collective-permute-start(s32[2,4]{1,0:T(2,128)S(1)} %copy-done.1), channel_id=1, source_target_pairs={{0,1008},{16,0},{32,16},{48,32},{64,48},{80,64},{96,80},{112,96},{... | collective-permute-start | bytes 104 | tf_op jit(solution)/shard_map/ppermute | solution.py:9
  76.1 13.0 %collective-permute-start.13 = (s32[2,1]{0,1:T(1,128)S(1)}, s32[2,1]{0,1:T(1,128)S(1)}, u32[]{:S(2)}, u32[]{:S(2)}) collective-permute-start(s32[2,1]{0,1:T(1,128)S(1)} %collective-permute-done.7), channel_id=1, source_target_pairs={{0,1008},{16,0},{32,16},{48,32},{64,48},{80,64},{96,80},{112,96},{... | collective-permute-start | bytes 32 | tf_op jit(solution)/shard_map/ppermute | solution.py:9
  89.2 13.0 %collective-permute-start.19 = (s32[2,1]{0,1:T(1,128)S(1)}, s32[2,1]{0,1:T(1,128)S(1)}, u32[]{:S(2)}, u32[]{:S(2)}) collective-permute-start(s32[2,1]{0,1:T(1,128)S(1)} %collective-permute-done.13), channel_id=1, source_target_pairs={{0,1008},{16,0},{32,16},{48,32},{64,48},{80,64},{96,80},{112,96},{... | collective-permute-start | bytes 32 | tf_op jit(solution)/shard_map/ppermute | solution.py:9
  102.2 16.4 %collective-permute-start.9 = (s32[4,1]{0,1:T(1,128)S(1)}, s32[4,1]{0,1:T(1,128)S(1)}, u32[]{:S(2)}, u32[]{:S(2)}) collective-permute-start(s32[4,1]{0,1:T(1,128)S(1)} %collective-permute-done.3), channel_id=1, source_target_pairs={{0,15},{1,0},{2,1},{3,2},{4,3},{5,4},{6,5},{7,6},{8,7},{9,8},{10,9... | collective-permute-start | bytes 56 | tf_op jit(solution)/shard_map/ppermute | solution.py:9
  118.8 29.3 %collective-permute-start.15 = (s32[4,1]{0,1:T(1,128)S(1)}, s32[4,1]{0,1:T(1,128)S(1)}, u32[]{:S(2)}, u32[]{:S(2)}) collective-permute-start(s32[4,1]{0,1:T(1,128)S(1)} %collective-permute-done.9), channel_id=1, source_target_pairs={{0,15},{1,0},{2,1},{3,2},{4,3},{5,4},{6,5},{7,6},{8,7},{9,8},{10,9... | collective-permute-start | bytes 56 | tf_op jit(solution)/shard_map/ppermute | solution.py:9
  120.7 13.0 %collective-permute-start.25 = (s32[2,1]{0,1:T(1,128)S(1)}, s32[2,1]{0,1:T(1,128)S(1)}, u32[]{:S(2)}, u32[]{:S(2)}) collective-permute-start(s32[2,1]{0,1:T(1,128)S(1)} %collective-permute-done.19), channel_id=1, source_target_pairs={{0,1008},{16,0},{32,16},{48,32},{64,48},{80,64},{96,80},{112,96},{... | collective-permute-start | bytes 32 | tf_op jit(solution)/shard_map/ppermute | solution.py:9
  133.7 64.8 %collective-permute-start.6 = (s32[2,4]{1,0:T(2,128)S(1)}, s32[2,4]{1,0:T(2,128)S(1)}, u32[]{:S(2)}, u32[]{:S(2)}) collective-permute-start(s32[2,4]{1,0:T(2,128)S(1)} %collective-permute-done), channel_id=1, source_target_pairs={{0,1008},{16,0},{32,16},{48,32},{64,48},{80,64},{96,80},{112,96},{... | collective-permute-start | bytes 104 | tf_op jit(solution)/shard_map/ppermute | solution.py:9
  148.1 13.0 %collective-permute-start.31 = (s32[2,1]{0,1:T(1,128)S(1)}, s32[2,1]{0,1:T(1,128)S(1)}, u32[]{:S(2)}, u32[]{:S(2)}) collective-permute-start(s32[2,1]{0,1:T(1,128)S(1)} %collective-permute-done.25), channel_id=1, source_target_pairs={{0,1008},{16,0},{32,16},{48,32},{64,48},{80,64},{96,80},{112,96},{... | collective-permute-start | bytes 32 | tf_op jit(solution)/shard_map/ppermute | solution.py:9
  161.1 13.0 %collective-permute-start.37 = (s32[2,1]{0,1:T(1,128)S(1)}, s32[2,1]{0,1:T(1,128)S(1)}, u32[]{:S(2)}, u32[]{:S(2)}) collective-permute-start(s32[2,1]{0,1:T(1,128)S(1)} %collective-permute-done.31), channel_id=1, source_target_pairs={{0,1008},{16,0},{32,16},{48,32},{64,48},{80,64},{96,80},{112,96},{... | collective-permute-start | bytes 32 | tf_op jit(solution)/shard_map/ppermute | solution.py:9
  174.1 11.5 %collective-permute-start.21 = (s32[4,1]{0,1:T(1,128)S(1)}, s32[4,1]{0,1:T(1,128)S(1)}, u32[]{:S(2)}, u32[]{:S(2)}) collective-permute-start(s32[4,1]{0,1:T(1,128)S(1)} %collective-permute-done.15), channel_id=1, source_target_pairs={{0,15},{1,0},{2,1},{3,2},{4,3},{5,4},{6,5},{7,6},{8,7},{9,8},{10,9... | collective-permute-start | bytes 56 | tf_op jit(solution)/shard_map/ppermute | solution.py:9
  185.9 45.1 %collective-permute-start.8 = (s32[4,4]{1,0:T(4,128)S(1)}, s32[4,4]{1,0:T(4,128)S(1)}, u32[]{:S(2)}, u32[]{:S(2)}) collective-permute-start(s32[4,4]{1,0:T(4,128)S(1)} %collective-permute-done.2), channel_id=1, source_target_pairs={{0,15},{1,0},{2,1},{3,2},{4,3},{5,4},{6,5},{7,6},{8,7},{9,8},{10,9... | collective-permute-start | bytes 200 | tf_op jit(solution)/shard_map/ppermute | solution.py:9
  188.3 20.3 %collective-permute-start.27 = (s32[4,1]{0,1:T(1,128)S(1)}, s32[4,1]{0,1:T(1,128)S(1)}, u32[]{:S(2)}, u32[]{:S(2)}) collective-permute-start(s32[4,1]{0,1:T(1,128)S(1)} %collective-permute-done.21), channel_id=1, source_target_pairs={{0,15},{1,0},{2,1},{3,2},{4,3},{5,4},{6,5},{7,6},{8,7},{9,8},{10,9... | collective-permute-start | bytes 56 | tf_op jit(solution)/shard_map/ppermute | solution.py:9
  198.5 13.0 %collective-permute-start.12 = (s32[2,4]{1,0:T(2,128)S(1)}, s32[2,4]{1,0:T(2,128)S(1)}, u32[]{:S(2)}, u32[]{:S(2)}) collective-permute-start(s32[2,4]{1,0:T(2,128)S(1)} %collective-permute-done.6), channel_id=1, source_target_pairs={{0,1008},{16,0},{32,16},{48,32},{64,48},{80,64},{96,80},{112,96},{... | collective-permute-start | bytes 104 | tf_op jit(solution)/shard_map/ppermute | solution.py:9
  208.8 17.1 %collective-permute-start.33 = (s32[4,1]{0,1:T(1,128)S(1)}, s32[4,1]{0,1:T(1,128)S(1)}, u32[]{:S(2)}, u32[]{:S(2)}) collective-permute-start(s32[4,1]{0,1:T(1,128)S(1)} %collective-permute-done.27), channel_id=1, source_target_pairs={{0,15},{1,0},{2,1},{3,2},{4,3},{5,4},{6,5},{7,6},{8,7},{9,8},{10,9... | collective-permute-start | bytes 56 | tf_op jit(solution)/shard_map/ppermute | solution.py:9
  211.6 21.6 %collective-permute-start.18 = (s32[2,4]{1,0:T(2,128)S(1)}, s32[2,4]{1,0:T(2,128)S(1)}, u32[]{:S(2)}, u32[]{:S(2)}) collective-permute-start(s32[2,4]{1,0:T(2,128)S(1)} %collective-permute-done.12), channel_id=1, source_target_pairs={{0,1008},{16,0},{32,16},{48,32},{64,48},{80,64},{96,80},{112,96},{... | collective-permute-start | bytes 104 | tf_op jit(solution)/shard_map/ppermute | solution.py:9
  226.0 4.8 collective-permute-start.39
  231.2 29.1 %collective-permute-start.14 = (s32[4,4]{1,0:T(4,128)S(1)}, s32[4,4]{1,0:T(4,128)S(1)}, u32[]{:S(2)}, u32[]{:S(2)}) collective-permute-start(s32[4,4]{1,0:T(4,128)S(1)} %collective-permute-done.8), channel_id=1, source_target_pairs={{0,15},{1,0},{2,1},{3,2},{4,3},{5,4},{6,5},{7,6},{8,7},{9,8},{10,9... | collective-permute-start | bytes 200 | tf_op jit(solution)/shard_map/ppermute | solution.py:9
  233.1 13.0 %collective-permute-start.24 = (s32[2,4]{1,0:T(2,128)S(1)}, s32[2,4]{1,0:T(2,128)S(1)}, u32[]{:S(2)}, u32[]{:S(2)}) collective-permute-start(s32[2,4]{1,0:T(2,128)S(1)} %collective-permute-done.18), channel_id=1, source_target_pairs={{0,1008},{16,0},{32,16},{48,32},{64,48},{80,64},{96,80},{112,96},{... | collective-permute-start | bytes 104 | tf_op jit(solution)/shard_map/ppermute | solution.py:9
  246.2 20.0 %collective-permute-start.30 = (s32[2,4]{1,0:T(2,128)S(1)}, s32[2,4]{1,0:T(2,128)S(1)}, u32[]{:S(2)}, u32[]{:S(2)}) collective-permute-start(s32[2,4]{1,0:T(2,128)S(1)} %collective-permute-done.24), channel_id=1, source_target_pairs={{0,1008},{16,0},{32,16},{48,32},{64,48},{80,64},{96,80},{112,96},{... | collective-permute-start | bytes 104 | tf_op jit(solution)/shard_map/ppermute | solution.py:9
  260.5 18.7 %collective-permute-start.20 = (s32[4,4]{1,0:T(4,128)S(1)}, s32[4,4]{1,0:T(4,128)S(1)}, u32[]{:S(2)}, u32[]{:S(2)}) collective-permute-start(s32[4,4]{1,0:T(4,128)S(1)} %collective-permute-done.14), channel_id=1, source_target_pairs={{0,15},{1,0},{2,1},{3,2},{4,3},{5,4},{6,5},{7,6},{8,7},{9,8},{10,9... | collective-permute-start | bytes 200 | tf_op jit(solution)/shard_map/ppermute | solution.py:9
  266.2 13.0 %collective-permute-start.36 = (s32[2,4]{1,0:T(2,128)S(1)}, s32[2,4]{1,0:T(2,128)S(1)}, u32[]{:S(2)}, u32[]{:S(2)}) collective-permute-start(s32[2,4]{1,0:T(2,128)S(1)} %collective-permute-done.30), channel_id=1, source_target_pairs={{0,1008},{16,0},{32,16},{48,32},{64,48},{80,64},{96,80},{112,96},{... | collective-permute-start | bytes 104 | tf_op jit(solution)/shard_map/ppermute | solution.py:9
  279.3 7.2 %collective-permute-start.26 = (s32[4,4]{1,0:T(4,128)S(1)}, s32[4,4]{1,0:T(4,128)S(1)}, u32[]{:S(2)}, u32[]{:S(2)}) collective-permute-start(s32[4,4]{1,0:T(4,128)S(1)} %collective-permute-done.20), channel_id=1, source_target_pairs={{0,15},{1,0},{2,1},{3,2},{4,3},{5,4},{6,5},{7,6},{8,7},{9,8},{10,9... | collective-permute-start | bytes 200 | tf_op jit(solution)/shard_map/ppermute | solution.py:9
  286.6 4.9 collective-permute-start.32
  291.5 9.8 %collective-permute-start.38 = (s32[4,4]{1,0:T(4,128)S(1)}, s32[4,4]{1,0:T(4,128)S(1)}, u32[]{:S(2)}, u32[]{:S(2)}) collective-permute-start(s32[4,4]{1,0:T(4,128)S(1)} %collective-permute-done.32), channel_id=1, source_target_pairs={{0,15},{1,0},{2,1},{3,2},{4,3},{5,4},{6,5},{7,6},{8,7},{9,8},{10,9... | collective-permute-start | bytes 200 | tf_op jit(solution)/shard_map/ppermute | solution.py:9
  301.4 35.2 %collective-permute-start.11 = (bf16[2,4,128,128]{3,2,1,0:T(8,128)(2,1)S(1)}, bf16[2,4,128,128]{3,2,1,0:T(8,128)(2,1)S(1)}, u32[]{:S(2)}, u32[]{:S(2)}) collective-permute-start(bf16[2,4,128,128]{3,2,1,0:T(8,128)(2,1)S(1)} %collective-permute-done.5), channel_id=1, source_target_pairs={{0,1008},{16,0},{32,16},{48,32},{64,48},{80,64},{96,80},{112,96},{... | collective-permute-start | bytes 786440 | tf_op jit(solution)/shard_map/ppermute | solution.py:9
  318.6 52.6 %collective-permute-start.10 = (bf16[4,4,128,128]{3,2,1,0:T(8,128)(2,1)S(1)}, bf16[4,4,128,128]{3,2,1,0:T(8,128)(2,1)S(1)}, u32[]{:S(2)}, u32[]{:S(2)}) collective-permute-start(bf16[4,4,128,128]{3,2,1,0:T(8,128)(2,1)S(1)} %collective-permute-done.4), channel_id=1, source_target_pairs={{0,15},{1,0},{2,1},{3,2},{4,3},{5,4},{6,5},{7,6},{8,7},{9,8},{10,9... | collective-permute-start | bytes 1572872 | tf_op jit(solution)/shard_map/ppermute | solution.py:9
  336.5 24.1 %collective-permute-start.17 = (bf16[2,4,128,128]{3,2,1,0:T(8,128)(2,1)S(1)}, bf16[2,4,128,128]{3,2,1,0:T(8,128)(2,1)S(1)}, u32[]{:S(2)}, u32[]{:S(2)}) collective-permute-start(bf16[2,4,128,128]{3,2,1,0:T(8,128)(2,1)S(1)} %collective-permute-done.11), channel_id=1, source_target_pairs={{0,1008},{16,0},{32,16},{48,32},{64,48},{80,64},{96,80},{112,96},{... | collective-permute-start | bytes 786440 | tf_op jit(solution)/shard_map/ppermute | solution.py:9
  360.6 29.6 %collective-permute-start.23 = (bf16[2,4,128,128]{3,2,1,0:T(8,128)(2,1)S(1)}, bf16[2,4,128,128]{3,2,1,0:T(8,128)(2,1)S(1)}, u32[]{:S(2)}, u32[]{:S(2)}) collective-permute-start(bf16[2,4,128,128]{3,2,1,0:T(8,128)(2,1)S(1)} %collective-permute-done.17), channel_id=1, source_target_pairs={{0,1008},{16,0},{32,16},{48,32},{64,48},{80,64},{96,80},{112,96},{... | collective-permute-start | bytes 786440 | tf_op jit(solution)/shard_map/ppermute | solution.py:9
  371.2 54.5 %collective-permute-start.16 = (bf16[4,4,128,128]{3,2,1,0:T(8,128)(2,1)S(1)}, bf16[4,4,128,128]{3,2,1,0:T(8,128)(2,1)S(1)}, u32[]{:S(2)}, u32[]{:S(2)}) collective-permute-start(bf16[4,4,128,128]{3,2,1,0:T(8,128)(2,1)S(1)} %collective-permute-done.10), channel_id=1, source_target_pairs={{0,15},{1,0},{2,1},{3,2},{4,3},{5,4},{6,5},{7,6},{8,7},{9,8},{10,9... | collective-permute-start | bytes 1572872 | tf_op jit(solution)/shard_map/ppermute | solution.py:9
  390.3 26.3 %collective-permute-start.29 = (bf16[2,4,128,128]{3,2,1,0:T(8,128)(2,1)S(1)}, bf16[2,4,128,128]{3,2,1,0:T(8,128)(2,1)S(1)}, u32[]{:S(2)}, u32[]{:S(2)}) collective-permute-start(bf16[2,4,128,128]{3,2,1,0:T(8,128)(2,1)S(1)} %collective-permute-done.23), channel_id=1, source_target_pairs={{0,1008},{16,0},{32,16},{48,32},{64,48},{80,64},{96,80},{112,96},{... | collective-permute-start | bytes 786440 | tf_op jit(solution)/shard_map/ppermute | solution.py:9
  416.5 47.4 %collective-permute-start.35 = (bf16[2,4,128,128]{3,2,1,0:T(8,128)(2,1)S(1)}, bf16[2,4,128,128]{3,2,1,0:T(8,128)(2,1)S(1)}, u32[]{:S(2)}, u32[]{:S(2)}) collective-permute-start(bf16[2,4,128,128]{3,2,1,0:T(8,128)(2,1)S(1)} %collective-permute-done.29), channel_id=1, source_target_pairs={{0,1008},{16,0},{32,16},{48,32},{64,48},{80,64},{96,80},{112,96},{... | collective-permute-start | bytes 786440 | tf_op jit(solution)/shard_map/ppermute | solution.py:9
  425.8 40.1 %collective-permute-start.22 = (bf16[4,4,128,128]{3,2,1,0:T(8,128)(2,1)S(1)}, bf16[4,4,128,128]{3,2,1,0:T(8,128)(2,1)S(1)}, u32[]{:S(2)}, u32[]{:S(2)}) collective-permute-start(bf16[4,4,128,128]{3,2,1,0:T(8,128)(2,1)S(1)} %collective-permute-done.16), channel_id=1, source_target_pairs={{0,15},{1,0},{2,1},{3,2},{4,3},{5,4},{6,5},{7,6},{8,7},{9,8},{10,9... | collective-permute-start | bytes 1572872 | tf_op jit(solution)/shard_map/ppermute | solution.py:9
  463.9 54.2 %collective-permute-start.41 = (bf16[2,4,128,128]{3,2,1,0:T(8,128)(2,1)S(1)}, bf16[2,4,128,128]{3,2,1,0:T(8,128)(2,1)S(1)}, u32[]{:S(2)}, u32[]{:S(2)}) collective-permute-start(bf16[2,4,128,128]{3,2,1,0:T(8,128)(2,1)S(1)} %collective-permute-done.35), channel_id=1, source_target_pairs={{0,1008},{16,0},{32,16},{48,32},{64,48},{80,64},{96,80},{112,96},{... | collective-permute-start | bytes 786440 | tf_op jit(solution)/shard_map/ppermute | solution.py:9
  465.9 21.4 %collective-permute-start.28 = (bf16[4,4,128,128]{3,2,1,0:T(8,128)(2,1)S(1)}, bf16[4,4,128,128]{3,2,1,0:T(8,128)(2,1)S(1)}, u32[]{:S(2)}, u32[]{:S(2)}) collective-permute-start(bf16[4,4,128,128]{3,2,1,0:T(8,128)(2,1)S(1)} %collective-permute-done.22), channel_id=1, source_target_pairs={{0,15},{1,0},{2,1},{3,2},{4,3},{5,4},{6,5},{7,6},{8,7},{9,8},{10,9... | collective-permute-start | bytes 1572872 | tf_op jit(solution)/shard_map/ppermute | solution.py:9
  487.3 13.4 %collective-permute-start.34 = (bf16[4,4,128,128]{3,2,1,0:T(8,128)(2,1)S(1)}, bf16[4,4,128,128]{3,2,1,0:T(8,128)(2,1)S(1)}, u32[]{:S(2)}, u32[]{:S(2)}) collective-permute-start(bf16[4,4,128,128]{3,2,1,0:T(8,128)(2,1)S(1)} %collective-permute-done.28), channel_id=1, source_target_pairs={{0,15},{1,0},{2,1},{3,2},{4,3},{5,4},{6,5},{7,6},{8,7},{9,8},{10,9... | collective-permute-start | bytes 1572872 | tf_op jit(solution)/shard_map/ppermute | solution.py:9
  500.8 17.3 %collective-permute-start.40 = (bf16[4,4,128,128]{3,2,1,0:T(8,128)(2,1)S(1)}, bf16[4,4,128,128]{3,2,1,0:T(8,128)(2,1)S(1)}, u32[]{:S(2)}, u32[]{:S(2)}) collective-permute-start(bf16[4,4,128,128]{3,2,1,0:T(8,128)(2,1)S(1)} %collective-permute-done.34), channel_id=1, source_target_pairs={{0,15},{1,0},{2,1},{3,2},{4,3},{5,4},{6,5},{7,6},{8,7},{9,8},{10,9... | collective-permute-start | bytes 1572872 | tf_op jit(solution)/shard_map/ppermute | solution.py:9
  518.1 2.8 copy-start
where the time goes:
time: 531 us; the launch traced here: 524 us
  starting transfers between devices  378 us (71%)
  waiting for transfers between devices  117 us (22%)
  matrix products  23.2 us (4%)
    ppermute x42, starting transfers between devices, passed_along(): return lax.ppermute(x, axis, [(i, (i + by) % peers) for i in range(peers)])  378 us
    ppermute x42, waiting for transfers between devices, passed_along(): return lax.ppermute(x, axis, [(i, (i + by) % peers) for i in range(peers)])  117 us
    dot_general x8, matrix products, block_products(): jnp.dot(weight, products.reshape(weight.shape[1], -1), precision=lax.Prec...  18.8 us
  transfers between devices with their start and end apart: 42, of which 19 were waited for; matrix products, arithmetic and copies ran while one was open for 4% of the time, Pallas kernels for 0%

commit v1 on v0

v1 whole, which is shorter than its diff:
```python
import functools

import jax
import jax.numpy as jnp
from jax import lax
from jax.experimental import pallas as pl
from jax.experimental.pallas import tpu as pltpu
from jax.sharding import PartitionSpec as P

BS = 128
VALUES = 4 * BS
ROWS = VALUES + 16
STEPS = 16.0
TOP = 32767.0
FLOOR = 2.0**-100


def level_of(biggest):
    return jnp.ceil(STEPS * jnp.log2(jnp.maximum(biggest, FLOOR))) + 1.0


def coded(values, level):
    scaled = values * (TOP * jnp.exp2(level * (-1.0 / STEPS)))
    return jnp.round(scaled).astype(jnp.int32).astype(jnp.int16)


def slot_sum(blocks, which, many, row, target):
    total = jnp.zeros((BS, BS), jnp.float32)
    live = many[row, 0]
    for d in range(4):
        hit = jnp.logical_and(d < live, which[row, d] == target)
        total = total + blocks[row, d].astype(jnp.float32) * jnp.where(hit, 1.0, 0.0)
    return total


def level_rows(levels):
    at = lax.broadcasted_iota(jnp.int32, (16, BS), 0)
    rows = jnp.zeros((16, BS), jnp.float32)
    for n, level in enumerate(levels):
        rows = jnp.where(at == n, level, rows)
    return rows.astype(jnp.int32).astype(jnp.int16)


def pack_b(which, many, blocks, out):
    levels = []
    for k in range(2):
        sums = [slot_sum(blocks, which, many, k, j) for j in range(2)]
        biggest = jnp.max(jnp.maximum(jnp.abs(sums[0]), jnp.abs(sums[1])), axis=1, keepdims=True)
        level = level_of(biggest)
        for j in range(2):
            out[pl.ds((2 * k + j) * BS, BS), :] = coded(sums[j], level)
        levels.append(jnp.transpose(jnp.broadcast_to(level, (BS, BS)))[0:1, :])
    out[pl.ds(VALUES, 16), :] = level_rows(levels)


def pack_a(which, many, half, blocks, own, sent):
    def one(first, out):
        levels = []
        for k in range(2):
            for i in range(2):
                total = slot_sum(blocks, which, many, first + k, i)
                level = level_of(jnp.max(jnp.abs(total), axis=0, keepdims=True))
                out[pl.ds((2 * k + i) * BS, BS), :] = coded(total, level)
                levels.append(level)
        out[pl.ds(VALUES, 16), :] = level_rows(levels)

    one(0, own)

    @pl.when(half[0] == 0)
    def _():
        sent[...] = own[...]

    @pl.when(half[0] == 1)
    def _():
        one(2, sent)


SMEM = pl.BlockSpec(memory_space=pltpu.SMEM)
VMEM = pl.BlockSpec(memory_space=pltpu.VMEM)
PIECE = jax.ShapeDtypeStruct((ROWS, BS), jnp.int16)


def packed_b(blocks, which, many):
    return pl.pallas_call(
        pack_b,
        out_shape=PIECE,
        in_specs=[SMEM, SMEM, VMEM],
        out_specs=VMEM,
        name="pack_b",
        cost_estimate=pl.CostEstimate(flops=2_000_000, bytes_accessed=400_000, transcendentals=0),
    )(which, many, blocks)


def packed_a(blocks, which, many, half):
    return pl.pallas_call(
        pack_a,
        out_shape=(PIECE, PIECE),
        in_specs=[SMEM, SMEM, SMEM, VMEM],
        out_specs=(VMEM, VMEM),
        name="pack_a",
        cost_estimate=pl.CostEstimate(flops=4_000_000, bytes_accessed=800_000, transcendentals=0),
    )(which, many, half, blocks)


def two_parts(x):
    high = x.astype(jnp.bfloat16)
    return high, (x - high.astype(jnp.float32)).astype(jnp.bfloat16)


def section(a, b):
    a_levels = a[pl.ds(VALUES, 16), :].astype(jnp.int32).astype(jnp.float32)
    b_levels = b[pl.ds(VALUES, 16), :].astype(jnp.int32).astype(jnp.float32)
    a_scales = jnp.exp2(a_levels * (1.0 / STEPS))
    b_scales = jnp.exp2(b_levels * (1.0 / STEPS))
    lefts = []
    rights = []
    for k in range(2):
        tall = []
        wide = []
        for i in range(2):
            v = a[pl.ds((2 * k + i) * BS, BS), :].astype(jnp.int32).astype(jnp.float32)
            n = 2 * k + i
            tall.append((v * (1.0 / TOP)) * a_scales[n : n + 1, :] * b_scales[k : k + 1, :])
            wide.append(b[pl.ds(n * BS, BS), :].astype(jnp.int32).astype(jnp.float32))
        lefts.append(jnp.concatenate(tall, axis=0))
        rights.append(jnp.concatenate(wide, axis=1))
    a_high, a_low = two_parts(jnp.concatenate(lefts, axis=1))
    b_high, b_low = two_parts(jnp.concatenate(rights, axis=0))
    dot = functools.partial(jnp.dot, preferred_element_type=jnp.float32)
    return dot(a_high, b_high) + (dot(a_high, b_low) + dot(a_low, b_high))


def final(keep, a0, a1, a2, a3, others, b0, b1, b2, b3, c0, c1, c2, c3, out):
    total = jnp.zeros((2 * BS, 2 * BS), jnp.float32)
    for t, (a, b, c) in enumerate(zip((a0, a1, a2, a3), (b0, b1, b2, b3), (c0, c1, c2, c3))):
        total = total + section(a, b) + section(others.at[t], c)
    total = total * (1.0 / TOP)
    for i in range(2):
        for j in range(2):
            kept = keep[i, j] == 1
            out[i, j] = jnp.where(kept, total[i * BS : (i + 1) * BS, j * BS : (j + 1) * BS], 0.0)


def finished(keep, *pieces):
    return pl.pallas_call(
        final,
        out_shape=jax.ShapeDtypeStruct((2, 2, BS, BS), jnp.float32),
        in_specs=[SMEM] + [VMEM] * 13,
        out_specs=VMEM,
        name="final",
        cost_estimate=pl.CostEstimate(flops=800_000_000, bytes_accessed=2_500_000, transcendentals=0),
        compiler_params=pltpu.CompilerParams(vmem_limit_bytes=32 << 20),
    )(keep, *pieces)


def moved(x, rows, cols, goal, takes_part=None):
    pairs = []
    for p in range(rows):
        for q in range(cols):
            if takes_part is None or takes_part(p, q):
                to_p, to_q = goal(p, q)
                pairs.append((p * cols + q, (to_p % rows) * cols + to_q % cols))
    return lax.ppermute(x, ("row", "col"), pairs)


def low_plane(p, q):
    return p % 2 == 0


def high_plane(p, q):
    return p % 2 == 1


def per_device(a_blocks, a_rows, a_count, b_blocks, b_cols, b_count, c_keep):
    rows = lax.axis_size("row")
    cols = lax.axis_size("col")
    go = functools.partial(moved, rows=rows, cols=cols)
    col_at = lax.axis_index("col")
    chip = col_at // 2
    core = col_at % 2
    in_quad = chip % 4

    b_own = packed_b(b_blocks, b_cols, b_count)
    b_next_low = go(b_own, goal=lambda p, q: (p - 1, q), takes_part=high_plane)
    half = jnp.where(chip < 4, 1, 0).astype(jnp.int32).reshape(1)
    a_own, a_sent = packed_a(a_blocks, a_rows, a_count, half)

    def swap_goal(p, q):
        return p, q ^ 8

    def quad_goal(t):
        return lambda p, q: (p, q // 8 * 8 + (q % 8 - 2 * t) % 8)

    a_far = go(a_sent, goal=swap_goal)
    b_same = [go(b_own, goal=lambda p, q, t=t: (p - 2 * t, q)) for t in (1, 2, 3)]
    a_same = []
    for t in (1, 2, 3):
        a_same.append(go(jnp.where(in_quad < t, a_far, a_own), goal=quad_goal(t)))
    b_next_high = go(b_own, goal=lambda p, q: (p - 1, q), takes_part=low_plane)
    b_next = jnp.where(lax.axis_index("row") % 2 == 0, b_next_low, b_next_high)
    b_other = [go(b_next, goal=lambda p, q, t=t: (p - 2 * t, q)) for t in (1, 2, 3)]
    mine = [a_own] + a_same
    give = jnp.where(core == 0, jnp.stack(mine[1:] + [a_far]), jnp.stack(mine))
    others = go(give, goal=lambda p, q: (p, q ^ 1))
    return finished(c_keep, *mine, others, b_own, *b_same, b_next, *b_other)


def solution(mesh):
    placed = (
        P("row", "col", None, None),
        P("row", "col"),
        P("row", "col"),
        P("row", "col", None, None),
        P("row", "col"),
        P("row", "col"),
        P("row", "col"),
    )
    return jax.shard_map(
        per_device,
        mesh=mesh,
        in_specs=placed,
        out_specs=P("row", "col", None, None),
        check_vma=False,
    )
```

time: 531 us -> 99.6 us (0.19); the launches traced: 524 us -> 98.9 us
  starting transfers between devices: 378 us -> 74.1 us
  waiting for transfers between devices: 117 us -> 14.8 us
  matrix products: 23.2 us -> 0 us
  Pallas kernels: 0 us -> 6.44 us
    ppermute x42 -> x13, starting transfers between devices: 378 us -> 74.1 us  [moved(): return lax.ppermute(x, ('row', 'col'), pairs)]
    ppermute x42 -> x13, waiting for transfers between devices: 117 us -> 14.8 us  [moved(): return lax.ppermute(x, ('row', 'col'), pairs)]
    dot_general x16 -> x0, matrix products: 23.2 us -> none  [the longest x8 18.8 us: block_products(): jnp.dot(weight, products.reshape(weight.shape[1], -1), precision=lax.Prec...]
    pallas_call x0 -> x3, Pallas kernels: none -> 6.44 us  [the longest x1 2.56 us: finished(): pl.pallas_call(final, out_shape=jax.ShapeDtypeStruct((2, 2, BS, BS), jnp....]
  transfers between devices with their start and end apart: 42 -> 13, of which waited for: 19 -> 4; matrix products, arithmetic and copies ran while one was open for 4% -> 1% of each run, Pallas kernels for 0% -> 2%
where the time goes in v1:
time: 99.6 us; the launch traced here: 98.9 us
  starting transfers between devices  74.1 us (74%)
  waiting for transfers between devices  14.8 us (15%)
  Pallas kernels  6.44 us (6%)
  local copies, waits for them, and re-layouts  2.02 us (2%)
  other arithmetic  1.21 us (1%)
    ppermute x13, starting transfers between devices, moved(): return lax.ppermute(x, ('row', 'col'), pairs)  74.1 us
    ppermute x13, waiting for transfers between devices, moved(): return lax.ppermute(x, ('row', 'col'), pairs)  14.8 us
    pallas_call x1, Pallas kernels, finished(): pl.pallas_call(final, out_shape=jax.ShapeDtypeStruct((2, 2, BS, BS), jnp....  2.56 us
    pallas_call x1, Pallas kernels, packed_a(): pl.pallas_call(pack_a, out_shape=(PIECE, PIECE), in_specs=[SMEM, SMEM, SM...  2.05 us
    unnamed x12, local copies, waits for them, and re-layouts  2.02 us
  transfers between devices with their start and end apart: 13, of which 4 were waited for; matrix products, arithmetic and copies ran while one was open for 1% of the time, Pallas kernels for 2%

profile of v1, /device:TPU:1, one launch (start us, length us, event | category | flops | bytes accessed | tf_op | source)
XLA Modules:
  0.0 98.9 jit_solution(9553750772422754585)
XLA Ops:
  0.0 0.0 copy-start.3
  0.0 0.7 copy-done.3
  0.7 0.7 copy.8.many
  1.3 2.0 %pack_a.1 = (s16[528,128]{1,0:T(8,128)(2,1)}, s16[528,128]{1,0:T(8,128)(2,1)}) custom-call(s32[4,4]{1,0:T(4,128)} %which.2, s32[4,1]{1,0:T(4,128)} %copy.8.many, s32[1]{0:T(128)} %bitcast.half, bf16[4,4,128,128]{3,2,1,0:T(8,128)(2,1)} %blocks.2), custom_call_target="tpu_custom_call" | custom-call | flops 4000000 | bytes 800000 | tf_op jit(solution)/shard_map/pack_a/pallas_call | solution.py:95
  3.4 11.3 %collective-permute-start = (s16[528,128]{1,0:T(8,128)(2,1)}, s16[528,128]{1,0:T(8,128)(2,1)S(1)}, u32[]{:S(2)}, u32[]{:S(2)}) collective-permute-start(s16[528,128]{1,0:T(8,128)(2,1)} %get-tuple-element.8), channel_id=1, source_target_pairs={{0,8},{1,9},{2,10},{3,11},{4,12},{5,13},{6,14},{7,15},{8,0},{9,1},... | collective-permute-start | bytes 405512 | tf_op jit(solution)/shard_map/ppermute | solution.py:163
  14.7 2.6 %collective-permute-done = s16[528,128]{1,0:T(8,128)(2,1)S(1)} collective-permute-done((s16[528,128]{1,0:T(8,128)(2,1)}, s16[528,128]{1,0:T(8,128)(2,1)S(1)}, u32[]{:S(2)}, u32[]{:S(2)}) %collective-permute-start) | collective-permute-done | bytes 135200 | tf_op jit(solution)/shard_map/ppermute | solution.py:163
  17.3 0.0 copy-start
  17.3 1.1 %broadcast_select_fusion.1 = (s16[528,128]{1,0:T(8,128)(2,1)S(1)}, s16[528,128]{1,0:T(8,128)(2,1)S(1)}, s16[528,128]{1,0:T(8,128)(2,1)S(1)}) fusion(s16[528,128]{1,0:T(8,128)(2,1)S(1)} %collective-permute-done, s16[528,128]{1,0:T(8,128)(2,1)} %get-tuple-element.7.a0, pred[]{:T(512)S(6)} %lt.30, pred[]{:T(512)S(6)} %lt.29, pred[]{:T(512)S(6)} %lt.28), kind=kLoop, calls=%fused_computation.2 | loop fusion | flops 202752 | bytes 675843 | tf_op jit(solution)/shard_map/jit(_where)/select_n | solution.py:198
  18.4 14.6 %collective-permute-start.1 = (s16[528,128]{1,0:T(8,128)(2,1)S(1)}, s16[528,128]{1,0:T(8,128)(2,1)S(1)}, u32[]{:S(2)}, u32[]{:S(2)}) collective-permute-start(s16[528,128]{1,0:T(8,128)(2,1)S(1)} %get-tuple-element.11), channel_id=1, source_target_pairs={{0,6},{1,7},{2,0},{3,1},{4,2},{5,3},{6,4},{7,5},{8,14},{9,15},{10,... | collective-permute-start | bytes 405512 | tf_op jit(solution)/shard_map/ppermute | solution.py:163
  32.9 1.9 %collective-permute-start.2 = (s16[528,128]{1,0:T(8,128)(2,1)S(1)}, s16[528,128]{1,0:T(8,128)(2,1)S(1)}, u32[]{:S(2)}, u32[]{:S(2)}) collective-permute-start(s16[528,128]{1,0:T(8,128)(2,1)S(1)} %get-tuple-element.10), channel_id=1, source_target_pairs={{0,4},{1,5},{2,6},{3,7},{4,0},{5,1},{6,2},{7,3},{8,12},{9,13},{10,... | collective-permute-start | bytes 405512 | tf_op jit(solution)/shard_map/ppermute | solution.py:163
  34.9 2.2 %collective-permute-start.3 = (s16[528,128]{1,0:T(8,128)(2,1)S(1)}, s16[528,128]{1,0:T(8,128)(2,1)S(1)}, u32[]{:S(2)}, u32[]{:S(2)}) collective-permute-start(s16[528,128]{1,0:T(8,128)(2,1)S(1)} %get-tuple-element.9), channel_id=1, source_target_pairs={{0,2},{1,3},{2,4},{3,5},{4,6},{5,7},{6,0},{7,1},{8,10},{9,11},{10,... | collective-permute-start | bytes 405512 | tf_op jit(solution)/shard_map/ppermute | solution.py:163
  37.1 0.0 collective-permute-done.1.a1
  37.1 8.2 %collective-permute-done.2.a2 = s16[528,128]{1,0:T(8,128)(2,1)S(1)} collective-permute-done((s16[528,128]{1,0:T(8,128)(2,1)S(1)}, s16[528,128]{1,0:T(8,128)(2,1)S(1)}, u32[]{:S(2)}, u32[]{:S(2)}) %collective-permute-start.2) | collective-permute-done | bytes 135200 | tf_op jit(solution)/shard_map/ppermute | solution.py:163
  45.3 0.0 collective-permute-done.3.a3
  45.3 0.0 copy-done
  45.3 0.0 copy-start.4
  45.3 0.1 add_select_fusion
  45.4 2.8 %collective-permute-start.4 = (s16[4,528,128]{2,1,0:T(8,128)(2,1)S(1)}, s16[4,528,128]{2,1,0:T(8,128)(2,1)S(1)}, u32[]{:S(2)}, u32[]{:S(2)}) collective-permute-start(s16[4,528,128]{2,1,0:T(8,128)(2,1)S(1)} %add_select_fusion), channel_id=1, source_target_pairs={{0,1},{1,0},{2,3},{3,2},{4,5},{5,4},{6,7},{7,6},{8,9},{9,8},{10,11... | collective-permute-start | bytes 1622024 | tf_op jit(solution)/shard_map/ppermute | solution.py:163
  48.2 0.0 copy-done.4
  48.2 0.7 copy.9.many
  48.9 1.8 %pack_b.1.b0 = s16[528,128]{1,0:T(8,128)(2,1)} custom-call(s32[2,4]{1,0:T(2,128)} %which.3, s32[2,1]{1,0:T(2,128)} %copy.9.many, bf16[2,4,128,128]{3,2,1,0:T(8,128)(2,1)} %blocks.3), custom_call_target="tpu_custom_call" | custom-call | flops 2000000 | bytes 400000 | tf_op jit(solution)/shard_map/pack_b/pallas_call | solution.py:84
  50.7 1.3 %collective-permute-start.8 = (s16[528,128]{1,0:T(8,128)(2,1)}, s16[528,128]{1,0:T(8,128)(2,1)S(1)}, u32[]{:S(2)}, u32[]{:S(2)}) collective-permute-start(s16[528,128]{1,0:T(8,128)(2,1)} %pack_b.1.b0), channel_id=1, source_target_pairs={{16,0},{17,1},{18,2},{19,3},{20,4},{21,5},{22,6},{23,7},{24,8},{25... | collective-permute-start | bytes 405512 | tf_op jit(solution)/shard_map/ppermute | solution.py:163
  52.0 20.3 %collective-permute-start.9 = (s16[528,128]{1,0:T(8,128)(2,1)}, s16[528,128]{1,0:T(8,128)(2,1)S(1)}, u32[]{:S(2)}, u32[]{:S(2)}) collective-permute-start(s16[528,128]{1,0:T(8,128)(2,1)} %pack_b.1.b0), channel_id=1, source_target_pairs={{0,1008},{1,1009},{2,1010},{3,1011},{4,1012},{5,1013},{6,1014},{7,... | collective-permute-start | bytes 405512 | tf_op jit(solution)/shard_map/ppermute | solution.py:163
  72.3 2.5 %collective-permute-start.5 = (s16[528,128]{1,0:T(8,128)(2,1)}, s16[528,128]{1,0:T(8,128)(2,1)S(1)}, u32[]{:S(2)}, u32[]{:S(2)}) collective-permute-start(s16[528,128]{1,0:T(8,128)(2,1)} %pack_b.1.b0), channel_id=1, source_target_pairs={{0,992},{1,993},{2,994},{3,995},{4,996},{5,997},{6,998},{7,999},{8... | collective-permute-start | bytes 405512 | tf_op jit(solution)/shard_map/ppermute | solution.py:163
  74.7 2.1 %collective-permute-start.6 = (s16[528,128]{1,0:T(8,128)(2,1)}, s16[528,128]{1,0:T(8,128)(2,1)S(1)}, u32[]{:S(2)}, u32[]{:S(2)}) collective-permute-start(s16[528,128]{1,0:T(8,128)(2,1)} %pack_b.1.b0), channel_id=1, source_target_pairs={{0,960},{1,961},{2,962},{3,963},{4,964},{5,965},{6,966},{7,967},{8... | collective-permute-start | bytes 405512 | tf_op jit(solution)/shard_map/ppermute | solution.py:163
  76.9 0.0 copy-start.1
  76.9 0.0 copy-start.2
  76.9 0.0 collective-permute-done.8
  76.9 3.5 %collective-permute-start.7 = (s16[528,128]{1,0:T(8,128)(2,1)}, s16[528,128]{1,0:T(8,128)(2,1)S(1)}, u32[]{:S(2)}, u32[]{:S(2)}) collective-permute-start(s16[528,128]{1,0:T(8,128)(2,1)} %pack_b.1.b0), channel_id=1, source_target_pairs={{0,928},{1,929},{2,930},{3,931},{4,932},{5,933},{6,934},{7,935},{8... | collective-permute-start | bytes 405512 | tf_op jit(solution)/shard_map/ppermute | solution.py:163
  80.5 0.0 collective-permute-done.9
  80.5 5.4 %collective-permute-start.10 = (s16[528,128]{1,0:T(8,128)(2,1)S(1)}, s16[528,128]{1,0:T(8,128)(2,1)S(1)}, u32[]{:S(2)}, u32[]{:S(2)}) collective-permute-start(s16[528,128]{1,0:T(8,128)(2,1)S(1)} %broadcast_select_fusion.c0), channel_id=1, source_target_pairs={{0,992},{1,993},{2,994},{3,995},{4,996},{5,997},{6,998},{7,999},{8... | collective-permute-start | bytes 405512 | tf_op jit(solution)/shard_map/ppermute | solution.py:163
  85.9 0.0 collective-permute-done.5.b1
  85.9 2.8 %collective-permute-start.11 = (s16[528,128]{1,0:T(8,128)(2,1)S(1)}, s16[528,128]{1,0:T(8,128)(2,1)S(1)}, u32[]{:S(2)}, u32[]{:S(2)}) collective-permute-start(s16[528,128]{1,0:T(8,128)(2,1)S(1)} %broadcast_select_fusion.c0), channel_id=1, source_target_pairs={{0,960},{1,961},{2,962},{3,963},{4,964},{5,965},{6,966},{7,967},{8... | collective-permute-start | bytes 405512 | tf_op jit(solution)/shard_map/ppermute | solution.py:163
  88.7 0.0 collective-permute-done.6.b2
  88.7 3.5 %collective-permute-start.12 = (s16[528,128]{1,0:T(8,128)(2,1)S(1)}, s16[528,128]{1,0:T(8,128)(2,1)S(1)}, u32[]{:S(2)}, u32[]{:S(2)}) collective-permute-start(s16[528,128]{1,0:T(8,128)(2,1)S(1)} %broadcast_select_fusion.c0), channel_id=1, source_target_pairs={{0,928},{1,929},{2,930},{3,931},{4,932},{5,933},{6,934},{7,935},{8... | collective-permute-start | bytes 405512 | tf_op jit(solution)/shard_map/ppermute | solution.py:163
  92.3 0.0 collective-permute-done.7.b3
  92.3 0.0 collective-permute-done.10.c1
  92.3 0.9 collective-permute-done.11.c2
  93.2 3.1 %collective-permute-done.12.c3 = s16[528,128]{1,0:T(8,128)(2,1)S(1)} collective-permute-done((s16[528,128]{1,0:T(8,128)(2,1)S(1)}, s16[528,128]{1,0:T(8,128)(2,1)S(1)}, u32[]{:S(2)}, u32[]{:S(2)}) %collective-permute-start.12) | collective-permute-done | bytes 135200 | tf_op jit(solution)/shard_map/ppermute | solution.py:163
  96.3 0.0 collective-permute-done.4.others
  96.3 0.0 copy-done.1
  96.3 0.0 copy-done.2
  96.3 2.6 %final.1 = f32[2,2,128,128]{3,2,1,0:T(8,128)} custom-call(s32[2,2]{1,0:T(2,128)S(1)} %copy-done.2, s16[528,128]{1,0:T(8,128)(2,1)S(1)} %copy-done, s16[528,128]{1,0:T(8,128)(2,1)S(1)} %collective-permute-done.1.a1, s16[528,128]{1,0:T(8,128)(2,1)S(1)} %collective-permute-done.2.a2, s16[528,128]{1,0:T(8,128)(2,1)S(1)} %collective-permute-done.3.a3, ...), custom_call_target="tpu_custom_call" | custom-call | flops 800000000 | bytes 2500000 | tf_op jit(solution)/shard_map/final/pallas_call | solution.py:145
  (1 shorter events, 0.0 us)
Async XLA Ops:
  0.0 0.7 copy-start.3
  3.4 13.9 %collective-permute-start = (s16[528,128]{1,0:T(8,128)(2,1)}, s16[528,128]{1,0:T(8,128)(2,1)S(1)}, u32[]{:S(2)}, u32[]{:S(2)}) collective-permute-start(s16[528,128]{1,0:T(8,128)(2,1)} %get-tuple-element.8), channel_id=1, source_target_pairs={{0,8},{1,9},{2,10},{3,11},{4,12},{5,13},{6,14},{7,15},{8,0},{9,1},... | collective-permute-start | bytes 405512 | tf_op jit(solution)/shard_map/ppermute | solution.py:163
  17.3 28.0 %copy-start = (s16[528,128]{1,0:T(8,128)(2,1)S(1)}, s16[528,128]{1,0:T(8,128)(2,1)}, u32[]{:S(2)}) copy-start(s16[528,128]{1,0:T(8,128)(2,1)} %get-tuple-element.7.a0) | copy-start | bytes 405508
  18.4 18.7 %collective-permute-start.1 = (s16[528,128]{1,0:T(8,128)(2,1)S(1)}, s16[528,128]{1,0:T(8,128)(2,1)S(1)}, u32[]{:S(2)}, u32[]{:S(2)}) collective-permute-start(s16[528,128]{1,0:T(8,128)(2,1)S(1)} %get-tuple-element.11), channel_id=1, source_target_pairs={{0,6},{1,7},{2,0},{3,1},{4,2},{5,3},{6,4},{7,5},{8,14},{9,15},{10,... | collective-permute-start | bytes 405512 | tf_op jit(solution)/shard_map/ppermute | solution.py:163
  32.9 12.4 %collective-permute-start.2 = (s16[528,128]{1,0:T(8,128)(2,1)S(1)}, s16[528,128]{1,0:T(8,128)(2,1)S(1)}, u32[]{:S(2)}, u32[]{:S(2)}) collective-permute-start(s16[528,128]{1,0:T(8,128)(2,1)S(1)} %get-tuple-element.10), channel_id=1, source_target_pairs={{0,4},{1,5},{2,6},{3,7},{4,0},{5,1},{6,2},{7,3},{8,12},{9,13},{10,... | collective-permute-start | bytes 405512 | tf_op jit(solution)/shard_map/ppermute | solution.py:163
  34.9 10.4 %collective-permute-start.3 = (s16[528,128]{1,0:T(8,128)(2,1)S(1)}, s16[528,128]{1,0:T(8,128)(2,1)S(1)}, u32[]{:S(2)}, u32[]{:S(2)}) collective-permute-start(s16[528,128]{1,0:T(8,128)(2,1)S(1)} %get-tuple-element.9), channel_id=1, source_target_pairs={{0,2},{1,3},{2,4},{3,5},{4,6},{5,7},{6,0},{7,1},{8,10},{9,11},{10,... | collective-permute-start | bytes 405512 | tf_op jit(solution)/shard_map/ppermute | solution.py:163
  45.3 2.9 %copy-start.4 = (s32[2,1]{0,1:T(1,128)S(1)}, s32[2,1]{0,1:T(1,128)}, u32[]{:S(2)}) copy-start(s32[2,1]{0,1:T(1,128)} %param.12) | copy-start | bytes 28
  45.4 50.9 %collective-permute-start.4 = (s16[4,528,128]{2,1,0:T(8,128)(2,1)S(1)}, s16[4,528,128]{2,1,0:T(8,128)(2,1)S(1)}, u32[]{:S(2)}, u32[]{:S(2)}) collective-permute-start(s16[4,528,128]{2,1,0:T(8,128)(2,1)S(1)} %add_select_fusion), channel_id=1, source_target_pairs={{0,1},{1,0},{2,3},{3,2},{4,5},{5,4},{6,7},{7,6},{8,9},{9,8},{10,11... | collective-permute-start | bytes 1622024 | tf_op jit(solution)/shard_map/ppermute | solution.py:163
  50.7 26.2 %collective-permute-start.8 = (s16[528,128]{1,0:T(8,128)(2,1)}, s16[528,128]{1,0:T(8,128)(2,1)S(1)}, u32[]{:S(2)}, u32[]{:S(2)}) collective-permute-start(s16[528,128]{1,0:T(8,128)(2,1)} %pack_b.1.b0), channel_id=1, source_target_pairs={{16,0},{17,1},{18,2},{19,3},{20,4},{21,5},{22,6},{23,7},{24,8},{25... | collective-permute-start | bytes 405512 | tf_op jit(solution)/shard_map/ppermute | solution.py:163
  52.0 28.4 %collective-permute-start.9 = (s16[528,128]{1,0:T(8,128)(2,1)}, s16[528,128]{1,0:T(8,128)(2,1)S(1)}, u32[]{:S(2)}, u32[]{:S(2)}) collective-permute-start(s16[528,128]{1,0:T(8,128)(2,1)} %pack_b.1.b0), channel_id=1, source_target_pairs={{0,1008},{1,1009},{2,1010},{3,1011},{4,1012},{5,1013},{6,1014},{7,... | collective-permute-start | bytes 405512 | tf_op jit(solution)/shard_map/ppermute | solution.py:163
  72.3 13.6 %collective-permute-start.5 = (s16[528,128]{1,0:T(8,128)(2,1)}, s16[528,128]{1,0:T(8,128)(2,1)S(1)}, u32[]{:S(2)}, u32[]{:S(2)}) collective-permute-start(s16[528,128]{1,0:T(8,128)(2,1)} %pack_b.1.b0), channel_id=1, source_target_pairs={{0,992},{1,993},{2,994},{3,995},{4,996},{5,997},{6,998},{7,999},{8... | collective-permute-start | bytes 405512 | tf_op jit(solution)/shard_map/ppermute | solution.py:163
  74.7 14.0 %collective-permute-start.6 = (s16[528,128]{1,0:T(8,128)(2,1)}, s16[528,128]{1,0:T(8,128)(2,1)S(1)}, u32[]{:S(2)}, u32[]{:S(2)}) collective-permute-start(s16[528,128]{1,0:T(8,128)(2,1)} %pack_b.1.b0), channel_id=1, source_target_pairs={{0,960},{1,961},{2,962},{3,963},{4,964},{5,965},{6,966},{7,967},{8... | collective-permute-start | bytes 405512 | tf_op jit(solution)/shard_map/ppermute | solution.py:163
  76.9 19.4 %copy-start.1 = (s16[528,128]{1,0:T(8,128)(2,1)S(1)}, s16[528,128]{1,0:T(8,128)(2,1)}, u32[]{:S(2)}) copy-start(s16[528,128]{1,0:T(8,128)(2,1)} %pack_b.1.b0) | copy-start | bytes 405508
  76.9 19.4 %copy-start.2 = (s32[2,2]{1,0:T(2,128)S(1)}, s32[2,2]{1,0:T(2,128)}, u32[]{:S(2)}) copy-start(s32[2,2]{1,0:T(2,128)} %keep.1) | copy-start | bytes 52
  76.9 15.4 %collective-permute-start.7 = (s16[528,128]{1,0:T(8,128)(2,1)}, s16[528,128]{1,0:T(8,128)(2,1)S(1)}, u32[]{:S(2)}, u32[]{:S(2)}) collective-permute-start(s16[528,128]{1,0:T(8,128)(2,1)} %pack_b.1.b0), channel_id=1, source_target_pairs={{0,928},{1,929},{2,930},{3,931},{4,932},{5,933},{6,934},{7,935},{8... | collective-permute-start | bytes 405512 | tf_op jit(solution)/shard_map/ppermute | solution.py:163
  80.5 11.8 %collective-permute-start.10 = (s16[528,128]{1,0:T(8,128)(2,1)S(1)}, s16[528,128]{1,0:T(8,128)(2,1)S(1)}, u32[]{:S(2)}, u32[]{:S(2)}) collective-permute-start(s16[528,128]{1,0:T(8,128)(2,1)S(1)} %broadcast_select_fusion.c0), channel_id=1, source_target_pairs={{0,992},{1,993},{2,994},{3,995},{4,996},{5,997},{6,998},{7,999},{8... | collective-permute-start | bytes 405512 | tf_op jit(solution)/shard_map/ppermute | solution.py:163
  85.9 7.3 %collective-permute-start.11 = (s16[528,128]{1,0:T(8,128)(2,1)S(1)}, s16[528,128]{1,0:T(8,128)(2,1)S(1)}, u32[]{:S(2)}, u32[]{:S(2)}) collective-permute-start(s16[528,128]{1,0:T(8,128)(2,1)S(1)} %broadcast_select_fusion.c0), channel_id=1, source_target_pairs={{0,960},{1,961},{2,962},{3,963},{4,964},{5,965},{6,966},{7,967},{8... | collective-permute-start | bytes 405512 | tf_op jit(solution)/shard_map/ppermute | solution.py:163
  88.7 7.6 %collective-permute-start.12 = (s16[528,128]{1,0:T(8,128)(2,1)S(1)}, s16[528,128]{1,0:T(8,128)(2,1)S(1)}, u32[]{:S(2)}, u32[]{:S(2)}) collective-permute-start(s16[528,128]{1,0:T(8,128)(2,1)S(1)} %broadcast_select_fusion.c0), channel_id=1, source_target_pairs={{0,928},{1,929},{2,930},{3,931},{4,932},{5,933},{6,934},{7,935},{8... | collective-permute-start | bytes 405512 | tf_op jit(solution)/shard_map/ppermute | solution.py:163

commit v2 on v1

--- a/solution.py
+++ b/solution.py
@@ -26,7 +26,7 @@
 
 def slot_sum(blocks, which, many, row, target):
     total = jnp.zeros((BS, BS), jnp.float32)
-    live = many[row, 0]
+    live = many[0, row]
     for d in range(4):
         hit = jnp.logical_and(d < live, which[row, d] == target)
         total = total + blocks[row, d].astype(jnp.float32) * jnp.where(hit, 1.0, 0.0)
@@ -53,7 +53,7 @@
     out[pl.ds(VALUES, 16), :] = level_rows(levels)
 
 
-def pack_a(which, many, half, blocks, own, sent):
+def pack_a(which, many, chip, blocks, own, sent):
     def one(first, out):
         levels = []
         for k in range(2):
@@ -66,13 +66,13 @@
 
     one(0, own)
 
-    @pl.when(half[0] == 0)
+    @pl.when(chip[0] < 4)
+    def _():
+        one(2, sent)
+
+    @pl.when(chip[0] >= 4)
     def _():
         sent[...] = own[...]
-
-    @pl.when(half[0] == 1)
-    def _():
-        one(2, sent)
 
 
 SMEM = pl.BlockSpec(memory_space=pltpu.SMEM)
@@ -91,15 +91,15 @@
     )(which, many, blocks)
 
 
-def packed_a(blocks, which, many, half):
+def packed_a(blocks, which, many, chip):
     return pl.pallas_call(
         pack_a,
-        out_shape=(PIECE, PIECE),
+        out_shape=(PIECE,) * 2,
         in_specs=[SMEM, SMEM, SMEM, VMEM],
-        out_specs=(VMEM, VMEM),
+        out_specs=(VMEM,) * 2,
         name="pack_a",
         cost_estimate=pl.CostEstimate(flops=4_000_000, bytes_accessed=800_000, transcendentals=0),
-    )(which, many, half, blocks)
+    )(which, many, chip, blocks)
 
 
 def two_parts(x):
@@ -130,27 +130,42 @@
     return dot(a_high, b_high) + (dot(a_high, b_low) + dot(a_low, b_high))
 
 
-def final(keep, a0, a1, a2, a3, others, b0, b1, b2, b3, c0, c1, c2, c3, out):
-    total = jnp.zeros((2 * BS, 2 * BS), jnp.float32)
-    for t, (a, b, c) in enumerate(zip((a0, a1, a2, a3), (b0, b1, b2, b3), (c0, c1, c2, c3))):
-        total = total + section(a, b) + section(others.at[t], c)
-    total = total * (1.0 / TOP)
+def kept(keep, total, out):
     for i in range(2):
         for j in range(2):
-            kept = keep[i, j] == 1
-            out[i, j] = jnp.where(kept, total[i * BS : (i + 1) * BS, j * BS : (j + 1) * BS], 0.0)
-
-
-def finished(keep, *pieces):
+            block = total[i * BS : (i + 1) * BS, j * BS : (j + 1) * BS] * (1.0 / TOP)
+            out[i, j] = jnp.where(keep[i, j] == 1, block, 0.0)
+
+
+def slots_of(spot):
+    chip, core = spot[0], spot[1]
+    return [lax.rem(chip + t, 4) for t in range(4)], [lax.rem(chip + core + t, 4) for t in range(4)]
+
+
+def kept(keep, total, out):
+    for i in range(2):
+        for j in range(2):
+            block = total[i * BS : (i + 1) * BS, j * BS : (j + 1) * BS] * (1.0 / TOP)
+            out[i, j] = jnp.where(keep[i, j] == 1, block, 0.0)
+
+
+def final(spot, keep, mine, others, z0, z1, z2, z3, out):
+    total = jnp.zeros((2 * BS, 2 * BS), jnp.float32)
+    for s, t, z in zip(*slots_of(spot), (z0, z1, z2, z3)):
+        total = total + section(mine.at[s], z.at[0]) + section(others.at[t], z.at[1])
+    kept(keep, total, out)
+
+
+def summed(body, keep, *pieces):
     return pl.pallas_call(
-        final,
+        body,
         out_shape=jax.ShapeDtypeStruct((2, 2, BS, BS), jnp.float32),
-        in_specs=[SMEM] + [VMEM] * 13,
+        in_specs=[SMEM] * len(keep) + [VMEM] * len(pieces),
         out_specs=VMEM,
-        name="final",
+        name=body.__name__,
         cost_estimate=pl.CostEstimate(flops=800_000_000, bytes_accessed=2_500_000, transcendentals=0),
         compiler_params=pltpu.CompilerParams(vmem_limit_bytes=32 << 20),
-    )(keep, *pieces)
+    )(*keep, *pieces)
 
 
 def moved(x, rows, cols, goal, takes_part=None):
@@ -178,31 +193,56 @@
     col_at = lax.axis_index("col")
     chip = col_at // 2
     core = col_at % 2
+
+    on_low = lax.axis_index("row") % 2 == 0
+    chip_at = chip.astype(jnp.int32).reshape(1)
     in_quad = chip % 4
-
-    b_own = packed_b(b_blocks, b_cols, b_count)
-    b_next_low = go(b_own, goal=lambda p, q: (p - 1, q), takes_part=high_plane)
-    half = jnp.where(chip < 4, 1, 0).astype(jnp.int32).reshape(1)
-    a_own, a_sent = packed_a(a_blocks, a_rows, a_count, half)
-
-    def swap_goal(p, q):
-        return p, q ^ 8
-
-    def quad_goal(t):
-        return lambda p, q: (p, q // 8 * 8 + (q % 8 - 2 * t) % 8)
-
-    a_far = go(a_sent, goal=swap_goal)
-    b_same = [go(b_own, goal=lambda p, q, t=t: (p - 2 * t, q)) for t in (1, 2, 3)]
-    a_same = []
-    for t in (1, 2, 3):
-        a_same.append(go(jnp.where(in_quad < t, a_far, a_own), goal=quad_goal(t)))
-    b_next_high = go(b_own, goal=lambda p, q: (p - 1, q), takes_part=low_plane)
-    b_next = jnp.where(lax.axis_index("row") % 2 == 0, b_next_low, b_next_high)
-    b_other = [go(b_next, goal=lambda p, q, t=t: (p - 2 * t, q)) for t in (1, 2, 3)]
-    mine = [a_own] + a_same
-    give = jnp.where(core == 0, jnp.stack(mine[1:] + [a_far]), jnp.stack(mine))
-    others = go(give, goal=lambda p, q: (p, q ^ 1))
-    return finished(c_keep, *mine, others, b_own, *b_same, b_next, *b_other)
+    spot = jnp.stack([in_quad, core]).astype(jnp.int32)
+    back = lambda p, q: (p - 1, q)
+
+    def spread(x, t, plane):
+        return go(x, goal=lambda p, q: (p - 2 * t, q), takes_part=plane)
+
+    def after(x, done):
+        return lax.optimization_barrier((x, done))[0]
+
+    slot = lax.broadcasted_iota(jnp.int32, (4, 1, 1), 0)
+    quads = [[8 * h + 2 * j + c for j in range(4)] for h in range(cols // 8) for c in range(2)]
+
+    def far_half(plane, blocks):
+        a_own, a_sent = packed_a(blocks, a_rows, a_count.T, chip_at)
+        a_far = go(a_sent, goal=lambda p, q: (p, q ^ 8), takes_part=plane)
+        return jnp.where(slot <= in_quad, a_own[None], a_far[None]), a_far
+
+    def nothing():
+        return jnp.zeros((4, *PIECE.shape), PIECE.dtype), jnp.zeros(PIECE.shape, PIECE.dtype)
+
+    def shared(plane, b_own, b_next, give, a_far):
+        mine = lax.all_to_all(give, "col", 0, 0, axis_index_groups=quads)
+        pair = jnp.stack([b_own, b_next])
+        pairs = [pair] + [spread(pair, t, plane) for t in (1, 2, 3)]
+        own_slot = jnp.logical_and(slot == in_quad, core == 0)
+        given = jnp.where(own_slot, a_far[None], after(mine, pairs))
+        others = go(given, goal=lambda p, q: (p, q ^ 1), takes_part=plane)
+        return summed(final, [spot, c_keep], mine, others, *pairs)
+
+    b_own = packed_b(b_blocks, b_cols, b_count.T)
+    b_next_low = go(b_own, goal=back, takes_part=high_plane)
+    blocks = after(a_blocks, b_own)
+    low_a = lax.cond(on_low, lambda x: far_half(low_plane, x), lambda x: nothing(), blocks)
+    b_next_high = go(after(b_own, low_a[0]), goal=back, takes_part=low_plane)
+    out, high_a = lax.cond(
+        on_low,
+        lambda x, b, n, a: (shared(low_plane, b, n, *a), nothing()),
+        lambda x, b, n, a: (jnp.zeros((2, 2, BS, BS), jnp.float32), far_half(high_plane, x)),
+        blocks, b_own, b_next_low, low_a,
+    )
+    return lax.cond(
+        on_low,
+        lambda o, b, n, a: o,
+        lambda o, b, n, a: shared(high_plane, b, n, *a),
+        out, b_own, b_next_high, high_a,
+    )
 
 
 def solution(mesh):

time: 99.6 us -> 82.7 us (0.83)
  starting transfers between devices: 74.1 us -> 54.4 us
  other arithmetic: 1.21 us -> 3.15 us
  waiting for transfers between devices: 14.8 us -> 16.4 us
  Pallas kernels: 6.44 us -> 5.12 us
    ppermute x13 -> x7, starting transfers between devices: 74.1 us -> 40.5 us  [moved(): return lax.ppermute(x, ('row', 'col'), pairs)]
    all_to_all x0 -> x1, starting transfers between devices: none -> 13.9 us  [shared(): mine = lax.all_to_all(give, 'col', 0, 0, axis_index_groups=quads)]
    select_n x3 -> x2, other arithmetic: 1.21 us -> 3.04 us  [the longest x1 1.96 us: far_half(): return (jnp.where(slot <= in_quad, a_own[None], a_far[None]), a_far)]
    ppermute x13 -> x7, waiting for transfers between devices: 14.8 us -> 16.4 us  [moved(): return lax.ppermute(x, ('row', 'col'), pairs)]
    unnamed x12 -> x8, local copies, waits for them, and re-layouts: 2.02 us -> 2.03 us
  transfers between devices with their start and end apart: 13 -> 8, of which waited for: 4 -> 4; matrix products, arithmetic and copies ran while one was open for 1% -> 5% of each run, Pallas kernels for 2% -> 5%
where the time goes in v2:
time: 82.7 us; the launch traced here: 82.2 us
  starting transfers between devices  54.4 us (66%)
  waiting for transfers between devices  16.4 us (20%)
  Pallas kernels  5.12 us (6%)
  other arithmetic  3.15 us (4%)
  local copies, waits for them, and re-layouts  2.95 us (4%)
    ppermute x7, starting transfers between devices, moved(): return lax.ppermute(x, ('row', 'col'), pairs)  40.5 us
    ppermute x7, waiting for transfers between devices, moved(): return lax.ppermute(x, ('row', 'col'), pairs)  16.4 us
    all_to_all x1, starting transfers between devices, shared(): mine = lax.all_to_all(give, 'col', 0, 0, axis_index_groups=quads)  13.9 us
    pallas_call x1, Pallas kernels, packed_a(): pl.pallas_call(pack_a, out_shape=(PIECE,) * 2, in_specs=[SMEM, SMEM, SMEM...  2.06 us
    unnamed x8, local copies, waits for them, and re-layouts  2.03 us
    select_n x1, other arithmetic, far_half(): return (jnp.where(slot <= in_quad, a_own[None], a_far[None]), a_far)  1.96 us
    pallas_call x1, Pallas kernels, summed(): pl.pallas_call(body, out_shape=jax.ShapeDtypeStruct((2, 2, BS, BS), jnp.f...  1.87 us
  transfers between devices with their start and end apart: 8, of which 4 were waited for; matrix products, arithmetic and copies ran while one was open for 5% of the time, Pallas kernels for 5%

profile of v2, /device:TPU:1, one launch (start us, length us, event | category | flops | bytes accessed | tf_op | source)
XLA Modules:
  0.0 82.2 jit_solution(9713652599356269463)
XLA Ops:
  0.0 1.2 %pack_b.1 = s16[528,128]{1,0:T(8,128)(2,1)S(1)} custom-call(s32[2,4]{1,0:T(2,128)} %which.1, s32[1,2]{1,0:T(1,128)} %bitcast.24, bf16[2,4,128,128]{3,2,1,0:T(8,128)(2,1)} %blocks.1), custom_call_target="tpu_custom_call" | custom-call | flops 2000000 | bytes 400000 | tf_op jit(solution)/shard_map/pack_b/pallas_call | solution.py:84
  1.2 1.3 %collective-permute-start.10 = (s16[528,128]{1,0:T(8,128)(2,1)S(1)}, s16[528,128]{1,0:T(8,128)(2,1)S(1)}, u32[]{:S(2)}, u32[]{:S(2)}) collective-permute-start(s16[528,128]{1,0:T(8,128)(2,1)S(1)} %pack_b.1), channel_id=1, source_target_pairs={{16,0},{17,1},{18,2},{19,3},{20,4},{21,5},{22,6},{23,7},{24,8},{25... | collective-permute-start | bytes 405512 | tf_op jit(solution)/shard_map/ppermute | solution.py:178
  2.5 0.0 copy-start.1
  2.5 0.0 copy-start.2
  2.5 0.7 copy-done.1
  3.2 0.0 copy-done.2
  3.2 18.0 %conditional.3 = (s16[4,528,128]{2,1,0:T(8,128)(2,1)}, s16[528,128]{1,0:T(8,128)(2,1)}) conditional(s32[]{:T(128)} %convert_element_type.2, () %tuple.37, (s32[]{:T(128)}, s32[4,1,1]{0,2,1:T(1,128)S(1)}, s32[4,1]{0,1:T(1,128)S(1)}, s32[4,4]{1,0:T(4,128)S(1)}, s32[1]{0:T(128)}, /*index=5*/bf16[4,4,128,128]{3,2,1,0:T(8,128)(2,1)}) %tuple.53), branch_computations={%region_0.1_spmd, %region_1.2_spmd} | conditional | flops 4270340 | bytes 2151764 | solution.py:232
  3.2 2.1 %pack_a.2 = (s16[528,128]{1,0:T(8,128)(2,1)}, s16[528,128]{1,0:T(8,128)(2,1)}) custom-call(s32[4,4]{1,0:T(4,128)S(1)} %get-tuple-element.72.which, s32[1,4]{1,0:T(1,128)S(1)} %bitcast.22, s32[1]{0:T(128)} %get-tuple-element.74.chip, bf16[4,4,128,128]{3,2,1,0:T(8,128)(2,1)} %get-tuple-element.75.blocks), custom_call_target="tpu_custom_call" | custom-call | flops 4000000 | bytes 800000 | tf_op jit(solution)/shard_map/cond/branch_1_fun/pack_a/pallas_call | solution.py:95
  5.3 11.3 %collective-permute-start = (s16[528,128]{1,0:T(8,128)(2,1)}, s16[528,128]{1,0:T(8,128)(2,1)}, u32[]{:S(2)}, u32[]{:S(2)}) collective-permute-start(s16[528,128]{1,0:T(8,128)(2,1)} %get-tuple-element.77), channel_id=1, source_target_pairs={{0,8},{1,9},{2,10},{3,11},{4,12},{5,13},{6,14},{7,15},{8,0},{9,1},... | collective-permute-start | bytes 405512 | tf_op jit(solution)/shard_map/cond/branch_1_fun/ppermute | solution.py:178
  16.6 2.7 %collective-permute-done = s16[528,128]{1,0:T(8,128)(2,1)} collective-permute-done((s16[528,128]{1,0:T(8,128)(2,1)}, s16[528,128]{1,0:T(8,128)(2,1)}, u32[]{:S(2)}, u32[]{:S(2)}) %collective-permute-start) | collective-permute-done | bytes 135200 | tf_op jit(solution)/shard_map/cond/branch_1_fun/ppermute | solution.py:178
  19.3 2.0 %broadcast_select_fusion = s16[4,528,128]{2,1,0:T(8,128)(2,1)} fusion(pred[4]{0:T(512)(128)(4,1)S(1)} %compare_bitcast_fusion, s16[528,128]{1,0:T(8,128)(2,1)} %collective-permute-done, s16[528,128]{1,0:T(8,128)(2,1)} %get-tuple-element.76), kind=kLoop, calls=%fused_computation | loop fusion | flops 270336 | bytes 811012 | tf_op jit(solution)/shard_map/cond/branch_1_fun/jit(_where)/select_n | solution.py:215
  21.2 8.5 %collective-permute-start.11 = (s16[528,128]{1,0:T(8,128)(2,1)S(1)}, s16[528,128]{1,0:T(8,128)(2,1)S(1)}, u32[]{:S(2)}, u32[]{:S(2)}) collective-permute-start(s16[528,128]{1,0:T(8,128)(2,1)S(1)} %pack_b.1), channel_id=1, source_target_pairs={{0,1008},{1,1009},{2,1010},{3,1011},{4,1012},{5,1013},{6,1014},{7,... | collective-permute-start | bytes 405512 | tf_op jit(solution)/shard_map/ppermute | solution.py:178
  29.8 0.1 pad_add_fusion.2
  29.9 0.0 collective-permute-done.10
  29.9 0.0 copy-start.3
  29.9 0.7 copy-done.3
  30.6 50.9 %conditional.4 = (s16[4,528,128]{2,1,0:T(8,128)(2,1)}, s16[528,128]{1,0:T(8,128)(2,1)S(1)}, f32[2,2,128,128]{3,2,1,0:T(8,128)S(1)}) conditional(s32[]{:T(128)} %convert_element_type.2, (s32[]{:T(128)}, s32[4,1,1]{0,2,1:T(1,128)S(1)}, s32[4,1]{0,1:T(1,128)S(1)}, s32[4,4]{1,0:T(4,128)S(1)}, s32[1]{0:T(128)}, ...), branch_computations={%region_2.3_spmd, %region_3.4_spmd} | conditional | flops 800405504 | bytes 11962018 | solution.py:234
  30.6 13.9 %all-to-all-start = ((s16[4,528,128]{2,1,0:T(8,128)(2,1)}), s16[4,528,128]{2,1,0:T(8,128)(2,1)S(1)}, u32[]{:S(2)}, u32[]{:S(2)}) async-start(s16[4,528,128]{2,1,0:T(8,128)(2,1)} %get-tuple-element.88), calls=%async_computation | async-start | bytes 1081344 | tf_op jit(solution)/shard_map/cond/branch_1_fun/all_to_all | solution.py:221
  44.5 8.8 %collective-permute-start.2 = (s16[2,528,128]{2,1,0:T(8,128)(2,1)S(1)}, s16[2,528,128]{2,1,0:T(8,128)(2,1)S(1)}, u32[]{:S(2)}, u32[]{:S(2)}) collective-permute-start(s16[2,528,128]{2,1,0:T(8,128)(2,1)S(1)} %pad_add_fusion.z0), channel_id=1, source_target_pairs={{0,992},{1,993},{2,994},{3,995},{4,996},{5,997},{6,998},{7,999},{8... | collective-permute-start | bytes 811016 | tf_op jit(solution)/shard_map/cond/branch_1_fun/ppermute | solution.py:178
  53.2 2.4 %collective-permute-start.3 = (s16[2,528,128]{2,1,0:T(8,128)(2,1)S(1)}, s16[2,528,128]{2,1,0:T(8,128)(2,1)S(1)}, u32[]{:S(2)}, u32[]{:S(2)}) collective-permute-start(s16[2,528,128]{2,1,0:T(8,128)(2,1)S(1)} %pad_add_fusion.z0), channel_id=1, source_target_pairs={{0,960},{1,961},{2,962},{3,963},{4,964},{5,965},{6,966},{7,967},{8... | collective-permute-start | bytes 811016 | tf_op jit(solution)/shard_map/cond/branch_1_fun/ppermute | solution.py:178
  55.7 3.3 %collective-permute-start.4 = (s16[2,528,128]{2,1,0:T(8,128)(2,1)S(1)}, s16[2,528,128]{2,1,0:T(8,128)(2,1)S(1)}, u32[]{:S(2)}, u32[]{:S(2)}) collective-permute-start(s16[2,528,128]{2,1,0:T(8,128)(2,1)S(1)} %pad_add_fusion.z0), channel_id=1, source_target_pairs={{0,928},{1,929},{2,930},{3,931},{4,932},{5,933},{6,934},{7,935},{8... | collective-permute-start | bytes 811016 | tf_op jit(solution)/shard_map/cond/branch_1_fun/ppermute | solution.py:178
  59.0 0.0 collective-permute-done.2.z1
  59.0 11.8 %collective-permute-done.3.z2 = s16[2,528,128]{2,1,0:T(8,128)(2,1)S(1)} collective-permute-done((s16[2,528,128]{2,1,0:T(8,128)(2,1)S(1)}, s16[2,528,128]{2,1,0:T(8,128)(2,1)S(1)}, u32[]{:S(2)}, u32[]{:S(2)}) %collective-permute-start.3) | collective-permute-done | bytes 270368 | tf_op jit(solution)/shard_map/cond/branch_1_fun/ppermute | solution.py:178
  70.8 0.4 collective-permute-done.4.z3
  71.2 0.0 all-to-all-done.mine
  71.2 1.1 %broadcast_select_fusion.2 = s16[4,528,128]{2,1,0:T(8,128)(2,1)S(1)} fusion(s16[4,528,128]{2,1,0:T(8,128)(2,1)S(1)} %all-to-all-done.mine, pred[4]{0:T(512)(128)(4,1)S(1)} %and_bitcast_fusion, s16[528,128]{1,0:T(8,128)(2,1)} %get-tuple-element.92), kind=kLoop, calls=%fused_computation.4 | loop fusion | flops 270336 | bytes 1216516 | tf_op jit(solution)/shard_map/cond/branch_1_fun/jit(_where)/select_n | solution.py:225
  72.3 4.9 %collective-permute-start.5 = (s16[4,528,128]{2,1,0:T(8,128)(2,1)S(1)}, s16[4,528,128]{2,1,0:T(8,128)(2,1)S(1)}, u32[]{:S(2)}, u32[]{:S(2)}) collective-permute-start(s16[4,528,128]{2,1,0:T(8,128)(2,1)S(1)} %broadcast_select_fusion.2), channel_id=1, source_target_pairs={{0,1},{1,0},{2,3},{3,2},{4,5},{5,4},{6,7},{7,6},{8,9},{9,8},{10,11... | collective-permute-start | bytes 1622024 | tf_op jit(solution)/shard_map/cond/branch_1_fun/ppermute | solution.py:178
  77.2 1.5 %collective-permute-done.5.others = s16[4,528,128]{2,1,0:T(8,128)(2,1)S(1)} collective-permute-done((s16[4,528,128]{2,1,0:T(8,128)(2,1)S(1)}, s16[4,528,128]{2,1,0:T(8,128)(2,1)S(1)}, u32[]{:S(2)}, u32[]{:S(2)}) %collective-permute-start.5) | collective-permute-done | bytes 540704 | tf_op jit(solution)/shard_map/cond/branch_1_fun/ppermute | solution.py:178
  78.7 1.9 %final.2 = f32[2,2,128,128]{3,2,1,0:T(8,128)S(1)} custom-call(s32[2]{0:T(128)S(1)} %get-tuple-element.86.spot, s32[2,2]{1,0:T(2,128)S(1)} %get-tuple-element.87.keep, s16[4,528,128]{2,1,0:T(8,128)(2,1)S(1)} %all-to-all-done.mine, s16[4,528,128]{2,1,0:T(8,128)(2,1)S(1)} %collective-permute-done.5.others, s16[2,528,128]{2,1,0:T(8,128)(2,1)S(1)} %pad_add_fusion.z0, ...), custom_call_target="tpu_custom_call" | custom-call | flops 800000000 | bytes 2500000 | tf_op jit(solution)/shard_map/cond/branch_1_fun/final/pallas_call | solution.py:160
  80.6 0.9 %broadcast.23 = s16[4,528,128]{2,1,0:T(8,128)(2,1)} broadcast(s16[]{:T(256)} %constant.48.clone), dimensions={} | broadcast | bytes 540674 | tf_op jit(solution)/shard_map/broadcast.9
  81.5 0.0 collective-permute-done.11
  81.5 0.0 copy-start
  81.5 0.7 copy-done
  (8 shorter events, 0.1 us)
Async XLA Ops:
  1.2 28.7 %collective-permute-start.10 = (s16[528,128]{1,0:T(8,128)(2,1)S(1)}, s16[528,128]{1,0:T(8,128)(2,1)S(1)}, u32[]{:S(2)}, u32[]{:S(2)}) collective-permute-start(s16[528,128]{1,0:T(8,128)(2,1)S(1)} %pack_b.1), channel_id=1, source_target_pairs={{16,0},{17,1},{18,2},{19,3},{20,4},{21,5},{22,6},{23,7},{24,8},{25... | collective-permute-start | bytes 405512 | tf_op jit(solution)/shard_map/ppermute | solution.py:178
  2.5 0.7 copy-start.1
  2.5 0.7 copy-start.2
  5.3 14.0 %collective-permute-start = (s16[528,128]{1,0:T(8,128)(2,1)}, s16[528,128]{1,0:T(8,128)(2,1)}, u32[]{:S(2)}, u32[]{:S(2)}) collective-permute-start(s16[528,128]{1,0:T(8,128)(2,1)} %get-tuple-element.77), channel_id=1, source_target_pairs={{0,8},{1,9},{2,10},{3,11},{4,12},{5,13},{6,14},{7,15},{8,0},{9,1},... | collective-permute-start | bytes 405512 | tf_op jit(solution)/shard_map/cond/branch_1_fun/ppermute | solution.py:178
  21.2 60.2 %collective-permute-start.11 = (s16[528,128]{1,0:T(8,128)(2,1)S(1)}, s16[528,128]{1,0:T(8,128)(2,1)S(1)}, u32[]{:S(2)}, u32[]{:S(2)}) collective-permute-start(s16[528,128]{1,0:T(8,128)(2,1)S(1)} %pack_b.1), channel_id=1, source_target_pairs={{0,1008},{1,1009},{2,1010},{3,1011},{4,1012},{5,1013},{6,1014},{7,... | collective-permute-start | bytes 405512 | tf_op jit(solution)/shard_map/ppermute | solution.py:178
  29.9 0.7 copy-start.3
  30.6 40.6 %all-to-all-start = ((s16[4,528,128]{2,1,0:T(8,128)(2,1)}), s16[4,528,128]{2,1,0:T(8,128)(2,1)S(1)}, u32[]{:S(2)}, u32[]{:S(2)}) async-start(s16[4,528,128]{2,1,0:T(8,128)(2,1)} %get-tuple-element.88), calls=%async_computation | async-start | bytes 1081344 | tf_op jit(solution)/shard_map/cond/branch_1_fun/all_to_all | solution.py:221
  44.5 14.6 %collective-permute-start.2 = (s16[2,528,128]{2,1,0:T(8,128)(2,1)S(1)}, s16[2,528,128]{2,1,0:T(8,128)(2,1)S(1)}, u32[]{:S(2)}, u32[]{:S(2)}) collective-permute-start(s16[2,528,128]{2,1,0:T(8,128)(2,1)S(1)} %pad_add_fusion.z0), channel_id=1, source_target_pairs={{0,992},{1,993},{2,994},{3,995},{4,996},{5,997},{6,998},{7,999},{8... | collective-permute-start | bytes 811016 | tf_op jit(solution)/shard_map/cond/branch_1_fun/ppermute | solution.py:178
  53.2 17.6 %collective-permute-start.3 = (s16[2,528,128]{2,1,0:T(8,128)(2,1)S(1)}, s16[2,528,128]{2,1,0:T(8,128)(2,1)S(1)}, u32[]{:S(2)}, u32[]{:S(2)}) collective-permute-start(s16[2,528,128]{2,1,0:T(8,128)(2,1)S(1)} %pad_add_fusion.z0), channel_id=1, source_target_pairs={{0,960},{1,961},{2,962},{3,963},{4,964},{5,965},{6,966},{7,967},{8... | collective-permute-start | bytes 811016 | tf_op jit(solution)/shard_map/cond/branch_1_fun/ppermute | solution.py:178
  55.7 15.5 %collective-permute-start.4 = (s16[2,528,128]{2,1,0:T(8,128)(2,1)S(1)}, s16[2,528,128]{2,1,0:T(8,128)(2,1)S(1)}, u32[]{:S(2)}, u32[]{:S(2)}) collective-permute-start(s16[2,528,128]{2,1,0:T(8,128)(2,1)S(1)} %pad_add_fusion.z0), channel_id=1, source_target_pairs={{0,928},{1,929},{2,930},{3,931},{4,932},{5,933},{6,934},{7,935},{8... | collective-permute-start | bytes 811016 | tf_op jit(solution)/shard_map/cond/branch_1_fun/ppermute | solution.py:178
  72.3 6.4 %collective-permute-start.5 = (s16[4,528,128]{2,1,0:T(8,128)(2,1)S(1)}, s16[4,528,128]{2,1,0:T(8,128)(2,1)S(1)}, u32[]{:S(2)}, u32[]{:S(2)}) collective-permute-start(s16[4,528,128]{2,1,0:T(8,128)(2,1)S(1)} %broadcast_select_fusion.2), channel_id=1, source_target_pairs={{0,1},{1,0},{2,3},{3,2},{4,5},{5,4},{6,7},{7,6},{8,9},{9,8},{10,11... | collective-permute-start | bytes 1622024 | tf_op jit(solution)/shard_map/cond/branch_1_fun/ppermute | solution.py:178
  81.5 0.7 copy-start

commit v3 on v2

--- a/solution.py
+++ b/solution.py
@@ -149,10 +149,10 @@
             out[i, j] = jnp.where(keep[i, j] == 1, block, 0.0)
 
 
-def final(spot, keep, mine, others, z0, z1, z2, z3, out):
+def final(spot, keep, mine, others, b0, b1, b2, b3, c0, c1, c2, c3, out):
     total = jnp.zeros((2 * BS, 2 * BS), jnp.float32)
-    for s, t, z in zip(*slots_of(spot), (z0, z1, z2, z3)):
-        total = total + section(mine.at[s], z.at[0]) + section(others.at[t], z.at[1])
+    for s, t, b, c in zip(*slots_of(spot), (b0, b1, b2, b3), (c0, c1, c2, c3)):
+        total = total + section(mine.at[s], b) + section(others.at[t], c)
     kept(keep, total, out)
 
 
@@ -209,39 +209,58 @@
     slot = lax.broadcasted_iota(jnp.int32, (4, 1, 1), 0)
     quads = [[8 * h + 2 * j + c for j in range(4)] for h in range(cols // 8) for c in range(2)]
 
-    def far_half(plane, blocks):
-        a_own, a_sent = packed_a(blocks, a_rows, a_count.T, chip_at)
+    def own_spread(plane, b_own):
+        def by_core(at):
+            part = lambda p, q: plane(p, q) and q % 2 == at
+            return lambda b: tuple(spread(b, t, part) for t in (1, 2, 3))
+
+        return lax.cond(core == 0, by_core(0), by_core(1), b_own)
+
+    def packed(b_own):
+        return packed_a(after(a_blocks, b_own), a_rows, a_count.T, chip_at)
+
+    def first_steps(plane, b_own, a_own, a_sent):
         a_far = go(a_sent, goal=lambda p, q: (p, q ^ 8), takes_part=plane)
-        return jnp.where(slot <= in_quad, a_own[None], a_far[None]), a_far
-
-    def nothing():
-        return jnp.zeros((4, *PIECE.shape), PIECE.dtype), jnp.zeros(PIECE.shape, PIECE.dtype)
-
-    def shared(plane, b_own, b_next, give, a_far):
-        mine = lax.all_to_all(give, "col", 0, 0, axis_index_groups=quads)
-        pair = jnp.stack([b_own, b_next])
-        pairs = [pair] + [spread(pair, t, plane) for t in (1, 2, 3)]
+        b_same = own_spread(plane, after(b_own, a_own))
+        return (jnp.where(slot <= in_quad, a_own[None], a_far[None]), a_far, *b_same)
+
+    def last_steps(plane, b_own, b_next, sets):
+        offered, a_far, *b_same = sets
+        mine = lax.all_to_all(offered, "col", 0, 0, axis_index_groups=quads)
+        b_other = [spread(b_next, t, plane) for t in (1, 2, 3)]
         own_slot = jnp.logical_and(slot == in_quad, core == 0)
-        given = jnp.where(own_slot, a_far[None], after(mine, pairs))
+        given = jnp.where(own_slot, a_far[None], after(mine, b_other))
         others = go(given, goal=lambda p, q: (p, q ^ 1), takes_part=plane)
-        return summed(final, [spot, c_keep], mine, others, *pairs)
+        out = summed(final, [spot, c_keep], mine, others, b_own, *b_same, b_next, *b_other)
+        return out, others, b_other
+
+    def blank():
+        return jnp.zeros(PIECE.shape, PIECE.dtype)
+
+    def open_low(b_own):
+        return first_steps(low_plane, b_own, *packed(b_own))
+
+    def open_high(b_own):
+        return (jnp.zeros((4, *PIECE.shape), PIECE.dtype), blank(), *packed(b_own), blank())
+
+    def close_low(b_own, b_next, sets):
+        out, others, b_other = last_steps(low_plane, b_own, b_next, sets)
+        return (out, others, blank(), *b_other)
+
+    def middle_high(b_own, b_next, sets):
+        empty = jnp.zeros((2, 2, BS, BS), jnp.float32)
+        return (empty, *first_steps(high_plane, b_own, sets[2], sets[3]))
 
     b_own = packed_b(b_blocks, b_cols, b_count.T)
     b_next_low = go(b_own, goal=back, takes_part=high_plane)
-    blocks = after(a_blocks, b_own)
-    low_a = lax.cond(on_low, lambda x: far_half(low_plane, x), lambda x: nothing(), blocks)
-    b_next_high = go(after(b_own, low_a[0]), goal=back, takes_part=low_plane)
-    out, high_a = lax.cond(
-        on_low,
-        lambda x, b, n, a: (shared(low_plane, b, n, *a), nothing()),
-        lambda x, b, n, a: (jnp.zeros((2, 2, BS, BS), jnp.float32), far_half(high_plane, x)),
-        blocks, b_own, b_next_low, low_a,
-    )
+    sets_low = lax.cond(on_low, open_low, open_high, b_own)
+    b_next_high = go(after(b_own, sets_low[0]), goal=back, takes_part=low_plane)
+    out, *sets_high = lax.cond(on_low, close_low, middle_high, b_own, b_next_low, sets_low)
     return lax.cond(
         on_low,
-        lambda o, b, n, a: o,
-        lambda o, b, n, a: shared(high_plane, b, n, *a),
-        out, b_own, b_next_high, high_a,
+        lambda o, b, n, sets: o,
+        lambda o, b, n, sets: last_steps(high_plane, b, n, sets)[0],
+        out, b_own, b_next_high, sets_high,
     )
 
 

time: 82.7 us -> 78.8 us (0.953)
  the two profiles are of different devices: /device:TPU:1 before, /device:TPU:577 now
where the time goes in v3:
time: 78.8 us; the launch traced here: 78.2 us
  starting transfers between devices  50.3 us (64%)
  waiting for transfers between devices  15.6 us (20%)
  Pallas kernels  5.6 us (7%)
  local copies, waits for them, and re-layouts  4.27 us (5%)
  other arithmetic  2.16 us (3%)
    ppermute x10, starting transfers between devices, moved(): return lax.ppermute(x, ('row', 'col'), pairs)  41 us
    ppermute x10, waiting for transfers between devices, moved(): return lax.ppermute(x, ('row', 'col'), pairs)  15.6 us
    all_to_all x1, starting transfers between devices, last_steps(): mine = lax.all_to_all(offered, 'col', 0, 0, axis_index_groups=quads)  9.27 us
    pallas_call x1, Pallas kernels, summed(): pl.pallas_call(body, out_shape=jax.ShapeDtypeStruct((2, 2, BS, BS), jnp.f...  2.35 us
    another operation x4, local copies, waits for them, and re-layouts  2.22 us
    pallas_call x1, Pallas kernels, packed_a(): pl.pallas_call(pack_a, out_shape=(PIECE,) * 2, in_specs=[SMEM, SMEM, SMEM...  2.06 us
    unnamed x8, local copies, waits for them, and re-layouts  2.03 us
    select_n x1, other arithmetic, first_steps(): jnp.where(slot <= in_quad, a_own[None], a_far[None])  1.9 us
  transfers between devices with their start and end apart: 11, of which 5 were waited for; matrix products, arithmetic and copies ran while one was open for 5% of the time, Pallas kernels for 3%

profile of v3, /device:TPU:577, one launch (start us, length us, event | category | flops | bytes accessed | tf_op | source)
XLA Modules:
  0.0 78.2 jit_solution(9176548871774878359)
XLA Ops:
  0.0 1.2 %pack_b.1 = s16[528,128]{1,0:T(8,128)(2,1)S(1)} custom-call(s32[2,4]{1,0:T(2,128)} %which.1, s32[1,2]{1,0:T(1,128)} %bitcast.16, bf16[2,4,128,128]{3,2,1,0:T(8,128)(2,1)} %blocks.1), custom_call_target="tpu_custom_call" | custom-call | flops 2000000 | bytes 400000 | tf_op jit(solution)/shard_map/pack_b/pallas_call | solution.py:84
  1.2 1.3 %collective-permute-start.22 = (s16[528,128]{1,0:T(8,128)(2,1)S(1)}, s16[528,128]{1,0:T(8,128)(2,1)S(1)}, u32[]{:S(2)}, u32[]{:S(2)}) collective-permute-start(s16[528,128]{1,0:T(8,128)(2,1)S(1)} %pack_b.1), channel_id=1, source_target_pairs={{16,0},{17,1},{18,2},{19,3},{20,4},{21,5},{22,6},{23,7},{24,8},{25... | collective-permute-start | bytes 405512 | tf_op jit(solution)/shard_map/ppermute | solution.py:178
  2.5 0.0 copy-start.1
  2.5 0.0 copy-start.2
  2.6 0.7 copy-done.1
  3.2 0.0 copy-done.2
  3.2 4.3 %conditional.5 = (s16[4,528,128]{2,1,0:T(8,128)(2,1)}, s16[528,128]{1,0:T(8,128)(2,1)}, s16[528,128]{1,0:T(8,128)(2,1)}, s16[528,128]{1,0:T(8,128)(2,1)}, s16[528,128]{1,0:T(8,128)(2,1)}) conditional(s32[]{:T(128)} %convert_element_type.11, (s32[4,1]{0,1:T(1,128)S(1)}, bf16[4,4,128,128]{3,2,1,0:T(8,128)(2,1)}, s32[4,4]{1,0:T(4,128)S(1)}, ...), branch_computations={%region_0.1_spmd, %region_1.4_spmd} | conditional | flops 4270342 | bytes 3773962 | solution.py:256
  3.2 2.1 %pack_a.2 = (s16[528,128]{1,0:T(8,128)(2,1)}, s16[528,128]{1,0:T(8,128)(2,1)}) custom-call(s32[4,4]{1,0:T(4,128)S(1)} %get-tuple-element.99.which, s32[1,4]{1,0:T(1,128)S(1)} %bitcast.14, s32[1]{0:T(128)} %get-tuple-element.101.chip, bf16[4,4,128,128]{3,2,1,0:T(8,128)(2,1)} %get-tuple-element.102.blocks), custom_call_target="tpu_custom_call" | custom-call | flops 4000000 | bytes 800000 | tf_op jit(solution)/shard_map/cond/branch_0_fun/pack_a/pallas_call | solution.py:95
  5.3 0.9 %broadcast.18 = s16[4,528,128]{2,1,0:T(8,128)(2,1)} broadcast(s16[]{:T(256)} %constant.47.clone), dimensions={} | broadcast | bytes 540674 | tf_op jit(solution)/shard_map/broadcast.3
  6.1 0.7 broadcast.19
  6.8 0.7 broadcast.19.clone
  7.5 1.3 %collective-permute-start.23 = (s16[528,128]{1,0:T(8,128)(2,1)S(1)}, s16[528,128]{1,0:T(8,128)(2,1)S(1)}, u32[]{:S(2)}, u32[]{:S(2)}) collective-permute-start(s16[528,128]{1,0:T(8,128)(2,1)S(1)} %pack_b.1), channel_id=1, source_target_pairs={{0,1008},{1,1009},{2,1010},{3,1011},{4,1012},{5,1013},{6,1014},{7,... | collective-permute-start | bytes 405512 | tf_op jit(solution)/shard_map/ppermute | solution.py:178
  8.8 0.1 pad_add_fusion
  8.9 0.0 collective-permute-done.22
  8.9 0.0 copy-start.3
  8.9 0.7 copy-done.3
  9.5 26.7 %conditional.6 = (s16[4,528,128]{2,1,0:T(8,128)(2,1)}, s16[528,128]{1,0:T(8,128)(2,1)S(1)}, s16[528,128]{1,0:T(8,128)(2,1)}, s16[528,128]{1,0:T(8,128)(2,1)}, s1...) conditional(s32[]{:T(128)} %convert_element_type.11, (s32[]{:T(128)}, s32[4,1,1]{0,2,1:T(1,128)S(1)}, ...), branch_computations={%region_4.7_spmd, %region_7.8_spmd} | conditional | flops 800270336 | bytes 9258680 | solution.py:258
  9.5 5.7 %collective-permute-start.13 = (s16[528,128]{1,0:T(8,128)(2,1)}, s16[528,128]{1,0:T(8,128)(2,1)S(1)}, u32[]{:S(2)}, u32[]{:S(2)}) collective-permute-start(s16[528,128]{1,0:T(8,128)(2,1)} %get-tuple-element.123), channel_id=1, source_target_pairs={{16,24},{17,25},{18,26},{19,27},{20,28},{21,29},{22,30},{23,31},{2... | collective-permute-start | bytes 405512 | tf_op jit(solution)/shard_map/cond/branch_0_fun/ppermute | solution.py:178
  15.2 19.1 %conditional.1 = (s16[528,128]{1,0:T(8,128)(2,1)}, s16[528,128]{1,0:T(8,128)(2,1)}, s16[528,128]{1,0:T(8,128)(2,1)}) conditional(s32[]{:T(128)} %convert_element_type.6, s16[528,128]{1,0:T(8,128)(2,1)S(1)} %get-tuple-element.126, s16[528,128]{1,0:T(8,128)(2,1)S(1)} %get-tuple-element.126), branch_computations={%region_5.5_spmd, %region_6.6_spmd} | conditional | bytes 1622160 | solution.py:217
  15.2 7.3 %collective-permute-start.6 = (s16[528,128]{1,0:T(8,128)(2,1)S(1)}, s16[528,128]{1,0:T(8,128)(2,1)}, u32[]{:S(2)}, u32[]{:S(2)}) collective-permute-start(s16[528,128]{1,0:T(8,128)(2,1)S(1)} %param.4), channel_id=1, source_target_pairs={{17,1009},{19,1011},{21,1013},{23,1015},{25,1017},{27,1019},{29,10... | collective-permute-start | bytes 405512 | tf_op jit(solution)/shard_map/cond/branch_0_fun/cond/branch_0_fun/ppermute | solution.py:178
  22.5 2.4 %collective-permute-start.7 = (s16[528,128]{1,0:T(8,128)(2,1)S(1)}, s16[528,128]{1,0:T(8,128)(2,1)}, u32[]{:S(2)}, u32[]{:S(2)}) collective-permute-start(s16[528,128]{1,0:T(8,128)(2,1)S(1)} %param.4), channel_id=1, source_target_pairs={{17,977},{19,979},{21,981},{23,983},{25,985},{27,987},{29,989},{31... | collective-permute-start | bytes 405512 | tf_op jit(solution)/shard_map/cond/branch_0_fun/cond/branch_0_fun/ppermute | solution.py:178
  25.0 3.3 %collective-permute-start.8 = (s16[528,128]{1,0:T(8,128)(2,1)S(1)}, s16[528,128]{1,0:T(8,128)(2,1)}, u32[]{:S(2)}, u32[]{:S(2)}) collective-permute-start(s16[528,128]{1,0:T(8,128)(2,1)S(1)} %param.4), channel_id=1, source_target_pairs={{17,945},{19,947},{21,949},{23,951},{25,953},{27,955},{29,957},{31... | collective-permute-start | bytes 405512 | tf_op jit(solution)/shard_map/cond/branch_0_fun/cond/branch_0_fun/ppermute | solution.py:178
  28.3 0.0 collective-permute-done.6
  28.3 4.5 %collective-permute-done.7 = s16[528,128]{1,0:T(8,128)(2,1)} collective-permute-done((s16[528,128]{1,0:T(8,128)(2,1)S(1)}, s16[528,128]{1,0:T(8,128)(2,1)}, u32[]{:S(2)}, u32[]{:S(2)}) %collective-permute-start.7) | collective-permute-done | bytes 135200 | tf_op jit(solution)/shard_map/cond/branch_0_fun/cond/branch_0_fun/ppermute | solution.py:178
  32.8 1.4 %collective-permute-done.8 = s16[528,128]{1,0:T(8,128)(2,1)} collective-permute-done((s16[528,128]{1,0:T(8,128)(2,1)S(1)}, s16[528,128]{1,0:T(8,128)(2,1)}, u32[]{:S(2)}, u32[]{:S(2)}) %collective-permute-start.8) | collective-permute-done | bytes 135200 | tf_op jit(solution)/shard_map/cond/branch_0_fun/cond/branch_0_fun/ppermute | solution.py:178
  34.3 0.0 collective-permute-done.13
  34.3 1.9 %broadcast_select_fusion.1 = s16[4,528,128]{2,1,0:T(8,128)(2,1)} fusion(pred[4]{0:T(512)(128)(4,1)S(1)} %compare_bitcast_fusion.1, s16[528,128]{1,0:T(8,128)(2,1)S(1)} %collective-permute-done.13, s16[528,128]{1,0:T(8,128)(2,1)} %get-tuple-element.122), kind=kLoop, calls=%fused_computation.2 | loop fusion | flops 270336 | bytes 811012 | tf_op jit(solution)/shard_map/cond/branch_0_fun/jit(_where)/select_n | solution.py:225
  36.2 0.0 collective-permute-done.23
  36.2 41.3 %conditional.7 = (f32[2,2,128,128]{3,2,1,0:T(8,128)S(1)}) conditional(s32[]{:T(128)} %convert_element_type.11, (s16[4,528,128]{2,1,0:T(8,128)(2,1)}, s32[]{:T(128)}, s32[4,1,1]{0,2,1:T(1,128)S(1)}, s32[]{:T(128)}, s16[528,128]{1,0:T(8,128)(2,1)S(1)}, /*index=5*/s16[528,128]{1,0:T(8,128)(2,1)S(1)}, s32[2]{0:T(128)S(1)}, s32[2,2]{1,0:T(2,128)S(1)}, ...), branch_computations={%region_8.9_spmd, %region_9.10_spmd} | conditional | flops 800270336 | bytes 9123470 | solution.py:259
  36.3 9.3 %all-to-all-start.1 = ((s16[4,528,128]{2,1,0:T(8,128)(2,1)}), s16[4,528,128]{2,1,0:T(8,128)(2,1)S(1)}, u32[]{:S(2)}, u32[]{:S(2)}) async-start(s16[4,528,128]{2,1,0:T(8,128)(2,1)} %get-tuple-element.145), calls=%async_computation.1 | async-start | bytes 1081344 | tf_op jit(solution)/shard_map/cond/branch_0_fun/all_to_all | solution.py:229
  45.5 12.8 %collective-permute-start.18 = (s16[528,128]{1,0:T(8,128)(2,1)S(1)}, s16[528,128]{1,0:T(8,128)(2,1)S(1)}, u32[]{:S(2)}, u32[]{:S(2)}) collective-permute-start(s16[528,128]{1,0:T(8,128)(2,1)S(1)} %get-tuple-element.150.c0), channel_id=1, source_target_pairs={{16,1008},{17,1009},{18,1010},{19,1011},{20,1012},{21,1013},{22,10... | collective-permute-start | bytes 405512 | tf_op jit(solution)/shard_map/cond/branch_0_fun/ppermute | solution.py:178
  58.4 1.9 %collective-permute-start.19 = (s16[528,128]{1,0:T(8,128)(2,1)S(1)}, s16[528,128]{1,0:T(8,128)(2,1)S(1)}, u32[]{:S(2)}, u32[]{:S(2)}) collective-permute-start(s16[528,128]{1,0:T(8,128)(2,1)S(1)} %get-tuple-element.150.c0), channel_id=1, source_target_pairs={{16,976},{17,977},{18,978},{19,979},{20,980},{21,981},{22,982},{23... | collective-permute-start | bytes 405512 | tf_op jit(solution)/shard_map/cond/branch_0_fun/ppermute | solution.py:178
  60.3 1.9 %collective-permute-start.20 = (s16[528,128]{1,0:T(8,128)(2,1)S(1)}, s16[528,128]{1,0:T(8,128)(2,1)S(1)}, u32[]{:S(2)}, u32[]{:S(2)}) collective-permute-start(s16[528,128]{1,0:T(8,128)(2,1)S(1)} %get-tuple-element.150.c0), channel_id=1, source_target_pairs={{16,944},{17,945},{18,946},{19,947},{20,948},{21,949},{22,950},{23... | collective-permute-start | bytes 405512 | tf_op jit(solution)/shard_map/cond/branch_0_fun/ppermute | solution.py:178
  62.2 0.0 collective-permute-done.18.c1
  62.2 5.8 %collective-permute-done.19.c2 = s16[528,128]{1,0:T(8,128)(2,1)S(1)} collective-permute-done((s16[528,128]{1,0:T(8,128)(2,1)S(1)}, s16[528,128]{1,0:T(8,128)(2,1)S(1)}, u32[]{:S(2)}, u32[]{:S(2)}) %collective-permute-start.19) | collective-permute-done | bytes 135200 | tf_op jit(solution)/shard_map/cond/branch_0_fun/ppermute | solution.py:178
  68.0 2.3 %collective-permute-done.20.c3 = s16[528,128]{1,0:T(8,128)(2,1)S(1)} collective-permute-done((s16[528,128]{1,0:T(8,128)(2,1)S(1)}, s16[528,128]{1,0:T(8,128)(2,1)S(1)}, u32[]{:S(2)}, u32[]{:S(2)}) %collective-permute-start.20) | collective-permute-done | bytes 135200 | tf_op jit(solution)/shard_map/cond/branch_0_fun/ppermute | solution.py:178
  70.3 0.0 all-to-all-done.1.mine
  70.3 0.2 broadcast_select_fusion.3
  70.5 3.1 %collective-permute-start.21 = (s16[4,528,128]{2,1,0:T(8,128)(2,1)S(1)}, s16[4,528,128]{2,1,0:T(8,128)(2,1)S(1)}, u32[]{:S(2)}, u32[]{:S(2)}) collective-permute-start(s16[4,528,128]{2,1,0:T(8,128)(2,1)S(1)} %broadcast_select_fusion.3), channel_id=1, source_target_pairs={{16,17},{17,16},{18,19},{19,18},{20,21},{21,20},{22,23},{23,22},{2... | collective-permute-start | bytes 1622024 | tf_op jit(solution)/shard_map/cond/branch_0_fun/ppermute | solution.py:178
  73.6 1.5 %collective-permute-done.21.others = s16[4,528,128]{2,1,0:T(8,128)(2,1)S(1)} collective-permute-done((s16[4,528,128]{2,1,0:T(8,128)(2,1)S(1)}, s16[4,528,128]{2,1,0:T(8,128)(2,1)S(1)}, u32[]{:S(2)}, u32[]{:S(2)}) %collective-permute-start.21) | collective-permute-done | bytes 540704 | tf_op jit(solution)/shard_map/cond/branch_0_fun/ppermute | solution.py:178
  75.1 2.4 %final.3 = f32[2,2,128,128]{3,2,1,0:T(8,128)S(1)} custom-call(s32[2]{0:T(128)S(1)} %get-tuple-element.143.spot, s32[2,2]{1,0:T(2,128)S(1)} %get-tuple-element.144.keep, s16[4,528,128]{2,1,0:T(8,128)(2,1)S(1)} %all-to-all-done.1.mine, s16[4,528,128]{2,1,0:T(8,128)(2,1)S(1)} %collective-permute-done.21.others, s16[528,128]{1,0:T(8,128)(2,1)S(1)} %get-tuple-element.152.b0, ...), custom_call_target="tpu_custom_call" | custom-call | flops 800000000 | bytes 2500000 | tf_op jit(solution)/shard_map/cond/branch_0_fun/final/pallas_call | solution.py:160
  77.5 0.0 copy-start
  77.5 0.7 copy-done
  (7 shorter events, 0.0 us)
Async XLA Ops:
  1.2 7.7 %collective-permute-start.22 = (s16[528,128]{1,0:T(8,128)(2,1)S(1)}, s16[528,128]{1,0:T(8,128)(2,1)S(1)}, u32[]{:S(2)}, u32[]{:S(2)}) collective-permute-start(s16[528,128]{1,0:T(8,128)(2,1)S(1)} %pack_b.1), channel_id=1, source_target_pairs={{16,0},{17,1},{18,2},{19,3},{20,4},{21,5},{22,6},{23,7},{24,8},{25... | collective-permute-start | bytes 405512 | tf_op jit(solution)/shard_map/ppermute | solution.py:178
  2.5 0.7 copy-start.1
  2.5 0.7 copy-start.2
  7.5 28.7 %collective-permute-start.23 = (s16[528,128]{1,0:T(8,128)(2,1)S(1)}, s16[528,128]{1,0:T(8,128)(2,1)S(1)}, u32[]{:S(2)}, u32[]{:S(2)}) collective-permute-start(s16[528,128]{1,0:T(8,128)(2,1)S(1)} %pack_b.1), channel_id=1, source_target_pairs={{0,1008},{1,1009},{2,1010},{3,1011},{4,1012},{5,1013},{6,1014},{7,... | collective-permute-start | bytes 405512 | tf_op jit(solution)/shard_map/ppermute | solution.py:178
  8.9 0.7 copy-start.3
  9.5 24.8 %collective-permute-start.13 = (s16[528,128]{1,0:T(8,128)(2,1)}, s16[528,128]{1,0:T(8,128)(2,1)S(1)}, u32[]{:S(2)}, u32[]{:S(2)}) collective-permute-start(s16[528,128]{1,0:T(8,128)(2,1)} %get-tuple-element.123), channel_id=1, source_target_pairs={{16,24},{17,25},{18,26},{19,27},{20,28},{21,29},{22,30},{23,31},{2... | collective-permute-start | bytes 405512 | tf_op jit(solution)/shard_map/cond/branch_0_fun/ppermute | solution.py:178
  15.2 13.0 %collective-permute-start.6 = (s16[528,128]{1,0:T(8,128)(2,1)S(1)}, s16[528,128]{1,0:T(8,128)(2,1)}, u32[]{:S(2)}, u32[]{:S(2)}) collective-permute-start(s16[528,128]{1,0:T(8,128)(2,1)S(1)} %param.4), channel_id=1, source_target_pairs={{17,1009},{19,1011},{21,1013},{23,1015},{25,1017},{27,1019},{29,10... | collective-permute-start | bytes 405512 | tf_op jit(solution)/shard_map/cond/branch_0_fun/cond/branch_0_fun/ppermute | solution.py:178
  22.5 10.3 %collective-permute-start.7 = (s16[528,128]{1,0:T(8,128)(2,1)S(1)}, s16[528,128]{1,0:T(8,128)(2,1)}, u32[]{:S(2)}, u32[]{:S(2)}) collective-permute-start(s16[528,128]{1,0:T(8,128)(2,1)S(1)} %param.4), channel_id=1, source_target_pairs={{17,977},{19,979},{21,981},{23,983},{25,985},{27,987},{29,989},{31... | collective-permute-start | bytes 405512 | tf_op jit(solution)/shard_map/cond/branch_0_fun/cond/branch_0_fun/ppermute | solution.py:178
  25.0 9.3 %collective-permute-start.8 = (s16[528,128]{1,0:T(8,128)(2,1)S(1)}, s16[528,128]{1,0:T(8,128)(2,1)}, u32[]{:S(2)}, u32[]{:S(2)}) collective-permute-start(s16[528,128]{1,0:T(8,128)(2,1)S(1)} %param.4), channel_id=1, source_target_pairs={{17,945},{19,947},{21,949},{23,951},{25,953},{27,955},{29,957},{31... | collective-permute-start | bytes 405512 | tf_op jit(solution)/shard_map/cond/branch_0_fun/cond/branch_0_fun/ppermute | solution.py:178
  36.3 34.1 %all-to-all-start.1 = ((s16[4,528,128]{2,1,0:T(8,128)(2,1)}), s16[4,528,128]{2,1,0:T(8,128)(2,1)S(1)}, u32[]{:S(2)}, u32[]{:S(2)}) async-start(s16[4,528,128]{2,1,0:T(8,128)(2,1)} %get-tuple-element.145), calls=%async_computation.1 | async-start | bytes 1081344 | tf_op jit(solution)/shard_map/cond/branch_0_fun/all_to_all | solution.py:229
  45.5 16.7 %collective-permute-start.18 = (s16[528,128]{1,0:T(8,128)(2,1)S(1)}, s16[528,128]{1,0:T(8,128)(2,1)S(1)}, u32[]{:S(2)}, u32[]{:S(2)}) collective-permute-start(s16[528,128]{1,0:T(8,128)(2,1)S(1)} %get-tuple-element.150.c0), channel_id=1, source_target_pairs={{16,1008},{17,1009},{18,1010},{19,1011},{20,1012},{21,1013},{22,10... | collective-permute-start | bytes 405512 | tf_op jit(solution)/shard_map/cond/branch_0_fun/ppermute | solution.py:178
  58.4 9.7 %collective-permute-start.19 = (s16[528,128]{1,0:T(8,128)(2,1)S(1)}, s16[528,128]{1,0:T(8,128)(2,1)S(1)}, u32[]{:S(2)}, u32[]{:S(2)}) collective-permute-start(s16[528,128]{1,0:T(8,128)(2,1)S(1)} %get-tuple-element.150.c0), channel_id=1, source_target_pairs={{16,976},{17,977},{18,978},{19,979},{20,980},{21,981},{22,982},{23... | collective-permute-start | bytes 405512 | tf_op jit(solution)/shard_map/cond/branch_0_fun/ppermute | solution.py:178
  60.3 10.1 %collective-permute-start.20 = (s16[528,128]{1,0:T(8,128)(2,1)S(1)}, s16[528,128]{1,0:T(8,128)(2,1)S(1)}, u32[]{:S(2)}, u32[]{:S(2)}) collective-permute-start(s16[528,128]{1,0:T(8,128)(2,1)S(1)} %get-tuple-element.150.c0), channel_id=1, source_target_pairs={{16,944},{17,945},{18,946},{19,947},{20,948},{21,949},{22,950},{23... | collective-permute-start | bytes 405512 | tf_op jit(solution)/shard_map/cond/branch_0_fun/ppermute | solution.py:178
  70.5 4.6 %collective-permute-start.21 = (s16[4,528,128]{2,1,0:T(8,128)(2,1)S(1)}, s16[4,528,128]{2,1,0:T(8,128)(2,1)S(1)}, u32[]{:S(2)}, u32[]{:S(2)}) collective-permute-start(s16[4,528,128]{2,1,0:T(8,128)(2,1)S(1)} %broadcast_select_fusion.3), channel_id=1, source_target_pairs={{16,17},{17,16},{18,19},{19,18},{20,21},{21,20},{22,23},{23,22},{2... | collective-permute-start | bytes 1622024 | tf_op jit(solution)/shard_map/cond/branch_0_fun/ppermute | solution.py:178
  77.5 0.7 copy-start

commit v4 on v3

--- a/solution.py
+++ b/solution.py
@@ -149,10 +149,19 @@
             out[i, j] = jnp.where(keep[i, j] == 1, block, 0.0)
 
 
-def final(spot, keep, mine, others, b0, b1, b2, b3, c0, c1, c2, c3, out):
+def even(spot, mine, b0, b1, b2, b3, out):
     total = jnp.zeros((2 * BS, 2 * BS), jnp.float32)
-    for s, t, b, c in zip(*slots_of(spot), (b0, b1, b2, b3), (c0, c1, c2, c3)):
-        total = total + section(mine.at[s], b) + section(others.at[t], c)
+    for s, b in zip(slots_of(spot)[0], (b0, b1, b2, b3)):
+        total = total + section(mine.at[s], b)
+    for i in range(2):
+        for j in range(2):
+            out[i, j] = total[i * BS : (i + 1) * BS, j * BS : (j + 1) * BS]
+
+
+def odd(spot, keep, begun, others, c0, c1, c2, c3, out):
+    total = jnp.concatenate([jnp.concatenate([begun[i, 0], begun[i, 1]], axis=1) for i in range(2)], axis=0)
+    for t, c in zip(slots_of(spot)[1], (c0, c1, c2, c3)):
+        total = total + section(others.at[t], c)
     kept(keep, total, out)
 
 
@@ -209,47 +218,55 @@
     slot = lax.broadcasted_iota(jnp.int32, (4, 1, 1), 0)
     quads = [[8 * h + 2 * j + c for j in range(4)] for h in range(cols // 8) for c in range(2)]
 
-    def own_spread(plane, b_own):
+    def own_spread(plane, b_own, steps):
         def by_core(at):
             part = lambda p, q: plane(p, q) and q % 2 == at
-            return lambda b: tuple(spread(b, t, part) for t in (1, 2, 3))
+            return lambda b: tuple(spread(b, t, part) for t in steps)
 
         return lax.cond(core == 0, by_core(0), by_core(1), b_own)
 
     def packed(b_own):
         return packed_a(after(a_blocks, b_own), a_rows, a_count.T, chip_at)
 
-    def first_steps(plane, b_own, a_own, a_sent):
+    def first_steps(plane, b_own, a_own, a_sent, steps):
         a_far = go(a_sent, goal=lambda p, q: (p, q ^ 8), takes_part=plane)
-        b_same = own_spread(plane, after(b_own, a_own))
-        return (jnp.where(slot <= in_quad, a_own[None], a_far[None]), a_far, *b_same)
-
-    def last_steps(plane, b_own, b_next, sets):
-        offered, a_far, *b_same = sets
-        mine = lax.all_to_all(offered, "col", 0, 0, axis_index_groups=quads)
+        return (a_far, *own_spread(plane, after(b_own, a_own), steps))
+
+    def offered(a_own, a_far):
+        return jnp.where(slot <= in_quad, a_own[None], a_far[None])
+
+    def last_steps(plane, b_own, b_next, offer, a_far, b_same):
+        mine = lax.all_to_all(offer, "col", 0, 0, axis_index_groups=quads)
         b_other = [spread(b_next, t, plane) for t in (1, 2, 3)]
         own_slot = jnp.logical_and(slot == in_quad, core == 0)
         given = jnp.where(own_slot, a_far[None], after(mine, b_other))
         others = go(given, goal=lambda p, q: (p, q ^ 1), takes_part=plane)
-        out = summed(final, [spot, c_keep], mine, others, b_own, *b_same, b_next, *b_other)
+        begun = summed(even, [spot], mine, b_own, *b_same)
+        out = summed(odd, [spot, c_keep], begun, others, b_next, *b_other)
         return out, others, b_other
 
     def blank():
         return jnp.zeros(PIECE.shape, PIECE.dtype)
 
     def open_low(b_own):
-        return first_steps(low_plane, b_own, *packed(b_own))
+        a_own, a_sent = packed(b_own)
+        return (a_own, *first_steps(low_plane, b_own, a_own, a_sent, (1, 2, 3)))
 
     def open_high(b_own):
-        return (jnp.zeros((4, *PIECE.shape), PIECE.dtype), blank(), *packed(b_own), blank())
+        a_own, a_sent = packed(b_own)
+        return (a_own, a_sent, blank(), blank(), blank())
 
     def close_low(b_own, b_next, sets):
-        out, others, b_other = last_steps(low_plane, b_own, b_next, sets)
+        a_own, a_far, *b_same = sets
+        offer = offered(a_own, a_far)
+        out, others, b_other = last_steps(low_plane, b_own, b_next, offer, a_far, b_same)
         return (out, others, blank(), *b_other)
 
     def middle_high(b_own, b_next, sets):
         empty = jnp.zeros((2, 2, BS, BS), jnp.float32)
-        return (empty, *first_steps(high_plane, b_own, sets[2], sets[3]))
+        a_own, a_sent = sets[:2]
+        a_far, *b_same = first_steps(high_plane, b_own, a_own, a_sent, (1, 2, 3))
+        return (empty, offered(a_own, a_far), a_far, *b_same)
 
     b_own = packed_b(b_blocks, b_cols, b_count.T)
     b_next_low = go(b_own, goal=back, takes_part=high_plane)
@@ -259,7 +276,7 @@
     return lax.cond(
         on_low,
         lambda o, b, n, sets: o,
-        lambda o, b, n, sets: last_steps(high_plane, b, n, sets)[0],
+        lambda o, b, n, sets: last_steps(high_plane, b, n, sets[0], sets[1], sets[2:])[0],
         out, b_own, b_next_high, sets_high,
     )
 

time: 78.8 us -> 77.2 us (0.980)
  the two profiles are of different devices: /device:TPU:577 before, /device:TPU:1 now
where the time goes in v4:
time: 77.2 us; the launch traced here: 76.6 us
  starting transfers between devices  50.6 us (66%)
  waiting for transfers between devices  13.6 us (18%)
  Pallas kernels  6.97 us (9%)
  other arithmetic  3.03 us (4%)
  local copies, waits for them, and re-layouts  2.08 us (3%)
    ppermute x10, starting transfers between devices, moved(): return lax.ppermute(x, ('row', 'col'), pairs)  44.1 us
    ppermute x10, waiting for transfers between devices, moved(): return lax.ppermute(x, ('row', 'col'), pairs)  13.6 us
    all_to_all x1, starting transfers between devices, last_steps(): mine = lax.all_to_all(offer, 'col', 0, 0, axis_index_groups=quads)  6.5 us
    pallas_call x2, Pallas kernels, summed(): pl.pallas_call(body, out_shape=jax.ShapeDtypeStruct((2, 2, BS, BS), jnp.f...  3.78 us
    unnamed x8, local copies, waits for them, and re-layouts  2.05 us
    pallas_call x1, Pallas kernels, packed_a(): pl.pallas_call(pack_a, out_shape=(PIECE,) * 2, in_specs=[SMEM, SMEM, SMEM...  2.01 us
    select_n x1, other arithmetic, offered(): return jnp.where(slot <= in_quad, a_own[None], a_far[None])  1.86 us
  transfers between devices with their start and end apart: 11, of which 4 were waited for; matrix products, arithmetic and copies ran while one was open for 4% of the time, Pallas kernels for 8%

profile of v4, /device:TPU:1, one launch (start us, length us, event | category | flops | bytes accessed | tf_op | source)
XLA Modules:
  0.0 76.6 jit_solution(9304654485736949326)
XLA Ops:
  0.0 1.2 %pack_b.1 = s16[528,128]{1,0:T(8,128)(2,1)S(1)} custom-call(s32[2,4]{1,0:T(2,128)} %which.1, s32[1,2]{1,0:T(1,128)} %bitcast.16, bf16[2,4,128,128]{3,2,1,0:T(8,128)(2,1)} %blocks.1), custom_call_target="tpu_custom_call" | custom-call | flops 2000000 | bytes 400000 | tf_op jit(solution)/shard_map/pack_b/pallas_call | solution.py:84
  1.2 1.3 %collective-permute-start.22 = (s16[528,128]{1,0:T(8,128)(2,1)S(1)}, s16[528,128]{1,0:T(8,128)(2,1)S(1)}, u32[]{:S(2)}, u32[]{:S(2)}) collective-permute-start(s16[528,128]{1,0:T(8,128)(2,1)S(1)} %pack_b.1), channel_id=1, source_target_pairs={{16,0},{17,1},{18,2},{19,3},{20,4},{21,5},{22,6},{23,7},{24,8},{25... | collective-permute-start | bytes 405512 | tf_op jit(solution)/shard_map/ppermute | solution.py:187
  2.5 0.0 copy-start.1
  2.5 0.0 copy-start.2
  2.5 0.7 copy-done.1
  3.2 0.0 copy-done.2
  3.2 33.9 %conditional.5 = (s16[528,128]{1,0:T(8,128)(2,1)S(1)}, s16[528,128]{1,0:T(8,128)(2,1)}, s16[528,128]{1,0:T(8,128)(2,1)}, s16[528,128]{1,0:T(8,128)(2,1)}, s16[528,128]{1,0:T(8,128)(2,1)}) conditional(s32[]{:T(128)} %convert_element_type.11, (s32[4,1]{0,1:T(1,128)S(1)}, bf16[4,4,128,128]{3,2,1,0:T(8,128)(2,1)}, s32[4,4]{1,0:T(4,128)S(1)}, ...), branch_computations={%region_0.1_spmd, %region_1.4_spmd} | conditional | flops 4000002 | bytes 2962926 | solution.py:273
  3.2 2.0 %pack_a.3 = (s16[528,128]{1,0:T(8,128)(2,1)S(1)}, s16[528,128]{1,0:T(8,128)(2,1)}) custom-call(s32[4,4]{1,0:T(4,128)S(1)} %get-tuple-element.102.which, s32[1,4]{1,0:T(1,128)S(1)} %bitcast.15, s32[1]{0:T(128)} %get-tuple-element.104.chip, bf16[4,4,128,128]{3,2,1,0:T(8,128)(2,1)} %get-tuple-element.107.blocks), custom_call_target="tpu_custom_call" | custom-call | flops 4000000 | bytes 800000 | tf_op jit(solution)/shard_map/cond/branch_1_fun/pack_a/pallas_call | solution.py:95
  5.2 11.3 %collective-permute-start.6 = (s16[528,128]{1,0:T(8,128)(2,1)}, s16[528,128]{1,0:T(8,128)(2,1)}, u32[]{:S(2)}, u32[]{:S(2)}) collective-permute-start(s16[528,128]{1,0:T(8,128)(2,1)} %get-tuple-element.109), channel_id=1, source_target_pairs={{0,8},{1,9},{2,10},{3,11},{4,12},{5,13},{6,14},{7,15},{8,0},{9,1},... | collective-permute-start | bytes 405512 | tf_op jit(solution)/shard_map/cond/branch_1_fun/ppermute | solution.py:187
  16.5 20.6 %conditional = (s16[528,128]{1,0:T(8,128)(2,1)}, s16[528,128]{1,0:T(8,128)(2,1)}, s16[528,128]{1,0:T(8,128)(2,1)}) conditional(s32[]{:T(128)} %convert_element_type.3, s16[528,128]{1,0:T(8,128)(2,1)S(1)} %get-tuple-element.111, s16[528,128]{1,0:T(8,128)(2,1)S(1)} %get-tuple-element.111), branch_computations={%region_2.2_spmd, %region_3.3_spmd} | conditional | bytes 1622160 | solution.py:226
  16.5 7.3 %collective-permute-start = (s16[528,128]{1,0:T(8,128)(2,1)S(1)}, s16[528,128]{1,0:T(8,128)(2,1)}, u32[]{:S(2)}, u32[]{:S(2)}) collective-permute-start(s16[528,128]{1,0:T(8,128)(2,1)S(1)} %param.1), channel_id=1, source_target_pairs={{1,993},{3,995},{5,997},{7,999},{9,1001},{11,1003},{13,1005},{15,1... | collective-permute-start | bytes 405512 | tf_op jit(solution)/shard_map/cond/branch_1_fun/cond/branch_0_fun/ppermute | solution.py:187
  23.8 2.4 %collective-permute-start.1 = (s16[528,128]{1,0:T(8,128)(2,1)S(1)}, s16[528,128]{1,0:T(8,128)(2,1)}, u32[]{:S(2)}, u32[]{:S(2)}) collective-permute-start(s16[528,128]{1,0:T(8,128)(2,1)S(1)} %param.1), channel_id=1, source_target_pairs={{1,961},{3,963},{5,965},{7,967},{9,969},{11,971},{13,973},{15,975}... | collective-permute-start | bytes 405512 | tf_op jit(solution)/shard_map/cond/branch_1_fun/cond/branch_0_fun/ppermute | solution.py:187
  26.3 3.3 %collective-permute-start.2 = (s16[528,128]{1,0:T(8,128)(2,1)S(1)}, s16[528,128]{1,0:T(8,128)(2,1)}, u32[]{:S(2)}, u32[]{:S(2)}) collective-permute-start(s16[528,128]{1,0:T(8,128)(2,1)S(1)} %param.1), channel_id=1, source_target_pairs={{1,929},{3,931},{5,933},{7,935},{9,937},{11,939},{13,941},{15,943}... | collective-permute-start | bytes 405512 | tf_op jit(solution)/shard_map/cond/branch_1_fun/cond/branch_0_fun/ppermute | solution.py:187
  29.6 0.0 collective-permute-done
  29.6 4.4 %collective-permute-done.1 = s16[528,128]{1,0:T(8,128)(2,1)} collective-permute-done((s16[528,128]{1,0:T(8,128)(2,1)S(1)}, s16[528,128]{1,0:T(8,128)(2,1)}, u32[]{:S(2)}, u32[]{:S(2)}) %collective-permute-start.1) | collective-permute-done | bytes 135200 | tf_op jit(solution)/shard_map/cond/branch_1_fun/cond/branch_0_fun/ppermute | solution.py:187
  34.0 3.1 %collective-permute-done.2 = s16[528,128]{1,0:T(8,128)(2,1)} collective-permute-done((s16[528,128]{1,0:T(8,128)(2,1)S(1)}, s16[528,128]{1,0:T(8,128)(2,1)}, u32[]{:S(2)}, u32[]{:S(2)}) %collective-permute-start.2) | collective-permute-done | bytes 135200 | tf_op jit(solution)/shard_map/cond/branch_1_fun/cond/branch_0_fun/ppermute | solution.py:187
  37.1 0.0 collective-permute-done.6
  37.1 1.3 %collective-permute-start.23 = (s16[528,128]{1,0:T(8,128)(2,1)S(1)}, s16[528,128]{1,0:T(8,128)(2,1)S(1)}, u32[]{:S(2)}, u32[]{:S(2)}) collective-permute-start(s16[528,128]{1,0:T(8,128)(2,1)S(1)} %pack_b.1), channel_id=1, source_target_pairs={{0,1008},{1,1009},{2,1010},{3,1011},{4,1012},{5,1013},{6,1014},{7,... | collective-permute-start | bytes 405512 | tf_op jit(solution)/shard_map/ppermute | solution.py:187
  38.4 0.1 pad_add_fusion
  38.5 0.0 collective-permute-done.22
  38.5 0.0 copy-start.3
  38.5 0.7 copy-done.3
  39.2 36.6 %conditional.6 = (s16[4,528,128]{2,1,0:T(8,128)(2,1)}, s16[528,128]{1,0:T(8,128)(2,1)S(1)}, s16[528,128]{1,0:T(8,128)(2,1)}, s16[528,128]{1,0:T(8,128)(2,1)}, s1...) conditional(s32[]{:T(128)} %convert_element_type.11, (s32[]{:T(128)}, s32[4,1,1]{0,2,1:T(1,128)S(1)}, ...), branch_computations={%region_4.7_spmd, %region_7.8_spmd} | conditional | flops 1600540672 | bytes 12569716 | solution.py:275
  39.2 1.9 %broadcast_select_fusion.1 = s16[4,528,128]{2,1,0:T(8,128)(2,1)} fusion(pred[4]{0:T(512)(128)(4,1)S(1)} %compare_bitcast_fusion.1, s16[528,128]{1,0:T(8,128)(2,1)S(1)} %get-tuple-element.130, s16[528,128]{1,0:T(8,128)(2,1)} %get-tuple-element.128), kind=kLoop, calls=%fused_computation.2 | loop fusion | flops 270336 | bytes 811012 | tf_op jit(solution)/shard_map/cond/branch_1_fun/jit(_where)/select_n | solution.py:236
  41.1 6.5 %all-to-all-start = ((s16[4,528,128]{2,1,0:T(8,128)(2,1)}), s16[4,528,128]{2,1,0:T(8,128)(2,1)S(1)}, u32[]{:S(2)}, u32[]{:S(2)}) async-start(s16[4,528,128]{2,1,0:T(8,128)(2,1)} %broadcast_select_fusion.1), calls=%async_computation | async-start | bytes 1081344 | tf_op jit(solution)/shard_map/cond/branch_1_fun/all_to_all | solution.py:239
  47.6 8.4 %collective-permute-start.14 = (s16[528,128]{1,0:T(8,128)(2,1)S(1)}, s16[528,128]{1,0:T(8,128)(2,1)}, u32[]{:S(2)}, u32[]{:S(2)}) collective-permute-start(s16[528,128]{1,0:T(8,128)(2,1)S(1)} %get-tuple-element.131.c0), channel_id=1, source_target_pairs={{0,992},{1,993},{2,994},{3,995},{4,996},{5,997},{6,998},{7,999},{8... | collective-permute-start | bytes 405512 | tf_op jit(solution)/shard_map/cond/branch_1_fun/ppermute | solution.py:187
  55.9 2.3 %collective-permute-start.15 = (s16[528,128]{1,0:T(8,128)(2,1)S(1)}, s16[528,128]{1,0:T(8,128)(2,1)}, u32[]{:S(2)}, u32[]{:S(2)}) collective-permute-start(s16[528,128]{1,0:T(8,128)(2,1)S(1)} %get-tuple-element.131.c0), channel_id=1, source_target_pairs={{0,960},{1,961},{2,962},{3,963},{4,964},{5,965},{6,966},{7,967},{8... | collective-permute-start | bytes 405512 | tf_op jit(solution)/shard_map/cond/branch_1_fun/ppermute | solution.py:187
  58.2 3.3 %collective-permute-start.16 = (s16[528,128]{1,0:T(8,128)(2,1)S(1)}, s16[528,128]{1,0:T(8,128)(2,1)}, u32[]{:S(2)}, u32[]{:S(2)}) collective-permute-start(s16[528,128]{1,0:T(8,128)(2,1)S(1)} %get-tuple-element.131.c0), channel_id=1, source_target_pairs={{0,928},{1,929},{2,930},{3,931},{4,932},{5,933},{6,934},{7,935},{8... | collective-permute-start | bytes 405512 | tf_op jit(solution)/shard_map/cond/branch_1_fun/ppermute | solution.py:187
  61.6 0.0 collective-permute-done.14.c1
  61.6 3.5 %collective-permute-done.15.c2 = s16[528,128]{1,0:T(8,128)(2,1)} collective-permute-done((s16[528,128]{1,0:T(8,128)(2,1)S(1)}, s16[528,128]{1,0:T(8,128)(2,1)}, u32[]{:S(2)}, u32[]{:S(2)}) %collective-permute-start.15) | collective-permute-done | bytes 135200 | tf_op jit(solution)/shard_map/cond/branch_1_fun/ppermute | solution.py:187
  65.1 2.6 %collective-permute-done.16.c3 = s16[528,128]{1,0:T(8,128)(2,1)} collective-permute-done((s16[528,128]{1,0:T(8,128)(2,1)S(1)}, s16[528,128]{1,0:T(8,128)(2,1)}, u32[]{:S(2)}, u32[]{:S(2)}) %collective-permute-start.16) | collective-permute-done | bytes 135200 | tf_op jit(solution)/shard_map/cond/branch_1_fun/ppermute | solution.py:187
  67.7 0.0 all-to-all-done.mine
  67.7 1.1 %broadcast_select_fusion.2 = s16[4,528,128]{2,1,0:T(8,128)(2,1)S(1)} fusion(s16[4,528,128]{2,1,0:T(8,128)(2,1)S(1)} %all-to-all-done.mine, pred[4]{0:T(512)(128)(4,1)S(1)} %and_bitcast_fusion, s16[528,128]{1,0:T(8,128)(2,1)} %get-tuple-element.128), kind=kLoop, calls=%fused_computation.3 | loop fusion | flops 270336 | bytes 1216516 | tf_op jit(solution)/shard_map/cond/branch_1_fun/jit(_where)/select_n | solution.py:242
  68.8 3.2 %collective-permute-start.17 = (s16[4,528,128]{2,1,0:T(8,128)(2,1)S(1)}, s16[4,528,128]{2,1,0:T(8,128)(2,1)}, u32[]{:S(2)}, u32[]{:S(2)}) collective-permute-start(s16[4,528,128]{2,1,0:T(8,128)(2,1)S(1)} %broadcast_select_fusion.2), channel_id=1, source_target_pairs={{0,1},{1,0},{2,3},{3,2},{4,5},{5,4},{6,7},{7,6},{8,9},{9,8},{10,11... | collective-permute-start | bytes 1622024 | tf_op jit(solution)/shard_map/cond/branch_1_fun/ppermute | solution.py:187
  72.0 1.8 %even.2.begun = f32[2,2,128,128]{3,2,1,0:T(8,128)S(1)} custom-call(s32[2]{0:T(128)S(1)} %get-tuple-element.133.spot, s16[4,528,128]{2,1,0:T(8,128)(2,1)S(1)} %all-to-all-done.mine, s16[528,128]{1,0:T(8,128)(2,1)S(1)} %get-tuple-element.135.b0, s16[528,128]{1,0:T(8,128)(2,1)} %get-tuple-element.136.b1, s16[528,128]{1,0:T(8,128)(2,1)} %get-tuple-element.137.b2, ...), custom_call_target="tpu_custom_call" | custom-call | flops 800000000 | bytes 2500000 | tf_op jit(solution)/shard_map/cond/branch_1_fun/even/pallas_call | solution.py:169
  73.8 0.0 collective-permute-done.17.others
  73.9 2.0 %odd.2 = f32[2,2,128,128]{3,2,1,0:T(8,128)S(1)} custom-call(s32[2]{0:T(128)S(1)} %get-tuple-element.133.spot, s32[2,2]{1,0:T(2,128)S(1)} %get-tuple-element.134.keep, f32[2,2,128,128]{3,2,1,0:T(8,128)S(1)} %even.2.begun, s16[4,528,128]{2,1,0:T(8,128)(2,1)} %collective-permute-done.17.others, s16[528,128]{1,0:T(8,128)(2,1)S(1)} %get-tuple-element.131.c0, ...), custom_call_target="tpu_custom_call" | custom-call | flops 800000000 | bytes 2500000 | tf_op jit(solution)/shard_map/cond/branch_1_fun/odd/pallas_call | solution.py:169
  75.9 0.0 collective-permute-done.23
  75.9 0.0 copy-start
  75.9 0.7 copy-done
  (7 shorter events, 0.1 us)
Async XLA Ops:
  1.2 37.3 %collective-permute-start.22 = (s16[528,128]{1,0:T(8,128)(2,1)S(1)}, s16[528,128]{1,0:T(8,128)(2,1)S(1)}, u32[]{:S(2)}, u32[]{:S(2)}) collective-permute-start(s16[528,128]{1,0:T(8,128)(2,1)S(1)} %pack_b.1), channel_id=1, source_target_pairs={{16,0},{17,1},{18,2},{19,3},{20,4},{21,5},{22,6},{23,7},{24,8},{25... | collective-permute-start | bytes 405512 | tf_op jit(solution)/shard_map/ppermute | solution.py:187
  2.5 0.7 copy-start.1
  2.5 0.7 copy-start.2
  5.2 31.9 %collective-permute-start.6 = (s16[528,128]{1,0:T(8,128)(2,1)}, s16[528,128]{1,0:T(8,128)(2,1)}, u32[]{:S(2)}, u32[]{:S(2)}) collective-permute-start(s16[528,128]{1,0:T(8,128)(2,1)} %get-tuple-element.109), channel_id=1, source_target_pairs={{0,8},{1,9},{2,10},{3,11},{4,12},{5,13},{6,14},{7,15},{8,0},{9,1},... | collective-permute-start | bytes 405512 | tf_op jit(solution)/shard_map/cond/branch_1_fun/ppermute | solution.py:187
  16.5 13.0 %collective-permute-start = (s16[528,128]{1,0:T(8,128)(2,1)S(1)}, s16[528,128]{1,0:T(8,128)(2,1)}, u32[]{:S(2)}, u32[]{:S(2)}) collective-permute-start(s16[528,128]{1,0:T(8,128)(2,1)S(1)} %param.1), channel_id=1, source_target_pairs={{1,993},{3,995},{5,997},{7,999},{9,1001},{11,1003},{13,1005},{15,1... | collective-permute-start | bytes 405512 | tf_op jit(solution)/shard_map/cond/branch_1_fun/cond/branch_0_fun/ppermute | solution.py:187
  23.8 10.2 %collective-permute-start.1 = (s16[528,128]{1,0:T(8,128)(2,1)S(1)}, s16[528,128]{1,0:T(8,128)(2,1)}, u32[]{:S(2)}, u32[]{:S(2)}) collective-permute-start(s16[528,128]{1,0:T(8,128)(2,1)S(1)} %param.1), channel_id=1, source_target_pairs={{1,961},{3,963},{5,965},{7,967},{9,969},{11,971},{13,973},{15,975}... | collective-permute-start | bytes 405512 | tf_op jit(solution)/shard_map/cond/branch_1_fun/cond/branch_0_fun/ppermute | solution.py:187
  26.3 10.8 %collective-permute-start.2 = (s16[528,128]{1,0:T(8,128)(2,1)S(1)}, s16[528,128]{1,0:T(8,128)(2,1)}, u32[]{:S(2)}, u32[]{:S(2)}) collective-permute-start(s16[528,128]{1,0:T(8,128)(2,1)S(1)} %param.1), channel_id=1, source_target_pairs={{1,929},{3,931},{5,933},{7,935},{9,937},{11,939},{13,941},{15,943}... | collective-permute-start | bytes 405512 | tf_op jit(solution)/shard_map/cond/branch_1_fun/cond/branch_0_fun/ppermute | solution.py:187
  37.1 38.7 %collective-permute-start.23 = (s16[528,128]{1,0:T(8,128)(2,1)S(1)}, s16[528,128]{1,0:T(8,128)(2,1)S(1)}, u32[]{:S(2)}, u32[]{:S(2)}) collective-permute-start(s16[528,128]{1,0:T(8,128)(2,1)S(1)} %pack_b.1), channel_id=1, source_target_pairs={{0,1008},{1,1009},{2,1010},{3,1011},{4,1012},{5,1013},{6,1014},{7,... | collective-permute-start | bytes 405512 | tf_op jit(solution)/shard_map/ppermute | solution.py:187
  38.5 0.7 copy-start.3
  41.1 26.6 %all-to-all-start = ((s16[4,528,128]{2,1,0:T(8,128)(2,1)}), s16[4,528,128]{2,1,0:T(8,128)(2,1)S(1)}, u32[]{:S(2)}, u32[]{:S(2)}) async-start(s16[4,528,128]{2,1,0:T(8,128)(2,1)} %broadcast_select_fusion.1), calls=%async_computation | async-start | bytes 1081344 | tf_op jit(solution)/shard_map/cond/branch_1_fun/all_to_all | solution.py:239
  47.6 14.0 %collective-permute-start.14 = (s16[528,128]{1,0:T(8,128)(2,1)S(1)}, s16[528,128]{1,0:T(8,128)(2,1)}, u32[]{:S(2)}, u32[]{:S(2)}) collective-permute-start(s16[528,128]{1,0:T(8,128)(2,1)S(1)} %get-tuple-element.131.c0), channel_id=1, source_target_pairs={{0,992},{1,993},{2,994},{3,995},{4,996},{5,997},{6,998},{7,999},{8... | collective-permute-start | bytes 405512 | tf_op jit(solution)/shard_map/cond/branch_1_fun/ppermute | solution.py:187
  55.9 9.2 %collective-permute-start.15 = (s16[528,128]{1,0:T(8,128)(2,1)S(1)}, s16[528,128]{1,0:T(8,128)(2,1)}, u32[]{:S(2)}, u32[]{:S(2)}) collective-permute-start(s16[528,128]{1,0:T(8,128)(2,1)S(1)} %get-tuple-element.131.c0), channel_id=1, source_target_pairs={{0,960},{1,961},{2,962},{3,963},{4,964},{5,965},{6,966},{7,967},{8... | collective-permute-start | bytes 405512 | tf_op jit(solution)/shard_map/cond/branch_1_fun/ppermute | solution.py:187
  58.2 9.4 %collective-permute-start.16 = (s16[528,128]{1,0:T(8,128)(2,1)S(1)}, s16[528,128]{1,0:T(8,128)(2,1)}, u32[]{:S(2)}, u32[]{:S(2)}) collective-permute-start(s16[528,128]{1,0:T(8,128)(2,1)S(1)} %get-tuple-element.131.c0), channel_id=1, source_target_pairs={{0,928},{1,929},{2,930},{3,931},{4,932},{5,933},{6,934},{7,935},{8... | collective-permute-start | bytes 405512 | tf_op jit(solution)/shard_map/cond/branch_1_fun/ppermute | solution.py:187
  68.8 5.1 %collective-permute-start.17 = (s16[4,528,128]{2,1,0:T(8,128)(2,1)S(1)}, s16[4,528,128]{2,1,0:T(8,128)(2,1)}, u32[]{:S(2)}, u32[]{:S(2)}) collective-permute-start(s16[4,528,128]{2,1,0:T(8,128)(2,1)S(1)} %broadcast_select_fusion.2), channel_id=1, source_target_pairs={{0,1},{1,0},{2,3},{3,2},{4,5},{5,4},{6,7},{7,6},{8,9},{9,8},{10,11... | collective-permute-start | bytes 1622024 | tf_op jit(solution)/shard_map/cond/branch_1_fun/ppermute | solution.py:187
  75.9 0.7 copy-start

commit v5 on v4

--- a/solution.py
+++ b/solution.py
@@ -80,26 +80,20 @@
 PIECE = jax.ShapeDtypeStruct((ROWS, BS), jnp.int16)
 
 
-def packed_b(blocks, which, many):
+def pack_all(b_which, b_many, a_which, a_many, chip, b_blocks, a_blocks, b_own, a_own, a_sent):
+    pack_b(b_which, b_many, b_blocks, b_own)
+    pack_a(a_which, a_many, chip, a_blocks, a_own, a_sent)
+
+
+def packed(*inputs):
     return pl.pallas_call(
-        pack_b,
-        out_shape=PIECE,
-        in_specs=[SMEM, SMEM, VMEM],
-        out_specs=VMEM,
-        name="pack_b",
-        cost_estimate=pl.CostEstimate(flops=2_000_000, bytes_accessed=400_000, transcendentals=0),
-    )(which, many, blocks)
-
-
-def packed_a(blocks, which, many, chip):
-    return pl.pallas_call(
-        pack_a,
-        out_shape=(PIECE,) * 2,
-        in_specs=[SMEM, SMEM, SMEM, VMEM],
-        out_specs=(VMEM,) * 2,
-        name="pack_a",
-        cost_estimate=pl.CostEstimate(flops=4_000_000, bytes_accessed=800_000, transcendentals=0),
-    )(which, many, chip, blocks)
+        pack_all,
+        out_shape=(PIECE,) * 3,
+        in_specs=[SMEM] * 5 + [VMEM] * 2,
+        out_specs=(VMEM,) * 3,
+        name="pack_all",
+        cost_estimate=pl.CostEstimate(flops=6_000_000, bytes_accessed=1_200_000, transcendentals=0),
+    )(*inputs)
 
 
 def two_parts(x):
@@ -225,9 +219,6 @@
 
         return lax.cond(core == 0, by_core(0), by_core(1), b_own)
 
-    def packed(b_own):
-        return packed_a(after(a_blocks, b_own), a_rows, a_count.T, chip_at)
-
     def first_steps(plane, b_own, a_own, a_sent, steps):
         a_far = go(a_sent, goal=lambda p, q: (p, q ^ 8), takes_part=plane)
         return (a_far, *own_spread(plane, after(b_own, a_own), steps))
@@ -235,48 +226,46 @@
     def offered(a_own, a_far):
         return jnp.where(slot <= in_quad, a_own[None], a_far[None])
 
-    def last_steps(plane, b_own, b_next, offer, a_far, b_same):
+    def last_steps(plane, b_own, b_next, offer, a_far, b_same, fills):
         mine = lax.all_to_all(offer, "col", 0, 0, axis_index_groups=quads)
         b_other = [spread(b_next, t, plane) for t in (1, 2, 3)]
         own_slot = jnp.logical_and(slot == in_quad, core == 0)
-        given = jnp.where(own_slot, a_far[None], after(mine, b_other))
+        filler = b_other[0] ^ 1 if fills else b_other[0]
+        given = jnp.where(own_slot, a_far[None], after(mine, (b_other, filler)))
         others = go(given, goal=lambda p, q: (p, q ^ 1), takes_part=plane)
         begun = summed(even, [spot], mine, b_own, *b_same)
         out = summed(odd, [spot, c_keep], begun, others, b_next, *b_other)
-        return out, others, b_other
+        return out, others, b_other, filler
 
     def blank():
         return jnp.zeros(PIECE.shape, PIECE.dtype)
 
-    def open_low(b_own):
-        a_own, a_sent = packed(b_own)
-        return (a_own, *first_steps(low_plane, b_own, a_own, a_sent, (1, 2, 3)))
-
-    def open_high(b_own):
-        a_own, a_sent = packed(b_own)
-        return (a_own, a_sent, blank(), blank(), blank())
-
-    def close_low(b_own, b_next, sets):
-        a_own, a_far, *b_same = sets
+    def open_low(b_own, a_own, a_sent):
+        return first_steps(low_plane, b_own, a_own, a_sent, (1, 2, 3))
+
+    def open_high(b_own, a_own, a_sent):
+        return tuple(blank() for _ in range(4))
+
+    def close_low(b_own, b_next, a_own, a_sent, sets):
+        a_far, *b_same = sets
         offer = offered(a_own, a_far)
-        out, others, b_other = last_steps(low_plane, b_own, b_next, offer, a_far, b_same)
-        return (out, others, blank(), *b_other)
-
-    def middle_high(b_own, b_next, sets):
+        out, others, b_other, filler = last_steps(low_plane, b_own, b_next, offer, a_far, b_same, True)
+        return (out, others, filler, *b_other)
+
+    def middle_high(b_own, b_next, a_own, a_sent, sets):
         empty = jnp.zeros((2, 2, BS, BS), jnp.float32)
-        a_own, a_sent = sets[:2]
         a_far, *b_same = first_steps(high_plane, b_own, a_own, a_sent, (1, 2, 3))
         return (empty, offered(a_own, a_far), a_far, *b_same)
 
-    b_own = packed_b(b_blocks, b_cols, b_count.T)
+    b_own, a_own, a_sent = packed(b_cols, b_count.T, a_rows, a_count.T, chip_at, b_blocks, a_blocks)
     b_next_low = go(b_own, goal=back, takes_part=high_plane)
-    sets_low = lax.cond(on_low, open_low, open_high, b_own)
+    sets_low = lax.cond(on_low, open_low, open_high, b_own, a_own, a_sent)
     b_next_high = go(after(b_own, sets_low[0]), goal=back, takes_part=low_plane)
-    out, *sets_high = lax.cond(on_low, close_low, middle_high, b_own, b_next_low, sets_low)
+    out, *sets_high = lax.cond(on_low, close_low, middle_high, b_own, b_next_low, a_own, a_sent, sets_low)
     return lax.cond(
         on_low,
         lambda o, b, n, sets: o,
-        lambda o, b, n, sets: last_steps(high_plane, b, n, sets[0], sets[1], sets[2:])[0],
+        lambda o, b, n, sets: last_steps(high_plane, b, n, sets[0], sets[1], sets[2:], False)[0],
         out, b_own, b_next_high, sets_high,
     )
 

time: 77.2 us -> 74.4 us (0.964)
  Pallas kernels: 6.97 us -> 5.38 us
  waiting for transfers between devices: 13.6 us -> 12.3 us
  other arithmetic: 3.03 us -> 3.97 us
    pallas_call x2 -> x1, Pallas kernels: 3.19 us -> 1.59 us  [packed(): pl.pallas_call(pack_all, out_shape=(PIECE,) * 3, in_specs=[SMEM] * 5 + [V...]
    ppermute x10, waiting for transfers between devices: 13.6 us -> 12.3 us  [moved(): return lax.ppermute(x, ('row', 'col'), pairs)]
    xor x0 -> x1, other arithmetic: none -> 0.94 us  [last_steps(): filler = b_other[0] ^ 1 if fills else b_other[0]]
    unnamed x8 -> x4, local copies, waits for them, and re-layouts: 2.05 us -> 1.37 us
  transfers between devices with their start and end apart: 11 -> 11, of which waited for: 4 -> 4; matrix products, arithmetic and copies ran while one was open for 4% -> 5% of each run, Pallas kernels for 8% -> 5%
where the time goes in v5:
time: 74.4 us; the launch traced here: 73.9 us
  starting transfers between devices  50.6 us (68%)
  waiting for transfers between devices  12.3 us (17%)
  Pallas kernels  5.38 us (7%)
  other arithmetic  3.97 us (5%)
  local copies, waits for them, and re-layouts  1.38 us (2%)
    ppermute x10, starting transfers between devices, moved(): return lax.ppermute(x, ('row', 'col'), pairs)  44.1 us
    ppermute x10, waiting for transfers between devices, moved(): return lax.ppermute(x, ('row', 'col'), pairs)  12.3 us
    all_to_all x1, starting transfers between devices, last_steps(): mine = lax.all_to_all(offer, 'col', 0, 0, axis_index_groups=quads)  6.5 us
    pallas_call x2, Pallas kernels, summed(): pl.pallas_call(body, out_shape=jax.ShapeDtypeStruct((2, 2, BS, BS), jnp.f...  3.79 us
    select_n x1, other arithmetic, offered(): return jnp.where(slot <= in_quad, a_own[None], a_far[None])  1.86 us
    pallas_call x1, Pallas kernels, packed(): pl.pallas_call(pack_all, out_shape=(PIECE,) * 3, in_specs=[SMEM] * 5 + [V...  1.59 us
  transfers between devices with their start and end apart: 11, of which 4 were waited for; matrix products, arithmetic and copies ran while one was open for 5% of the time, Pallas kernels for 5%

profile of v5, /device:TPU:1, one launch (start us, length us, event | category | flops | bytes accessed | tf_op | source)
XLA Modules:
  0.0 73.9 jit_solution(2986265515125510149)
XLA Ops:
  0.0 1.6 %pack_all.1 = (s16[528,128]{1,0:T(8,128)(2,1)S(1)}, s16[528,128]{1,0:T(8,128)(2,1)S(1)}, s16[528,128]{1,0:T(8,128)(2,1)S(1)}) custom-call(s32[2,4]{1,0:T(2,128)} %b_which.1, s32[1,2]{1,0:T(1,128)} %bitcast.13, s32[4,4]{1,0:T(4,128)} %a_which.1, s32[1,4]{1,0:T(1,128)} %bitcast.14, s32[1]{0:T(128)} %bitcast.6.chip, bf16[2,4,128,128]{3,2,1,0:T(8,128)(2,1)} %b_blocks.1, ...), custom_call_target="tpu_custom_call" | custom-call | flops 6000000 | bytes 1200000 | tf_op jit(solution)/shard_map/pack_all/pallas_call | solution.py:89
  1.6 1.3 %collective-permute-start.22 = (s16[528,128]{1,0:T(8,128)(2,1)S(1)}, s16[528,128]{1,0:T(8,128)(2,1)S(1)}, u32[]{:S(2)}, u32[]{:S(2)}) collective-permute-start(s16[528,128]{1,0:T(8,128)(2,1)S(1)} %get-tuple-element.151), channel_id=1, source_target_pairs={{16,0},{17,1},{18,2},{19,3},{20,4},{21,5},{22,6},{23,7},{24,8},{25... | collective-permute-start | bytes 405512 | tf_op jit(solution)/shard_map/ppermute | solution.py:181
  2.9 31.9 %conditional.5 = (s16[528,128]{1,0:T(8,128)(2,1)}, s16[528,128]{1,0:T(8,128)(2,1)}, s16[528,128]{1,0:T(8,128)(2,1)}, s16[528,128]{1,0:T(8,128)(2,1)}) conditional(s32[]{:T(128)} %convert_element_type.11, () %tuple.53, (s16[528,128]{1,0:T(8,128)(2,1)S(1)}, s32[]{:T(128)}, s16[528,128]{1,0:T(8,128)(2,1)S(1)}) %tuple.54), branch_computations={%region_0.1_spmd, %region_1.4_spmd} | conditional | flops 2 | bytes 2162918 | solution.py:262
  2.9 11.3 %collective-permute-start.6 = (s16[528,128]{1,0:T(8,128)(2,1)S(1)}, s16[528,128]{1,0:T(8,128)(2,1)}, u32[]{:S(2)}, u32[]{:S(2)}) collective-permute-start(s16[528,128]{1,0:T(8,128)(2,1)S(1)} %get-tuple-element.82), channel_id=1, source_target_pairs={{0,8},{1,9},{2,10},{3,11},{4,12},{5,13},{6,14},{7,15},{8,0},{9,1},... | collective-permute-start | bytes 405512 | tf_op jit(solution)/shard_map/cond/branch_1_fun/ppermute | solution.py:181
  14.3 20.6 %conditional = (s16[528,128]{1,0:T(8,128)(2,1)}, s16[528,128]{1,0:T(8,128)(2,1)}, s16[528,128]{1,0:T(8,128)(2,1)}) conditional(s32[]{:T(128)} %convert_element_type.3, s16[528,128]{1,0:T(8,128)(2,1)S(1)} %get-tuple-element.84, s16[528,128]{1,0:T(8,128)(2,1)S(1)} %get-tuple-element.84), branch_computations={%region_2.2_spmd, %region_3.3_spmd} | conditional | bytes 1622160 | solution.py:220
  14.3 7.3 %collective-permute-start = (s16[528,128]{1,0:T(8,128)(2,1)S(1)}, s16[528,128]{1,0:T(8,128)(2,1)}, u32[]{:S(2)}, u32[]{:S(2)}) collective-permute-start(s16[528,128]{1,0:T(8,128)(2,1)S(1)} %param.1), channel_id=1, source_target_pairs={{1,993},{3,995},{5,997},{7,999},{9,1001},{11,1003},{13,1005},{15,1... | collective-permute-start | bytes 405512 | tf_op jit(solution)/shard_map/cond/branch_1_fun/cond/branch_0_fun/ppermute | solution.py:181
  21.6 2.4 %collective-permute-start.1 = (s16[528,128]{1,0:T(8,128)(2,1)S(1)}, s16[528,128]{1,0:T(8,128)(2,1)}, u32[]{:S(2)}, u32[]{:S(2)}) collective-permute-start(s16[528,128]{1,0:T(8,128)(2,1)S(1)} %param.1), channel_id=1, source_target_pairs={{1,961},{3,963},{5,965},{7,967},{9,969},{11,971},{13,973},{15,975}... | collective-permute-start | bytes 405512 | tf_op jit(solution)/shard_map/cond/branch_1_fun/cond/branch_0_fun/ppermute | solution.py:181
  24.0 3.3 %collective-permute-start.2 = (s16[528,128]{1,0:T(8,128)(2,1)S(1)}, s16[528,128]{1,0:T(8,128)(2,1)}, u32[]{:S(2)}, u32[]{:S(2)}) collective-permute-start(s16[528,128]{1,0:T(8,128)(2,1)S(1)} %param.1), channel_id=1, source_target_pairs={{1,929},{3,931},{5,933},{7,935},{9,937},{11,939},{13,941},{15,943}... | collective-permute-start | bytes 405512 | tf_op jit(solution)/shard_map/cond/branch_1_fun/cond/branch_0_fun/ppermute | solution.py:181
  27.3 0.0 collective-permute-done
  27.3 4.4 %collective-permute-done.1 = s16[528,128]{1,0:T(8,128)(2,1)} collective-permute-done((s16[528,128]{1,0:T(8,128)(2,1)S(1)}, s16[528,128]{1,0:T(8,128)(2,1)}, u32[]{:S(2)}, u32[]{:S(2)}) %collective-permute-start.1) | collective-permute-done | bytes 135200 | tf_op jit(solution)/shard_map/cond/branch_1_fun/cond/branch_0_fun/ppermute | solution.py:181
  31.8 3.1 %collective-permute-done.2 = s16[528,128]{1,0:T(8,128)(2,1)} collective-permute-done((s16[528,128]{1,0:T(8,128)(2,1)S(1)}, s16[528,128]{1,0:T(8,128)(2,1)}, u32[]{:S(2)}, u32[]{:S(2)}) %collective-permute-start.2) | collective-permute-done | bytes 135200 | tf_op jit(solution)/shard_map/cond/branch_1_fun/cond/branch_0_fun/ppermute | solution.py:181
  34.9 0.0 collective-permute-done.6
  34.9 1.3 %collective-permute-start.23 = (s16[528,128]{1,0:T(8,128)(2,1)S(1)}, s16[528,128]{1,0:T(8,128)(2,1)S(1)}, u32[]{:S(2)}, u32[]{:S(2)}) collective-permute-start(s16[528,128]{1,0:T(8,128)(2,1)S(1)} %get-tuple-element.151), channel_id=1, source_target_pairs={{0,1008},{1,1009},{2,1010},{3,1011},{4,1012},{5,1013},{6,1014},{7,... | collective-permute-start | bytes 405512 | tf_op jit(solution)/shard_map/ppermute | solution.py:181
  36.2 0.1 pad_add_fusion
  36.3 0.0 collective-permute-done.22
  36.3 0.0 copy-start.1
  36.3 0.7 copy-done.1
  37.0 36.2 %conditional.6 = (s16[4,528,128]{2,1,0:T(8,128)(2,1)}, s16[528,128]{1,0:T(8,128)(2,1)S(1)}, s16[528,128]{1,0:T(8,128)(2,1)}, s16[528,128]{1,0:T(8,128)(2,1)}, s1...) conditional(s32[]{:T(128)} %convert_element_type.11, (s32[]{:T(128)}, s32[4,1,1]{0,2,1:T(1,128)S(1)}, ...), branch_computations={%region_4.7_spmd, %region_7.8_spmd} | conditional | flops 1600608256 | bytes 12704882 | solution.py:264
  37.0 1.9 %broadcast_select_fusion.1 = s16[4,528,128]{2,1,0:T(8,128)(2,1)} fusion(pred[4]{0:T(512)(128)(4,1)S(1)} %compare_bitcast_fusion.1, s16[528,128]{1,0:T(8,128)(2,1)S(1)} %get-tuple-element.103, s16[528,128]{1,0:T(8,128)(2,1)} %get-tuple-element.101), kind=kLoop, calls=%fused_computation.2 | loop fusion | flops 270336 | bytes 811012 | tf_op jit(solution)/shard_map/cond/branch_1_fun/jit(_where)/select_n | solution.py:227
  38.8 6.5 %all-to-all-start = ((s16[4,528,128]{2,1,0:T(8,128)(2,1)}), s16[4,528,128]{2,1,0:T(8,128)(2,1)S(1)}, u32[]{:S(2)}, u32[]{:S(2)}) async-start(s16[4,528,128]{2,1,0:T(8,128)(2,1)} %broadcast_select_fusion.1), calls=%async_computation | async-start | bytes 1081344 | tf_op jit(solution)/shard_map/cond/branch_1_fun/all_to_all | solution.py:230
  45.3 7.9 %collective-permute-start.14 = (s16[528,128]{1,0:T(8,128)(2,1)S(1)}, s16[528,128]{1,0:T(8,128)(2,1)}, u32[]{:S(2)}, u32[]{:S(2)}) collective-permute-start(s16[528,128]{1,0:T(8,128)(2,1)S(1)} %get-tuple-element.104.c0), channel_id=1, source_target_pairs={{0,992},{1,993},{2,994},{3,995},{4,996},{5,997},{6,998},{7,999},{8... | collective-permute-start | bytes 405512 | tf_op jit(solution)/shard_map/cond/branch_1_fun/ppermute | solution.py:181
  53.2 2.4 %collective-permute-start.15 = (s16[528,128]{1,0:T(8,128)(2,1)S(1)}, s16[528,128]{1,0:T(8,128)(2,1)}, u32[]{:S(2)}, u32[]{:S(2)}) collective-permute-start(s16[528,128]{1,0:T(8,128)(2,1)S(1)} %get-tuple-element.104.c0), channel_id=1, source_target_pairs={{0,960},{1,961},{2,962},{3,963},{4,964},{5,965},{6,966},{7,967},{8... | collective-permute-start | bytes 405512 | tf_op jit(solution)/shard_map/cond/branch_1_fun/ppermute | solution.py:181
  55.7 3.3 %collective-permute-start.16 = (s16[528,128]{1,0:T(8,128)(2,1)S(1)}, s16[528,128]{1,0:T(8,128)(2,1)}, u32[]{:S(2)}, u32[]{:S(2)}) collective-permute-start(s16[528,128]{1,0:T(8,128)(2,1)S(1)} %get-tuple-element.104.c0), channel_id=1, source_target_pairs={{0,928},{1,929},{2,930},{3,931},{4,932},{5,933},{6,934},{7,935},{8... | collective-permute-start | bytes 405512 | tf_op jit(solution)/shard_map/cond/branch_1_fun/ppermute | solution.py:181
  59.0 0.0 collective-permute-done.14.c1
  59.0 0.9 %broadcast_xor_fusion = s16[528,128]{1,0:T(8,128)(2,1)S(1)} fusion(s16[528,128]{1,0:T(8,128)(2,1)} %collective-permute-done.14.c1), kind=kLoop, calls=%fused_computation.4 | loop fusion | flops 67584 | bytes 270336 | tf_op jit(solution)/shard_map/cond/branch_1_fun/xor | solution.py:233
  59.9 2.8 %collective-permute-done.15.c2 = s16[528,128]{1,0:T(8,128)(2,1)} collective-permute-done((s16[528,128]{1,0:T(8,128)(2,1)S(1)}, s16[528,128]{1,0:T(8,128)(2,1)}, u32[]{:S(2)}, u32[]{:S(2)}) %collective-permute-start.15) | collective-permute-done | bytes 135200 | tf_op jit(solution)/shard_map/cond/branch_1_fun/ppermute | solution.py:181
  62.7 2.0 %collective-permute-done.16.c3 = s16[528,128]{1,0:T(8,128)(2,1)} collective-permute-done((s16[528,128]{1,0:T(8,128)(2,1)S(1)}, s16[528,128]{1,0:T(8,128)(2,1)}, u32[]{:S(2)}, u32[]{:S(2)}) %collective-permute-start.16) | collective-permute-done | bytes 135200 | tf_op jit(solution)/shard_map/cond/branch_1_fun/ppermute | solution.py:181
  64.7 0.0 all-to-all-done.mine
  64.7 1.1 %broadcast_select_fusion.2 = s16[4,528,128]{2,1,0:T(8,128)(2,1)S(1)} fusion(s16[4,528,128]{2,1,0:T(8,128)(2,1)S(1)} %all-to-all-done.mine, pred[4]{0:T(512)(128)(4,1)S(1)} %and_bitcast_fusion, s16[528,128]{1,0:T(8,128)(2,1)} %get-tuple-element.101), kind=kLoop, calls=%fused_computation.3 | loop fusion | flops 270336 | bytes 1216516 | tf_op jit(solution)/shard_map/cond/branch_1_fun/jit(_where)/select_n | solution.py:234
  65.8 3.6 %collective-permute-start.17 = (s16[4,528,128]{2,1,0:T(8,128)(2,1)S(1)}, s16[4,528,128]{2,1,0:T(8,128)(2,1)}, u32[]{:S(2)}, u32[]{:S(2)}) collective-permute-start(s16[4,528,128]{2,1,0:T(8,128)(2,1)S(1)} %broadcast_select_fusion.2), channel_id=1, source_target_pairs={{0,1},{1,0},{2,3},{3,2},{4,5},{5,4},{6,7},{7,6},{8,9},{9,8},{10,11... | collective-permute-start | bytes 1622024 | tf_op jit(solution)/shard_map/cond/branch_1_fun/ppermute | solution.py:181
  69.3 1.8 %even.2.begun = f32[2,2,128,128]{3,2,1,0:T(8,128)S(1)} custom-call(s32[2]{0:T(128)S(1)} %get-tuple-element.106.spot, s16[4,528,128]{2,1,0:T(8,128)(2,1)S(1)} %all-to-all-done.mine, s16[528,128]{1,0:T(8,128)(2,1)S(1)} %get-tuple-element.108.b0, s16[528,128]{1,0:T(8,128)(2,1)} %get-tuple-element.109.b1, s16[528,128]{1,0:T(8,128)(2,1)} %get-tuple-element.110.b2, ...), custom_call_target="tpu_custom_call" | custom-call | flops 800000000 | bytes 2500000 | tf_op jit(solution)/shard_map/cond/branch_1_fun/even/pallas_call | solution.py:163
  71.2 0.0 collective-permute-done.17.others
  71.2 2.0 %odd.2 = f32[2,2,128,128]{3,2,1,0:T(8,128)S(1)} custom-call(s32[2]{0:T(128)S(1)} %get-tuple-element.106.spot, s32[2,2]{1,0:T(2,128)S(1)} %get-tuple-element.107.keep, f32[2,2,128,128]{3,2,1,0:T(8,128)S(1)} %even.2.begun, s16[4,528,128]{2,1,0:T(8,128)(2,1)} %collective-permute-done.17.others, s16[528,128]{1,0:T(8,128)(2,1)S(1)} %get-tuple-element.104.c0, ...), custom_call_target="tpu_custom_call" | custom-call | flops 800000000 | bytes 2500000 | tf_op jit(solution)/shard_map/cond/branch_1_fun/odd/pallas_call | solution.py:163
  73.2 0.0 collective-permute-done.23
  73.2 0.0 copy-start
  73.2 0.7 copy-done
  (6 shorter events, 0.0 us)
Async XLA Ops:
  1.6 34.7 %collective-permute-start.22 = (s16[528,128]{1,0:T(8,128)(2,1)S(1)}, s16[528,128]{1,0:T(8,128)(2,1)S(1)}, u32[]{:S(2)}, u32[]{:S(2)}) collective-permute-start(s16[528,128]{1,0:T(8,128)(2,1)S(1)} %get-tuple-element.151), channel_id=1, source_target_pairs={{16,0},{17,1},{18,2},{19,3},{20,4},{21,5},{22,6},{23,7},{24,8},{25... | collective-permute-start | bytes 405512 | tf_op jit(solution)/shard_map/ppermute | solution.py:181
  2.9 31.9 %collective-permute-start.6 = (s16[528,128]{1,0:T(8,128)(2,1)S(1)}, s16[528,128]{1,0:T(8,128)(2,1)}, u32[]{:S(2)}, u32[]{:S(2)}) collective-permute-start(s16[528,128]{1,0:T(8,128)(2,1)S(1)} %get-tuple-element.82), channel_id=1, source_target_pairs={{0,8},{1,9},{2,10},{3,11},{4,12},{5,13},{6,14},{7,15},{8,0},{9,1},... | collective-permute-start | bytes 405512 | tf_op jit(solution)/shard_map/cond/branch_1_fun/ppermute | solution.py:181
  14.3 13.0 %collective-permute-start = (s16[528,128]{1,0:T(8,128)(2,1)S(1)}, s16[528,128]{1,0:T(8,128)(2,1)}, u32[]{:S(2)}, u32[]{:S(2)}) collective-permute-start(s16[528,128]{1,0:T(8,128)(2,1)S(1)} %param.1), channel_id=1, source_target_pairs={{1,993},{3,995},{5,997},{7,999},{9,1001},{11,1003},{13,1005},{15,1... | collective-permute-start | bytes 405512 | tf_op jit(solution)/shard_map/cond/branch_1_fun/cond/branch_0_fun/ppermute | solution.py:181
  21.6 10.2 %collective-permute-start.1 = (s16[528,128]{1,0:T(8,128)(2,1)S(1)}, s16[528,128]{1,0:T(8,128)(2,1)}, u32[]{:S(2)}, u32[]{:S(2)}) collective-permute-start(s16[528,128]{1,0:T(8,128)(2,1)S(1)} %param.1), channel_id=1, source_target_pairs={{1,961},{3,963},{5,965},{7,967},{9,969},{11,971},{13,973},{15,975}... | collective-permute-start | bytes 405512 | tf_op jit(solution)/shard_map/cond/branch_1_fun/cond/branch_0_fun/ppermute | solution.py:181
  24.0 10.8 %collective-permute-start.2 = (s16[528,128]{1,0:T(8,128)(2,1)S(1)}, s16[528,128]{1,0:T(8,128)(2,1)}, u32[]{:S(2)}, u32[]{:S(2)}) collective-permute-start(s16[528,128]{1,0:T(8,128)(2,1)S(1)} %param.1), channel_id=1, source_target_pairs={{1,929},{3,931},{5,933},{7,935},{9,937},{11,939},{13,941},{15,943}... | collective-permute-start | bytes 405512 | tf_op jit(solution)/shard_map/cond/branch_1_fun/cond/branch_0_fun/ppermute | solution.py:181
  34.9 38.3 %collective-permute-start.23 = (s16[528,128]{1,0:T(8,128)(2,1)S(1)}, s16[528,128]{1,0:T(8,128)(2,1)S(1)}, u32[]{:S(2)}, u32[]{:S(2)}) collective-permute-start(s16[528,128]{1,0:T(8,128)(2,1)S(1)} %get-tuple-element.151), channel_id=1, source_target_pairs={{0,1008},{1,1009},{2,1010},{3,1011},{4,1012},{5,1013},{6,1014},{7,... | collective-permute-start | bytes 405512 | tf_op jit(solution)/shard_map/ppermute | solution.py:181
  36.3 0.7 copy-start.1
  38.8 25.9 %all-to-all-start = ((s16[4,528,128]{2,1,0:T(8,128)(2,1)}), s16[4,528,128]{2,1,0:T(8,128)(2,1)S(1)}, u32[]{:S(2)}, u32[]{:S(2)}) async-start(s16[4,528,128]{2,1,0:T(8,128)(2,1)} %broadcast_select_fusion.1), calls=%async_computation | async-start | bytes 1081344 | tf_op jit(solution)/shard_map/cond/branch_1_fun/all_to_all | solution.py:230
  45.3 13.7 %collective-permute-start.14 = (s16[528,128]{1,0:T(8,128)(2,1)S(1)}, s16[528,128]{1,0:T(8,128)(2,1)}, u32[]{:S(2)}, u32[]{:S(2)}) collective-permute-start(s16[528,128]{1,0:T(8,128)(2,1)S(1)} %get-tuple-element.104.c0), channel_id=1, source_target_pairs={{0,992},{1,993},{2,994},{3,995},{4,996},{5,997},{6,998},{7,999},{8... | collective-permute-start | bytes 405512 | tf_op jit(solution)/shard_map/cond/branch_1_fun/ppermute | solution.py:181
  53.2 9.5 %collective-permute-start.15 = (s16[528,128]{1,0:T(8,128)(2,1)S(1)}, s16[528,128]{1,0:T(8,128)(2,1)}, u32[]{:S(2)}, u32[]{:S(2)}) collective-permute-start(s16[528,128]{1,0:T(8,128)(2,1)S(1)} %get-tuple-element.104.c0), channel_id=1, source_target_pairs={{0,960},{1,961},{2,962},{3,963},{4,964},{5,965},{6,966},{7,967},{8... | collective-permute-start | bytes 405512 | tf_op jit(solution)/shard_map/cond/branch_1_fun/ppermute | solution.py:181
  55.7 9.0 %collective-permute-start.16 = (s16[528,128]{1,0:T(8,128)(2,1)S(1)}, s16[528,128]{1,0:T(8,128)(2,1)}, u32[]{:S(2)}, u32[]{:S(2)}) collective-permute-start(s16[528,128]{1,0:T(8,128)(2,1)S(1)} %get-tuple-element.104.c0), channel_id=1, source_target_pairs={{0,928},{1,929},{2,930},{3,931},{4,932},{5,933},{6,934},{7,935},{8... | collective-permute-start | bytes 405512 | tf_op jit(solution)/shard_map/cond/branch_1_fun/ppermute | solution.py:181
  65.8 5.4 %collective-permute-start.17 = (s16[4,528,128]{2,1,0:T(8,128)(2,1)S(1)}, s16[4,528,128]{2,1,0:T(8,128)(2,1)}, u32[]{:S(2)}, u32[]{:S(2)}) collective-permute-start(s16[4,528,128]{2,1,0:T(8,128)(2,1)S(1)} %broadcast_select_fusion.2), channel_id=1, source_target_pairs={{0,1},{1,0},{2,3},{3,2},{4,5},{5,4},{6,7},{7,6},{8,9},{9,8},{10,11... | collective-permute-start | bytes 1622024 | tf_op jit(solution)/shard_map/cond/branch_1_fun/ppermute | solution.py:181
  73.2 0.7 copy-start

commit v6 on v5

--- a/solution.py
+++ b/solution.py
@@ -241,14 +241,14 @@
         return jnp.zeros(PIECE.shape, PIECE.dtype)
 
     def open_low(b_own, a_own, a_sent):
-        return first_steps(low_plane, b_own, a_own, a_sent, (1, 2, 3))
+        a_far, *b_same = first_steps(low_plane, b_own, a_own, a_sent, (1, 2, 3))
+        return (offered(a_own, a_far), a_far, *b_same)
 
     def open_high(b_own, a_own, a_sent):
-        return tuple(blank() for _ in range(4))
+        return (jnp.zeros((4, *PIECE.shape), PIECE.dtype), *[blank() for _ in range(4)])
 
     def close_low(b_own, b_next, a_own, a_sent, sets):
-        a_far, *b_same = sets
-        offer = offered(a_own, a_far)
+        offer, a_far, *b_same = sets
         out, others, b_other, filler = last_steps(low_plane, b_own, b_next, offer, a_far, b_same, True)
         return (out, others, filler, *b_other)
 

time: 74.4 us -> 74.9 us (level)
  the two profiles are of different devices: /device:TPU:1 before, /device:TPU:577 now
where the time goes in v6:
time: 74.9 us; the launch traced here: 74.4 us
  starting transfers between devices  49.2 us (66%)
  waiting for transfers between devices  14 us (19%)
  local copies, waits for them, and re-layouts  4.94 us (7%)
  Pallas kernels  4.73 us (6%)
  other arithmetic  1.24 us (2%)
    ppermute x10, starting transfers between devices, moved(): return lax.ppermute(x, ('row', 'col'), pairs)  38.8 us
    ppermute x10, waiting for transfers between devices, moved(): return lax.ppermute(x, ('row', 'col'), pairs)  14 us
    all_to_all x1, starting transfers between devices, last_steps(): mine = lax.all_to_all(offer, 'col', 0, 0, axis_index_groups=quads)  10.4 us
    another operation x6, local copies, waits for them, and re-layouts  3.56 us
    pallas_call x2, Pallas kernels, summed(): pl.pallas_call(body, out_shape=jax.ShapeDtypeStruct((2, 2, BS, BS), jnp.f...  3.14 us
    pallas_call x1, Pallas kernels, packed(): pl.pallas_call(pack_all, out_shape=(PIECE,) * 3, in_specs=[SMEM] * 5 + [V...  1.59 us
  transfers between devices with their start and end apart: 11, of which 5 were waited for; matrix products, arithmetic and copies ran while one was open for 6% of the time, Pallas kernels for 2%

profile of v6, /device:TPU:577, one launch (start us, length us, event | category | flops | bytes accessed | tf_op | source)
XLA Modules:
  0.0 74.4 jit_solution(11740788422903469374)
XLA Ops:
  0.0 1.6 %pack_all.1 = (s16[528,128]{1,0:T(8,128)(2,1)S(1)}, s16[528,128]{1,0:T(8,128)(2,1)S(1)}, s16[528,128]{1,0:T(8,128)(2,1)S(1)}) custom-call(s32[2,4]{1,0:T(2,128)} %b_which.1, s32[1,2]{1,0:T(1,128)} %bitcast.13, s32[4,4]{1,0:T(4,128)} %a_which.1, s32[1,4]{1,0:T(1,128)} %bitcast.14, s32[1]{0:T(128)} %bitcast.6.chip, bf16[2,4,128,128]{3,2,1,0:T(8,128)(2,1)} %b_blocks.1, ...), custom_call_target="tpu_custom_call" | custom-call | flops 6000000 | bytes 1200000 | tf_op jit(solution)/shard_map/pack_all/pallas_call | solution.py:89
  1.6 1.3 %collective-permute-start.22 = (s16[528,128]{1,0:T(8,128)(2,1)S(1)}, s16[528,128]{1,0:T(8,128)(2,1)S(1)}, u32[]{:S(2)}, u32[]{:S(2)}) collective-permute-start(s16[528,128]{1,0:T(8,128)(2,1)S(1)} %get-tuple-element.160), channel_id=1, source_target_pairs={{16,0},{17,1},{18,2},{19,3},{20,4},{21,5},{22,6},{23,7},{24,8},{25... | collective-permute-start | bytes 405512 | tf_op jit(solution)/shard_map/ppermute | solution.py:181
  3.0 3.6 %conditional.5 = (s16[4,528,128]{2,1,0:T(8,128)(2,1)}, s16[528,128]{1,0:T(8,128)(2,1)}, s16[528,128]{1,0:T(8,128)(2,1)}, s16[528,128]{1,0:T(8,128)(2,1)}, s16[528,128]{1,0:T(8,128)(2,1)}) conditional(s32[]{:T(128)} %convert_element_type.11, () %tuple.53, (s32[]{:T(128)}, s32[4,1,1]{0,2,1:T(1,128)S(1)}, s16[528,128]{1,0:T(8,128)(2,1)S(1)}, ...), branch_computations={%region_0.1_spmd, %region_1.4_spmd} | conditional | flops 270342 | bytes 2973962 | solution.py:262
  3.0 0.9 %broadcast.18 = s16[4,528,128]{2,1,0:T(8,128)(2,1)} broadcast(s16[]{:T(256)} %constant.47.clone), dimensions={} | broadcast | bytes 540674 | tf_op jit(solution)/shard_map/broadcast.3
  3.8 0.7 broadcast.19
  4.5 0.7 broadcast.19.clone
  5.2 0.7 broadcast.19.clone.1
  5.9 0.7 broadcast.19.clone.2
  6.5 1.3 %collective-permute-start.23 = (s16[528,128]{1,0:T(8,128)(2,1)S(1)}, s16[528,128]{1,0:T(8,128)(2,1)S(1)}, u32[]{:S(2)}, u32[]{:S(2)}) collective-permute-start(s16[528,128]{1,0:T(8,128)(2,1)S(1)} %get-tuple-element.160), channel_id=1, source_target_pairs={{0,1008},{1,1009},{2,1010},{3,1011},{4,1012},{5,1013},{6,1014},{7,... | collective-permute-start | bytes 405512 | tf_op jit(solution)/shard_map/ppermute | solution.py:181
  7.8 0.1 pad_add_fusion
  7.9 0.0 collective-permute-done.22
  7.9 0.0 copy-start.1
  7.9 0.7 copy-done.1
  8.6 25.0 %conditional.6 = (s16[4,528,128]{2,1,0:T(8,128)(2,1)}, s16[528,128]{1,0:T(8,128)(2,1)S(1)}, s16[528,128]{1,0:T(8,128)(2,1)}, s16[528,128]{1,0:T(8,128)(2,1)}, s1...) conditional(s32[]{:T(128)} %convert_element_type.11, (s32[]{:T(128)}, s32[4,1,1]{0,2,1:T(1,128)S(1)}, ...), branch_computations={%region_4.7_spmd, %region_7.8_spmd} | conditional | flops 1600337920 | bytes 11893846 | solution.py:264
  8.6 5.7 %collective-permute-start.13 = (s16[528,128]{1,0:T(8,128)(2,1)S(1)}, s16[528,128]{1,0:T(8,128)(2,1)S(1)}, u32[]{:S(2)}, u32[]{:S(2)}) collective-permute-start(s16[528,128]{1,0:T(8,128)(2,1)S(1)} %get-tuple-element.99), channel_id=1, source_target_pairs={{16,24},{17,25},{18,26},{19,27},{20,28},{21,29},{22,30},{23,31},{2... | collective-permute-start | bytes 405512 | tf_op jit(solution)/shard_map/cond/branch_0_fun/ppermute | solution.py:181
  14.3 18.3 %conditional.1 = (s16[528,128]{1,0:T(8,128)(2,1)}, s16[528,128]{1,0:T(8,128)(2,1)}, s16[528,128]{1,0:T(8,128)(2,1)}) conditional(s32[]{:T(128)} %convert_element_type.6, s16[528,128]{1,0:T(8,128)(2,1)S(1)} %get-tuple-element.102, s16[528,128]{1,0:T(8,128)(2,1)S(1)} %get-tuple-element.102), branch_computations={%region_5.5_spmd, %region_6.6_spmd} | conditional | bytes 1622160 | solution.py:220
  14.3 7.3 %collective-permute-start.6 = (s16[528,128]{1,0:T(8,128)(2,1)S(1)}, s16[528,128]{1,0:T(8,128)(2,1)}, u32[]{:S(2)}, u32[]{:S(2)}) collective-permute-start(s16[528,128]{1,0:T(8,128)(2,1)S(1)} %param.4), channel_id=1, source_target_pairs={{17,1009},{19,1011},{21,1013},{23,1015},{25,1017},{27,1019},{29,10... | collective-permute-start | bytes 405512 | tf_op jit(solution)/shard_map/cond/branch_0_fun/cond/branch_0_fun/ppermute | solution.py:181
  21.6 2.4 %collective-permute-start.7 = (s16[528,128]{1,0:T(8,128)(2,1)S(1)}, s16[528,128]{1,0:T(8,128)(2,1)}, u32[]{:S(2)}, u32[]{:S(2)}) collective-permute-start(s16[528,128]{1,0:T(8,128)(2,1)S(1)} %param.4), channel_id=1, source_target_pairs={{17,977},{19,979},{21,981},{23,983},{25,985},{27,987},{29,989},{31... | collective-permute-start | bytes 405512 | tf_op jit(solution)/shard_map/cond/branch_0_fun/cond/branch_0_fun/ppermute | solution.py:181
  24.0 3.3 %collective-permute-start.8 = (s16[528,128]{1,0:T(8,128)(2,1)S(1)}, s16[528,128]{1,0:T(8,128)(2,1)}, u32[]{:S(2)}, u32[]{:S(2)}) collective-permute-start(s16[528,128]{1,0:T(8,128)(2,1)S(1)} %param.4), channel_id=1, source_target_pairs={{17,945},{19,947},{21,949},{23,951},{25,953},{27,955},{29,957},{31... | collective-permute-start | bytes 405512 | tf_op jit(solution)/shard_map/cond/branch_0_fun/cond/branch_0_fun/ppermute | solution.py:181
  27.3 0.0 collective-permute-done.6
  27.3 4.5 %collective-permute-done.7 = s16[528,128]{1,0:T(8,128)(2,1)} collective-permute-done((s16[528,128]{1,0:T(8,128)(2,1)S(1)}, s16[528,128]{1,0:T(8,128)(2,1)}, u32[]{:S(2)}, u32[]{:S(2)}) %collective-permute-start.7) | collective-permute-done | bytes 135200 | tf_op jit(solution)/shard_map/cond/branch_0_fun/cond/branch_0_fun/ppermute | solution.py:181
  31.9 0.7 collective-permute-done.8
  32.5 0.0 collective-permute-done.13
  32.5 1.0 %broadcast_select_fusion.1 = s16[4,528,128]{2,1,0:T(8,128)(2,1)} fusion(pred[4]{0:T(512)(128)(4,1)S(1)} %compare_bitcast_fusion.1, s16[528,128]{1,0:T(8,128)(2,1)S(1)} %collective-permute-done.13, s16[528,128]{1,0:T(8,128)(2,1)S(1)} %get-tuple-element.98), kind=kLoop, calls=%fused_computation.2 | loop fusion | flops 270336 | bytes 811012 | tf_op jit(solution)/shard_map/cond/branch_0_fun/jit(_where)/select_n | solution.py:227
  33.5 1.0 %collective-permute-done.23 = s16[528,128]{1,0:T(8,128)(2,1)S(1)} collective-permute-done((s16[528,128]{1,0:T(8,128)(2,1)S(1)}, s16[528,128]{1,0:T(8,128)(2,1)S(1)}, u32[]{:S(2)}, u32[]{:S(2)}) %collective-permute-start.23) | collective-permute-done | bytes 135200 | tf_op jit(solution)/shard_map/ppermute | solution.py:181
  34.5 39.1 %conditional.7 = (f32[2,2,128,128]{3,2,1,0:T(8,128)S(1)}) conditional(s32[]{:T(128)} %convert_element_type.11, (s16[4,528,128]{2,1,0:T(8,128)(2,1)}, s32[2]{0:T(128)S(1)}, s16[528,128]{1,0:T(8,128)(2,1)S(1)}, s16[528,128]{1,0:T(8,128)(2,1)}, s16[528,128]{1,0:T(8,128)(2,1)}, /*index=5*/s16[528,128]{1,0:T(8,128)(2,1)}, s32[]{:T(128)}, ...), branch_computations={%region_8.9_spmd, %region_9.10_spmd} | conditional | flops 1600270336 | bytes 11623470 | solution.py:265
  34.5 10.4 %all-to-all-start.1 = ((s16[4,528,128]{2,1,0:T(8,128)(2,1)}), s16[4,528,128]{2,1,0:T(8,128)(2,1)S(1)}, u32[]{:S(2)}, u32[]{:S(2)}) async-start(s16[4,528,128]{2,1,0:T(8,128)(2,1)} %get-tuple-element.121), calls=%async_computation.1 | async-start | bytes 1081344 | tf_op jit(solution)/shard_map/cond/branch_0_fun/all_to_all | solution.py:230
  44.9 11.2 %collective-permute-start.18 = (s16[528,128]{1,0:T(8,128)(2,1)S(1)}, s16[528,128]{1,0:T(8,128)(2,1)S(1)}, u32[]{:S(2)}, u32[]{:S(2)}) collective-permute-start(s16[528,128]{1,0:T(8,128)(2,1)S(1)} %get-tuple-element.130.c0), channel_id=1, source_target_pairs={{16,1008},{17,1009},{18,1010},{19,1011},{20,1012},{21,1013},{22,10... | collective-permute-start | bytes 405512 | tf_op jit(solution)/shard_map/cond/branch_0_fun/ppermute | solution.py:181
  56.1 1.9 %collective-permute-start.19 = (s16[528,128]{1,0:T(8,128)(2,1)S(1)}, s16[528,128]{1,0:T(8,128)(2,1)S(1)}, u32[]{:S(2)}, u32[]{:S(2)}) collective-permute-start(s16[528,128]{1,0:T(8,128)(2,1)S(1)} %get-tuple-element.130.c0), channel_id=1, source_target_pairs={{16,976},{17,977},{18,978},{19,979},{20,980},{21,981},{22,982},{23... | collective-permute-start | bytes 405512 | tf_op jit(solution)/shard_map/cond/branch_0_fun/ppermute | solution.py:181
  58.0 1.9 %collective-permute-start.20 = (s16[528,128]{1,0:T(8,128)(2,1)S(1)}, s16[528,128]{1,0:T(8,128)(2,1)S(1)}, u32[]{:S(2)}, u32[]{:S(2)}) collective-permute-start(s16[528,128]{1,0:T(8,128)(2,1)S(1)} %get-tuple-element.130.c0), channel_id=1, source_target_pairs={{16,944},{17,945},{18,946},{19,947},{20,948},{21,949},{22,950},{23... | collective-permute-start | bytes 405512 | tf_op jit(solution)/shard_map/cond/branch_0_fun/ppermute | solution.py:181
  59.9 0.0 collective-permute-done.18.c1
  60.0 3.4 %collective-permute-done.19.c2 = s16[528,128]{1,0:T(8,128)(2,1)S(1)} collective-permute-done((s16[528,128]{1,0:T(8,128)(2,1)S(1)}, s16[528,128]{1,0:T(8,128)(2,1)S(1)}, u32[]{:S(2)}, u32[]{:S(2)}) %collective-permute-start.19) | collective-permute-done | bytes 135200 | tf_op jit(solution)/shard_map/cond/branch_0_fun/ppermute | solution.py:181
  63.3 4.5 %collective-permute-done.20.c3 = s16[528,128]{1,0:T(8,128)(2,1)S(1)} collective-permute-done((s16[528,128]{1,0:T(8,128)(2,1)S(1)}, s16[528,128]{1,0:T(8,128)(2,1)S(1)}, u32[]{:S(2)}, u32[]{:S(2)}) %collective-permute-start.20) | collective-permute-done | bytes 135200 | tf_op jit(solution)/shard_map/cond/branch_0_fun/ppermute | solution.py:181
  67.8 0.0 all-to-all-done.1.mine
  67.8 0.2 broadcast_select_fusion.3
  68.0 2.5 %collective-permute-start.21 = (s16[4,528,128]{2,1,0:T(8,128)(2,1)S(1)}, s16[4,528,128]{2,1,0:T(8,128)(2,1)S(1)}, u32[]{:S(2)}, u32[]{:S(2)}) collective-permute-start(s16[4,528,128]{2,1,0:T(8,128)(2,1)S(1)} %broadcast_select_fusion.3), channel_id=1, source_target_pairs={{16,17},{17,16},{18,19},{19,18},{20,21},{21,20},{22,23},{23,22},{2... | collective-permute-start | bytes 1622024 | tf_op jit(solution)/shard_map/cond/branch_0_fun/ppermute | solution.py:181
  70.5 1.8 %even.3.begun = f32[2,2,128,128]{3,2,1,0:T(8,128)S(1)} custom-call(s32[2]{0:T(128)S(1)} %get-tuple-element.119.spot, s16[4,528,128]{2,1,0:T(8,128)(2,1)S(1)} %all-to-all-done.1.mine, s16[528,128]{1,0:T(8,128)(2,1)S(1)} %get-tuple-element.122.b0, s16[528,128]{1,0:T(8,128)(2,1)} %get-tuple-element.123.b1, s16[528,128]{1,0:T(8,128)(2,1)} %get-tuple-element.124.b2, ...), custom_call_target="tpu_custom_call" | custom-call | flops 800000000 | bytes 2500000 | tf_op jit(solution)/shard_map/cond/branch_0_fun/even/pallas_call | solution.py:163
  72.3 0.0 collective-permute-done.21.others
  72.3 1.3 %odd.3 = f32[2,2,128,128]{3,2,1,0:T(8,128)S(1)} custom-call(s32[2]{0:T(128)S(1)} %get-tuple-element.119.spot, s32[2,2]{1,0:T(2,128)S(1)} %get-tuple-element.120.keep, f32[2,2,128,128]{3,2,1,0:T(8,128)S(1)} %even.3.begun, s16[4,528,128]{2,1,0:T(8,128)(2,1)S(1)} %collective-permute-done.21.others, s16[528,128]{1,0:T(8,128)(2,1)S(1)} %get-tuple-element.130.c0, ...), custom_call_target="tpu_custom_call" | custom-call | flops 800000000 | bytes 2500000 | tf_op jit(solution)/shard_map/cond/branch_0_fun/odd/pallas_call | solution.py:163
  73.7 0.0 copy-start
  73.7 0.7 copy-done
  (6 shorter events, 0.0 us)
Async XLA Ops:
  1.6 6.3 %collective-permute-start.22 = (s16[528,128]{1,0:T(8,128)(2,1)S(1)}, s16[528,128]{1,0:T(8,128)(2,1)S(1)}, u32[]{:S(2)}, u32[]{:S(2)}) collective-permute-start(s16[528,128]{1,0:T(8,128)(2,1)S(1)} %get-tuple-element.160), channel_id=1, source_target_pairs={{16,0},{17,1},{18,2},{19,3},{20,4},{21,5},{22,6},{23,7},{24,8},{25... | collective-permute-start | bytes 405512 | tf_op jit(solution)/shard_map/ppermute | solution.py:181
  6.5 28.0 %collective-permute-start.23 = (s16[528,128]{1,0:T(8,128)(2,1)S(1)}, s16[528,128]{1,0:T(8,128)(2,1)S(1)}, u32[]{:S(2)}, u32[]{:S(2)}) collective-permute-start(s16[528,128]{1,0:T(8,128)(2,1)S(1)} %get-tuple-element.160), channel_id=1, source_target_pairs={{0,1008},{1,1009},{2,1010},{3,1011},{4,1012},{5,1013},{6,1014},{7,... | collective-permute-start | bytes 405512 | tf_op jit(solution)/shard_map/ppermute | solution.py:181
  7.9 0.7 copy-start.1
  8.6 24.0 %collective-permute-start.13 = (s16[528,128]{1,0:T(8,128)(2,1)S(1)}, s16[528,128]{1,0:T(8,128)(2,1)S(1)}, u32[]{:S(2)}, u32[]{:S(2)}) collective-permute-start(s16[528,128]{1,0:T(8,128)(2,1)S(1)} %get-tuple-element.99), channel_id=1, source_target_pairs={{16,24},{17,25},{18,26},{19,27},{20,28},{21,29},{22,30},{23,31},{2... | collective-permute-start | bytes 405512 | tf_op jit(solution)/shard_map/cond/branch_0_fun/ppermute | solution.py:181
  14.3 13.0 %collective-permute-start.6 = (s16[528,128]{1,0:T(8,128)(2,1)S(1)}, s16[528,128]{1,0:T(8,128)(2,1)}, u32[]{:S(2)}, u32[]{:S(2)}) collective-permute-start(s16[528,128]{1,0:T(8,128)(2,1)S(1)} %param.4), channel_id=1, source_target_pairs={{17,1009},{19,1011},{21,1013},{23,1015},{25,1017},{27,1019},{29,10... | collective-permute-start | bytes 405512 | tf_op jit(solution)/shard_map/cond/branch_0_fun/cond/branch_0_fun/ppermute | solution.py:181
  21.6 10.3 %collective-permute-start.7 = (s16[528,128]{1,0:T(8,128)(2,1)S(1)}, s16[528,128]{1,0:T(8,128)(2,1)}, u32[]{:S(2)}, u32[]{:S(2)}) collective-permute-start(s16[528,128]{1,0:T(8,128)(2,1)S(1)} %param.4), channel_id=1, source_target_pairs={{17,977},{19,979},{21,981},{23,983},{25,985},{27,987},{29,989},{31... | collective-permute-start | bytes 405512 | tf_op jit(solution)/shard_map/cond/branch_0_fun/cond/branch_0_fun/ppermute | solution.py:181
  24.0 8.5 %collective-permute-start.8 = (s16[528,128]{1,0:T(8,128)(2,1)S(1)}, s16[528,128]{1,0:T(8,128)(2,1)}, u32[]{:S(2)}, u32[]{:S(2)}) collective-permute-start(s16[528,128]{1,0:T(8,128)(2,1)S(1)} %param.4), channel_id=1, source_target_pairs={{17,945},{19,947},{21,949},{23,951},{25,953},{27,955},{29,957},{31... | collective-permute-start | bytes 405512 | tf_op jit(solution)/shard_map/cond/branch_0_fun/cond/branch_0_fun/ppermute | solution.py:181
  34.5 33.3 %all-to-all-start.1 = ((s16[4,528,128]{2,1,0:T(8,128)(2,1)}), s16[4,528,128]{2,1,0:T(8,128)(2,1)S(1)}, u32[]{:S(2)}, u32[]{:S(2)}) async-start(s16[4,528,128]{2,1,0:T(8,128)(2,1)} %get-tuple-element.121), calls=%async_computation.1 | async-start | bytes 1081344 | tf_op jit(solution)/shard_map/cond/branch_0_fun/all_to_all | solution.py:230
  44.9 15.1 %collective-permute-start.18 = (s16[528,128]{1,0:T(8,128)(2,1)S(1)}, s16[528,128]{1,0:T(8,128)(2,1)S(1)}, u32[]{:S(2)}, u32[]{:S(2)}) collective-permute-start(s16[528,128]{1,0:T(8,128)(2,1)S(1)} %get-tuple-element.130.c0), channel_id=1, source_target_pairs={{16,1008},{17,1009},{18,1010},{19,1011},{20,1012},{21,1013},{22,10... | collective-permute-start | bytes 405512 | tf_op jit(solution)/shard_map/cond/branch_0_fun/ppermute | solution.py:181
  56.1 7.3 %collective-permute-start.19 = (s16[528,128]{1,0:T(8,128)(2,1)S(1)}, s16[528,128]{1,0:T(8,128)(2,1)S(1)}, u32[]{:S(2)}, u32[]{:S(2)}) collective-permute-start(s16[528,128]{1,0:T(8,128)(2,1)S(1)} %get-tuple-element.130.c0), channel_id=1, source_target_pairs={{16,976},{17,977},{18,978},{19,979},{20,980},{21,981},{22,982},{23... | collective-permute-start | bytes 405512 | tf_op jit(solution)/shard_map/cond/branch_0_fun/ppermute | solution.py:181
  58.0 9.8 %collective-permute-start.20 = (s16[528,128]{1,0:T(8,128)(2,1)S(1)}, s16[528,128]{1,0:T(8,128)(2,1)S(1)}, u32[]{:S(2)}, u32[]{:S(2)}) collective-permute-start(s16[528,128]{1,0:T(8,128)(2,1)S(1)} %get-tuple-element.130.c0), channel_id=1, source_target_pairs={{16,944},{17,945},{18,946},{19,947},{20,948},{21,949},{22,950},{23... | collective-permute-start | bytes 405512 | tf_op jit(solution)/shard_map/cond/branch_0_fun/ppermute | solution.py:181
  68.0 4.3 %collective-permute-start.21 = (s16[4,528,128]{2,1,0:T(8,128)(2,1)S(1)}, s16[4,528,128]{2,1,0:T(8,128)(2,1)S(1)}, u32[]{:S(2)}, u32[]{:S(2)}) collective-permute-start(s16[4,528,128]{2,1,0:T(8,128)(2,1)S(1)} %broadcast_select_fusion.3), channel_id=1, source_target_pairs={{16,17},{17,16},{18,19},{19,18},{20,21},{21,20},{22,23},{23,22},{2... | collective-permute-start | bytes 1622024 | tf_op jit(solution)/shard_map/cond/branch_0_fun/ppermute | solution.py:181
  73.7 0.7 copy-start
